TPU v7x, 32 devices: a whole 2x2x4 slice. The times are simulated.
32 devices in a mesh: blk: 16 (over z, y, x), slab: 2 (over core).
Axes of the slice: x: 2, y: 2, z: 4, core: 2. Of those that a mesh axis runs over, the one named last changes fastest.
Arguments:
- amplitudes: bfloat16 [960, 8192], P('blk', 'slab'), may hold values from -6 to 6
- ladder_ints: bfloat16 [8192, 8192], P('slab', 'blk'), may hold values from -0.0625 to 0.0625
- cycle_ints: bfloat16 [2, 64, 120, 512], P('slab', 'blk'), may hold values from -0.0625 to 0.0625
- block_dims: int32 [2, 2], replicated, may hold values from 24 to 64, as said below
Outputs:
- ladder_res: bfloat16 [960, 8192], P('slab', 'blk')
- cycle_res: bfloat16 [2, 512, 512], P('slab', 'blk')
Inputs may be any that keep to these rules, and one draw needn't show every extreme that they name: `block_dims`: every block's two sizes lie within the padded size; in every draw some block's first size equals 64 and some block's second size equals 24.
All inputs are finite; a program needn't handle non-finite values.
Results may differ from a plain program's by a relative error of at most 0.0014.
Values may be sent and summed in bfloat16 or wider, within the bound.
No kernel may reach another device: no remote copies, remote signals or barrier semaphores. Data moves between devices by JAX's collectives and lax.ppermute only.
A program may use at most 128 MiB of HBM per device.

v0:
```python
import jax
import jax.numpy as jnp
from jax import lax
from jax.sharding import PartitionSpec as P

BS = 64


def block_sizes(block_dims, owner):
    blocks_count = block_dims.shape[0]
    select = owner[:, None] == lax.iota(jnp.int32, blocks_count)[None, :]
    size_first = jnp.sum(jnp.where(select, block_dims[None, :, 0], 0), 1)
    size_second = jnp.sum(jnp.where(select, block_dims[None, :, 1], 0), 1)
    return (size_first, size_second)


def column_valid(block_dims, first_column, column_count):
    column = first_column + lax.iota(jnp.int32, column_count)
    owner = column // (BS * BS)
    size_first, size_second = block_sizes(block_dims, owner)
    return (column // BS % BS < size_first) & (column % BS < size_second)


def local(amplitudes, ladder_ints, cycle_ints, block_dims):
    slab_index = lax.axis_index("slab")
    blk_index = lax.axis_index("blk")
    block_width = amplitudes.shape[1]
    valid = column_valid(block_dims, slab_index * block_width, block_width)
    masked = jnp.where(valid[None, :], amplitudes, jnp.zeros((), amplitudes.dtype))
    gathered = lax.all_gather(masked, "blk", axis=0, tiled=True)
    pair_rows = gathered.shape[0]
    ladder_sum = lax.psum_scatter(
        jnp.dot(gathered, ladder_ints, preferred_element_type=jnp.float32),
        "slab",
        scatter_dimension=0,
        tiled=True,
    )
    out_columns = ladder_ints.shape[1]
    out_valid = column_valid(block_dims, blk_index * out_columns, out_columns)
    ladder_res = jnp.where(out_valid[None, :], ladder_sum, 0.0).astype(jnp.bfloat16)
    occupied = cycle_ints.shape[2]
    j_window = pair_rows // occupied
    columns = lax.all_to_all(masked, "blk", split_axis=1, concat_axis=0, tiled=True)
    c_part = cycle_ints.shape[1]
    amp_part = columns.reshape(occupied, j_window, c_part, BS)
    cycle_term = jnp.einsum(
        "cke,kjcd->ejd", cycle_ints[0], amp_part, preferred_element_type=jnp.float32
    )
    cycle_term = cycle_term.reshape(cycle_term.shape[0], j_window * BS)
    cycle_sum = lax.psum_scatter(cycle_term, "blk", scatter_dimension=0, tiled=True)
    local_rows = cycle_sum.shape[0]
    own_block = jnp.full((1,), slab_index, jnp.int32)
    size_first, size_second = block_sizes(block_dims, own_block)
    row_virtual = (blk_index * local_rows + lax.iota(jnp.int32, local_rows)) % BS
    column_virtual = lax.iota(jnp.int32, j_window * BS) % BS
    allowed = (row_virtual[:, None] < size_first[0]) & (column_virtual[None, :] < size_second[0])
    cycle_res = jnp.where(allowed, cycle_sum, 0.0).astype(jnp.bfloat16)[None]
    return (ladder_res, cycle_res)


def solution(mesh):
    in_specs = (P("blk", "slab"), P("slab", "blk"), P("slab", "blk", None, None), P())
    out_specs = (P("slab", "blk"), P("slab", "blk", None))
    return jax.shard_map(local, mesh=mesh, in_specs=in_specs, out_specs=out_specs, check_vma=False)
```

profile of v0, /device:TPU:0, one launch (start us, length us, event | category | flops | bytes accessed | tf_op | source)
XLA Modules:
  0.0 228.8 jit_solution(9464650035485257012)
XLA Ops:
  7.2 0.0 copy-start
  7.2 0.0 all-gather.3.cloned.1.call-start
  7.2 1.0 slice_reduce_fusion
  8.2 0.2 select_reduce_fusion
  8.4 1.9 fusion.32
  10.4 0.0 all-gather.3.cloned.1.call-update
  10.4 0.0 reduce-scatter.5.cloned.1.call-start
  10.4 1.1 broadcast_select_fusion
  11.5 0.1 copy.17
  11.7 0.1 copy.13
  11.8 30.0 %all_to_all.16 = bf16[60,16,256]{2,0,1:T(8,128)(2,1)S(1)} all-to-all(bf16[60,16,256]{2,0,1:T(8,128)(2,1)S(1)} %copy.13), channel_id=1, replica_groups=mesh['blk'=16,'slab'=2] {'blk'}, dimensions={1} | all-to-all | bytes 983040 | tf_op jit(solution)/shard_map/all_to_all | solution.py:43
  41.8 0.4 reshape.217
  42.2 0.0 copy-done
  42.2 0.7 fusion
  43.0 1.3 copy.15
  44.3 0.0 reduce-scatter.5.cloned.1.call-update
  44.3 0.0 reduce-scatter.3.cloned.1.call-start
  44.4 89.4 %all-gather.3.cloned.1.call-done = bf16[16,60,4096]{2,1,0:T(8,128)(2,1)} async-done(((bf16[1,60,4096]{2,1,0:T(8,128)(2,1)}), bf16[16,60,4096]{2,1,0:T(8,128)(2,1)}) %all-gather.3.cloned.1.call-update) | async-done | bytes 7864336 | tf_op jit(solution)/shard_map/all_gather | solution.py:30
  133.8 9.3 %reshape.220 = bf16[960,4096]{1,0:T(8,128)(2,1)} reshape(bf16[16,60,4096]{2,1,0:T(8,128)(2,1)} %all-gather.3.cloned.1.call-done) | data formatting | bytes 15728640
  143.0 9.9 %fusion.29 = f32[960,512]{1,0:T(8,128)} fusion(bf16[960,4096]{1,0:T(8,128)(2,1)} %reshape.220, bf16[4096,512]{1,0:T(8,128)(2,1)} %param.5), kind=kOutput, calls=%fused_computation.73 | convolution fusion | flops 4026531840 | bytes 14024704 | tf_op jit(solution)/shard_map/dot_general | solution.py:33
  153.0 0.0 reduce-scatter.3.cloned.1.call-update
  153.0 0.6 fusion.25
  153.6 0.7 fusion.18
  154.3 0.7 fusion.27
  155.0 0.1 select_reduce_fusion.3
  155.1 56.8 %reduce-scatter.5.cloned.1.call-done = f32[32,512]{1,0:T(8,128)} async-done(((f32[512,512]{1,0:T(8,128)}), f32[32,512]{1,0:T(8,128)}) %reduce-scatter.5.cloned.1.call-update) | async-done | bytes 65552 | tf_op jit(solution)/shard_map/reduce_scatter | solution.py:50
  211.9 1.5 fusion.3
  213.4 6.7 %reduce-scatter.3.cloned.1.call-done = f32[480,512]{1,0:T(8,128)} async-done(((f32[960,512]{1,0:T(8,128)}), f32[480,512]{1,0:T(8,128)}) %reduce-scatter.3.cloned.1.call-update) | async-done | bytes 983056 | tf_op jit(solution)/shard_map/reduce_scatter | solution.py:32
  220.1 2.1 select_convert_fusion
  (5 shorter events, 0.1 us)
Async XLA Ops:
  7.2 35.1 %copy-start = (bf16[1,4,120,512]{3,2,1,0:T(8,128)(2,1)S(1)}, bf16[1,4,120,512]{3,2,1,0:T(8,128)(2,1)}, u32[]{:S(2)}) copy-start(bf16[1,4,120,512]{3,2,1,0:T(8,128)(2,1)} %param.6) | copy-start | bytes 1474564
  7.2 126.6 %all-gather.3.cloned.1.call-start = ((), (), s32[]{:S(2)}) async-start(), calls=%async_computation.5 | async-start | bytes 8912896 | tf_op jit(solution)/shard_map/all_gather | solution.py:30
  10.4 201.5 %reduce-scatter.5.cloned.1.call-start = ((), (), s32[]{:S(2)}) async-start(), calls=%async_computation.4 | async-start | bytes 1114112 | tf_op jit(solution)/shard_map/reduce_scatter | solution.py:50
  44.3 175.8 %reduce-scatter.3.cloned.1.call-start = ((), (), s32[]{:S(2)}) async-start(), calls=%async_computation.3 | async-start | bytes 2949120 | tf_op jit(solution)/shard_map/reduce_scatter | solution.py:32
Sparse Core Ops, SparseCore 0:
  10.8 122.9 all-gather.2
  136.0 75.7 reduce-scatter.4
  214.2 5.8 reduce-scatter.2
where the time goes:
time: 229 us
  waiting for transfers between devices  153 us (67%)
  blocking collectives  30 us (13%)
  between operations  13.8 us (6%)
  local copies, waits for them, and re-layouts  12.3 us (5%)
  matrix products  10.6 us (5%)
  other arithmetic  8.93 us (4%)
    all_gather x1, waiting for transfers between devices, local(): gathered = lax.all_gather(masked, 'blk', axis=0, tiled=True)  89.4 us
    reduce_scatter x1, waiting for transfers between devices, local(): lax.psum_scatter(cycle_term, 'blk', scatter_dimension=0, tiled=True)  56.8 us
    all_to_all x1, blocking collectives, local(): lax.all_to_all(masked, 'blk', split_axis=1, concat_axis=0, tiled=True)  30 us
    dot_general x1, matrix products, local(): jnp.dot(gathered, ladder_ints, preferred_element_type=jnp.float32)  9.92 us
    unnamed x4, local copies, waits for them, and re-layouts  9.38 us
    reduce_scatter x1, waiting for transfers between devices, local(): lax.psum_scatter(jnp.dot(gathered, ladder_ints, preferred_element_type=jn...  6.75 us
  transfers between devices with their start and end apart: 3, of which 3 were waited for; matrix products, arithmetic and copies ran while one was open for 12% of the time, Pallas kernels for 0%

commit v1 on v0

--- a/solution.py
+++ b/solution.py
@@ -1,9 +1,18 @@
+import functools
+
 import jax
 import jax.numpy as jnp
+import numpy as np
 from jax import lax
+from jax.experimental import pallas as pl
+from jax.experimental.pallas import tpu as pltpu
 from jax.sharding import PartitionSpec as P
 
 BS = 64
+LEAST = 24
+GROUP = 16
+PIECE = 64
+AXES = ("blk", "slab")
 
 
 def block_sizes(block_dims, owner):
@@ -21,7 +30,15 @@
     return (column // BS % BS < size_first) & (column % BS < size_second)
 
 
-def local(amplitudes, ladder_ints, cycle_ints, block_dims):
+def cycle_allowed(block_dims, slab_index, blk_index, local_rows, columns):
+    own_block = jnp.full((1,), slab_index, jnp.int32)
+    size_first, size_second = block_sizes(block_dims, own_block)
+    row_virtual = (blk_index * local_rows + lax.iota(jnp.int32, local_rows)) % BS
+    column_virtual = lax.iota(jnp.int32, columns) % BS
+    return (row_virtual[:, None] < size_first[0]) & (column_virtual[None, :] < size_second[0])
+
+
+def plain(amplitudes, ladder_ints, cycle_ints, block_dims):
     slab_index = lax.axis_index("slab")
     blk_index = lax.axis_index("blk")
     block_width = amplitudes.shape[1]
@@ -48,17 +65,521 @@
     )
     cycle_term = cycle_term.reshape(cycle_term.shape[0], j_window * BS)
     cycle_sum = lax.psum_scatter(cycle_term, "blk", scatter_dimension=0, tiled=True)
-    local_rows = cycle_sum.shape[0]
-    own_block = jnp.full((1,), slab_index, jnp.int32)
-    size_first, size_second = block_sizes(block_dims, own_block)
-    row_virtual = (blk_index * local_rows + lax.iota(jnp.int32, local_rows)) % BS
-    column_virtual = lax.iota(jnp.int32, j_window * BS) % BS
-    allowed = (row_virtual[:, None] < size_first[0]) & (column_virtual[None, :] < size_second[0])
+    allowed = cycle_allowed(block_dims, slab_index, blk_index, cycle_sum.shape[0], j_window * BS)
     cycle_res = jnp.where(allowed, cycle_sum, 0.0).astype(jnp.bfloat16)[None]
     return (ladder_res, cycle_res)
+
+
+def send(value, target, cores=(0, 1)):
+    pairs = []
+    for chip in range(16):
+        for core in cores:
+            x, y, z = target(chip & 1, chip >> 1 & 1, chip >> 2, core)
+            pairs.append((2 * chip + core, 2 * (4 * (z % 4) + 2 * y + x) + core))
+    return lax.ppermute(value, AXES, pairs)
+
+
+def along_x(x, y, z, core):
+    return (1 - x, y, z)
+
+
+def along_y(x, y, z, core):
+    return (x, 1 - y, z)
+
+
+def across(x, y, z, core):
+    return (1 - x, 1 - y, z)
+
+
+def first_axis(x, y, z, core):
+    return along_x(x, y, z, core) if core == 0 else along_y(x, y, z, core)
+
+
+def second_axis(x, y, z, core):
+    return along_y(x, y, z, core) if core == 0 else along_x(x, y, z, core)
+
+
+def up(step):
+    return lambda x, y, z, core: (x, y, z + step)
+
+
+def to_other_core(value, cores):
+    return lax.ppermute(value, "slab", [(core, 1 - core) for core in cores])
+
+
+def compact_tables(width):
+    column = np.arange(GROUP * width)
+    c, d = column // width, column % width
+    return np.stack([c * BS + d, c // 4 * GROUP + c % 4, d] + [c * 0] * 5).astype(np.int32)
+
+
+def prep_kernel(width, least, dims, amp, moved, wide, narrow, out, rows):
+    def tiles(table, group_width):
+        result = []
+        for lo in range(0, GROUP * group_width, 128):
+            start = lo // group_width // 2 * 128
+            stop = -(-((lo + 127) // group_width + 1) // 2) * 128
+            source = table[0:1, lo : lo + 128] - start
+            at = lax.broadcasted_iota(jnp.int32, (stop - start, 128), 0)
+            pick = jnp.where(at == source, 1.0, 0.0).astype(jnp.bfloat16)
+            result.append((lo, start, stop, pick))
+        return result
+
+    def compact(source, group, table, picks, block, to):
+        def part(at):
+            column = at // (4 * BS) * (GROUP * BS) + group * (4 * BS) + at % (4 * BS)
+            return source[:, column : column + 128]
+
+        for lo, start, stop, pick in picks:
+            window = jnp.concatenate([part(at) for at in range(start, stop, 128)], 1)
+            value = jnp.dot(window, pick, preferred_element_type=jnp.float32)
+            c, d = table[1:2, lo : lo + 128] + 4 * group, table[2:3, lo : lo + 128]
+            keep = (c < dims[block, 0]) & (d < dims[block, 1])
+            rows[0:60, to + lo : to + lo + 128] = jnp.where(keep, value, 0.0).astype(jnp.bfloat16)
+
+    core, shift = lax.axis_index("slab"), lax.axis_index("blk") % 2 * 4
+    wide_columns, narrow_columns = GROUP * width, GROUP * least
+    rows[...] = jnp.zeros_like(rows)
+
+    @pl.when(core == 0)
+    def _():
+        picks = tiles(wide, width)
+        for g in range(3):
+            compact(amp, g, wide, picks, 0, g * wide_columns)
+
+    @pl.when(core == 1)
+    def _():
+        compact(moved, 3, wide, tiles(wide, width), 0, 0)
+        picks = tiles(narrow, least)
+        for g in range(4):
+            compact(amp, g, narrow, picks, 1, wide_columns + g * narrow_columns)
+
+    shape = (PIECE, PIECE)
+    down = lax.broadcasted_iota(jnp.int32, shape, 0) - lax.broadcasted_iota(jnp.int32, shape, 1)
+    down = jnp.where(down == shift, 1.0, 0.0).astype(jnp.bfloat16)
+    out[...] = jnp.dot(down, rows[...], preferred_element_type=jnp.float32).astype(jnp.bfloat16)
+
+
+def prep(width, least, columns, block_dims, amplitudes, moved):
+    smem = pl.BlockSpec(memory_space=pltpu.SMEM)
+    vmem = pl.BlockSpec(memory_space=pltpu.VMEM)
+    return pl.pallas_call(
+        functools.partial(prep_kernel, width, least),
+        out_shape=jax.ShapeDtypeStruct((PIECE, columns), jnp.bfloat16),
+        in_specs=[smem] + [vmem] * 4,
+        out_specs=vmem,
+        scratch_shapes=[pltpu.VMEM((PIECE, columns), jnp.bfloat16)],
+        name="prep",
+    )(
+        block_dims,
+        amplitudes,
+        moved,
+        jnp.asarray(compact_tables(width)),
+        jnp.asarray(compact_tables(least)),
+    )
+
+
+def compact_rows(ladder_ints, moved_ints, width, least, columns, core):
+    def pad(rows):
+        return jnp.pad(rows, ((0, columns - rows.shape[0]), (0, 0)))
+
+    out_columns = ladder_ints.shape[1]
+
+    def cut(rows, keep):
+        rows = rows.reshape(4, -1, 4, BS, out_columns)[:, :, :, :keep]
+        return rows.transpose(1, 0, 2, 3, 4).reshape(-1, out_columns)
+
+    def of_first():
+        groups = ladder_ints.reshape(4, 4, 4 * BS, out_columns)
+        return pad(cut(groups[:, :3], width))
+
+    def of_second():
+        return pad(jnp.concatenate([cut(moved_ints, width), cut(ladder_ints, least)]))
+
+    return lax.cond(core == 0, of_first, of_second)
+
+
+def distance_of(slot, core):
+    swapped = (slot & 1) * 2 + (slot >> 1)
+    return jnp.where(core == 0, slot, swapped)
+
+
+def chip_of(n, core, blk_index):
+    near = (n >= 4) & (n < 12)
+    z_step = jnp.where(near, (n & 1) * 2 + 1, jnp.where(n < 4, 0, 2))
+    slot = jnp.where(near, (n - 4) >> 1, n & 3)
+    z = (blk_index // 4 - z_step) & 3
+    return z * 4 + ((blk_index & 3) ^ distance_of(slot, core))
+
+
+VMEM = pl.BlockSpec(memory_space=pltpu.VMEM)
+SMEM = pl.BlockSpec(memory_space=pltpu.SMEM)
+ROOM = pltpu.CompilerParams(vmem_limit_bytes=48 * 1024 * 1024)
+EARLY_PIECES = 10
+
+
+def slots_kernel(part_0, part_1, part_2, part_3, early, late, other_early, other_late):
+    core, blk_index = lax.axis_index("slab"), lax.axis_index("blk")
+    occupied = part_0.shape[1]
+    slot = lax.broadcasted_iota(jnp.int32, (128, 1), 0)
+    at = lax.broadcasted_iota(jnp.int32, (128, occupied), 1)
+    cut = 8 * EARLY_PIECES
+    rest = 128 - cut
+    for order, first_pieces, last_pieces in ((core, early, late), (1 - core, other_early, other_late)):
+        chip = chip_of(slot >> 3, order, blk_index)
+        k = 15 * (chip >> 1) + 7 * (chip & 1) + (slot & 7)
+        pick = jnp.where(at == k, 1.0, 0.0).astype(jnp.bfloat16)
+        for step, part in enumerate((part_0, part_1, part_2, part_3)):
+            first = (blk_index // 4 - step & 3) * 4
+            part = jnp.concatenate([part[c] for c in range(4)], 1)
+            rows = jnp.dot(pick, part, preferred_element_type=jnp.float32).astype(jnp.bfloat16)
+            for c in range(4):
+                of_c = rows[:, 128 * c : 128 * c + 128]
+                first_pieces[pl.ds(pl.multiple_of((first + c) * cut, 16), cut), :] = of_c[:cut]
+                last_pieces[pl.ds(pl.multiple_of((first + c) * rest, 16), rest), :] = of_c[cut:]
+
+
+def slots_of_pieces(parts):
+    rows = 8 * EARLY_PIECES
+    shapes = [
+        jax.ShapeDtypeStruct((GROUP * rows, 128), jnp.bfloat16),
+        jax.ShapeDtypeStruct((GROUP * (128 - rows), 128), jnp.bfloat16),
+    ]
+    return pl.pallas_call(
+        slots_kernel,
+        out_shape=shapes * 2,
+        in_specs=[VMEM] * 4,
+        out_specs=[VMEM] * 4,
+        compiler_params=ROOM,
+        name="slots",
+    )(*parts)
+
+
+def products(pieces, rows_w, total):
+    depth = rows_w.shape[0]
+    step = max(n for n in range(128, 1025, 128) if depth % n == 0)
+    total[...] = jnp.zeros_like(total)
+
+    def body(n, carry):
+        at = pl.ds(pl.multiple_of(n * step, 128), step)
+        left = [piece[:, :, at].reshape(-1, step) for piece in pieces]
+        total[...] += jnp.dot(
+            jnp.concatenate(left, 0), rows_w[at, :], preferred_element_type=jnp.float32
+        )
+        return carry
+
+    lax.fori_loop(0, depth // step, body, 0)
+
+
+def ladder_early_kernel(*refs):
+    products(refs[:-2], refs[-2], refs[-1])
+
+
+def ladder_early(pieces, rows_w):
+    shape = (EARLY_PIECES * PIECE, rows_w.shape[1])
+    return pl.pallas_call(
+        ladder_early_kernel,
+        out_shape=jax.ShapeDtypeStruct(shape, jnp.float32),
+        in_specs=[VMEM] * (len(pieces) + 1),
+        out_specs=VMEM,
+        compiler_params=ROOM,
+        name="ladder_early",
+    )(*pieces, rows_w)
+
+
+def ladder_late_kernel(*refs):
+    pieces = refs[:-5]
+    rows_w, early, mine, other, total = refs[-5:]
+    core, blk_index = lax.axis_index("slab"), lax.axis_index("blk")
+    products(pieces, rows_w, total)
+
+    def place(n, value):
+        chip = chip_of(n, core, blk_index)
+
+        @pl.when(chip // 8 == core)
+        def _():
+            mine[chip & 7] = value
+
+        @pl.when(chip // 8 != core)
+        def _():
+            other[chip & 7] = value
+
+    def of_early(n, carry):
+        place(n, early[pl.ds(pl.multiple_of(n * PIECE, PIECE), PIECE), :])
+        return carry
+
+    def of_late(n, carry):
+        place(n + EARLY_PIECES, total[pl.ds(pl.multiple_of(n * PIECE, PIECE), PIECE), :])
+        return carry
+
+    lax.fori_loop(0, EARLY_PIECES, of_early, 0)
+    lax.fori_loop(0, 16 - EARLY_PIECES, of_late, 0)
+
+
+def ladder_late(pieces, rows_w, early):
+    out_columns = rows_w.shape[1]
+    half = jax.ShapeDtypeStruct((8, PIECE, out_columns), jnp.float32)
+    return pl.pallas_call(
+        ladder_late_kernel,
+        out_shape=[half, half],
+        in_specs=[VMEM] * (len(pieces) + 2),
+        out_specs=[VMEM, VMEM],
+        scratch_shapes=[pltpu.VMEM(((16 - EARLY_PIECES) * PIECE, out_columns), jnp.float32)],
+        compiler_params=ROOM,
+        name="ladder_late",
+    )(*pieces, rows_w, early)
+
+
+def ladder_end_kernel(dims, mine, other, out, rows):
+    out_columns = out.shape[1]
+    column = lax.axis_index("blk") * out_columns
+    column = column + lax.broadcasted_iota(jnp.int32, (1, out_columns), 1)
+    block, c, d = column >> 12, column >> 6 & 63, column & 63
+    size_first = jnp.where(block == 0, dims[0, 0], dims[1, 0])
+    size_second = jnp.where(block == 0, dims[0, 1], dims[1, 1])
+    keep = (c < size_first) & (d < size_second)
+
+    def body(pair, carry):
+        even = mine[2 * pair] + other[2 * pair]
+        odd = mine[2 * pair + 1] + other[2 * pair + 1]
+        both = jnp.concatenate([even[:56], even[56:] + odd[:8], odd[8:]], 0)
+        rows[pl.ds(pl.multiple_of(pair * 120, 8), 120), :] = jnp.where(keep, both, 0.0)
+        return carry
+
+    lax.fori_loop(0, 4, body, 0)
+    out[...] = rows[...].astype(jnp.bfloat16)
+
+
+def ladder_end(block_dims, mine, other):
+    shape = (480, mine.shape[2])
+    return pl.pallas_call(
+        ladder_end_kernel,
+        out_shape=jax.ShapeDtypeStruct(shape, jnp.bfloat16),
+        in_specs=[SMEM, VMEM, VMEM],
+        out_specs=VMEM,
+        scratch_shapes=[pltpu.VMEM(shape, jnp.float32)],
+        compiler_params=ROOM,
+        name="ladder_end",
+    )(block_dims, mine, other)
+
+
+def turn(pieces, group_width, start, spread, turned):
+    wide = GROUP * group_width
+    count = sum(piece.shape[0] for piece in pieces)
+    rows, each = count * PIECE, 8 * count
+    n = 0
+    for piece in pieces:
+
+        def body(i, carry, piece=piece, n=n):
+            part = piece[i, :, pl.ds(start, wide)].astype(jnp.float32)
+            for b in range(wide // 128):
+                at = pl.multiple_of((b * count + n + i) * PIECE, PIECE)
+                spread[pl.ds(at, PIECE), :] = part[:, 128 * b : 128 * b + 128]
+            return carry
+
+        lax.fori_loop(0, piece.shape[0], body, 0)
+        n += piece.shape[0]
+    spread[wide // 128 * rows : wide // 128 * rows + rows, :] = jnp.zeros((rows, 128), jnp.float32)
+
+    def columns(pair, carry):
+        for c in range(GROUP):
+            lo = c * group_width
+            base = lo // 128
+            blocks = [base] if lo % 128 + BS <= 128 else [base, base + 1]
+            halves = []
+            for odd in range(2):
+                window = [
+                    spread[pl.ds(b * rows + 2 * pair + odd, each, stride=8), :] for b in blocks
+                ]
+                window = jnp.concatenate(window, 1)
+                halves.append(window[:, lo % 128 : lo % 128 + BS])
+            at = pl.ds(pl.multiple_of(pair * 128, 128), 128)
+            turned[c * each : (c + 1) * each, at] = jnp.concatenate(halves, 1).astype(turned.dtype)
+        return carry
+
+    lax.fori_loop(0, 4, columns, 0)
+
+
+def first_part(core, plane):
+    return (core == 0) == (plane < 3)
+
+
+def group_starts(width, least, core, plane):
+    first = jnp.where(core == 0, plane, 0) * (GROUP * width)
+    own = GROUP * width + plane * (GROUP * least)
+    return pl.multiple_of(first, 128), pl.multiple_of(own, 128)
+
+
+def cycle_early_kernel(width, least, *refs):
+    pieces, (first, own, spread) = refs[:-3], refs[-3:]
+    core, plane = lax.axis_index("slab"), lax.axis_index("blk") & 3
+    first_start, own_start = group_starts(width, least, core, plane)
+
+    @pl.when(first_part(core, plane))
+    def _():
+        turn(pieces, width, first_start, spread, first)
+
+    @pl.when(core == 1)
+    def _():
+        turn(pieces, least, own_start, spread, own)
+
+
+def cycle_early(width, least, pieces):
+    count = sum(p.shape[0] for p in pieces)
+    shape = jax.ShapeDtypeStruct((GROUP * 8 * count, 8 * BS), jnp.bfloat16)
+    blocks = GROUP * max(width, least) // 128 + 1
+    return pl.pallas_call(
+        functools.partial(cycle_early_kernel, width, least),
+        out_shape=[shape, shape],
+        in_specs=[VMEM] * len(pieces),
+        out_specs=[VMEM, VMEM],
+        scratch_shapes=[pltpu.VMEM((blocks * count * PIECE, 128), jnp.float32)],
+        compiler_params=ROOM,
+        name="cycle_early",
+    )(*pieces)
+
+
+def cycle_late_kernel(width, least, *refs):
+    pieces, refs = refs[:-10], refs[-10:]
+    turned_first, turned_own, slots_first, late_first, slots_own, late_own, first, own = refs[:8]
+    spread, turned = refs[8:]
+    core, plane = lax.axis_index("slab"), lax.axis_index("blk") & 3
+    first_start, own_start = group_starts(width, least, core, plane)
+
+    def total(slots, early, slots_late, out):
+        pairs = ((slots, early), (slots_late, turned))
+        out[...] = sum(
+            lax.dot_general(
+                left[...], right[...], (((0,), (0,)), ((), ())), preferred_element_type=jnp.float32
+            )
+            for left, right in pairs
+        )
+
+    first[...] = jnp.zeros_like(first)
+    own[...] = jnp.zeros_like(own)
+
+    @pl.when(first_part(core, plane))
+    def _():
+        turn(pieces, width, first_start, spread, turned)
+        total(slots_first, turned_first, late_first, first)
+
+    @pl.when(core == 1)
+    def _():
+        turn(pieces, least, own_start, spread, turned)
+        total(slots_own, turned_own, late_own, own)
+
+
+def cycle_late(width, least, pieces, turned, slots_first, slots_own):
+    count = sum(p.shape[0] for p in pieces)
+    shape = jax.ShapeDtypeStruct((128, 8 * BS), jnp.float32)
+    blocks = GROUP * max(width, least) // 128 + 1
+    return pl.pallas_call(
+        functools.partial(cycle_late_kernel, width, least),
+        out_shape=[shape, shape],
+        in_specs=[VMEM] * (6 + len(pieces)),
+        out_specs=[VMEM, VMEM],
+        scratch_shapes=[
+            pltpu.VMEM((blocks * count * PIECE, 128), jnp.float32),
+            pltpu.VMEM((GROUP * 8 * count, 8 * BS), jnp.bfloat16),
+        ],
+        compiler_params=ROOM,
+        name="cycle_late",
+    )(*pieces, *turned, *slots_first, *slots_own)
+
+
+def after(value, *others):
+    return lax.optimization_barrier((value,) + others)[0]
+
+
+def compacted(width, least, amplitudes, ladder_ints, cycle_ints, block_dims, moved, moved_ints):
+    core = lax.axis_index("slab")
+    blk_index = lax.axis_index("blk")
+    plane, z = blk_index % 4, blk_index // 4
+    wide_columns, narrow_columns = GROUP * width, GROUP * least
+    columns = max(3 * wide_columns, wide_columns + 4 * narrow_columns)
+
+    own = prep(width, least, columns, block_dims, amplitudes, moved)[None]
+    near = [send(own, up(step)) for step in (1, 3)]
+    plane_1 = send(own, first_axis)
+    plane_2 = send(own, second_axis)
+    moved_ints = to_other_core(after(moved_ints, own), (0,))
+    plane_12 = send(plane_1, second_axis)
+    rows_w = compact_rows(ladder_ints, moved_ints, width, least, columns, core)
+    near = after(jnp.concatenate(near), plane_1, plane_2)
+    far = send(after(own, near), up(2))
+    near_1 = send(near, first_axis)
+    near_2 = send(near, second_axis)
+    near_12 = send(near_1, second_axis)
+    far_1 = send(far, first_axis)
+    far_2 = send(far, second_axis)
+    far_12 = send(far_1, second_axis)
+    shares = after(cycle_ints[0], far)
+
+    def share(step):
+        part = lax.dynamic_slice_in_dim(shares, (z + step) % 4 * 128, 128, 2)
+        return send(part, up(step)) if step else part
+
+    slots = slots_of_pieces([share(step) for step in range(4)])
+    slots_first = [
+        jnp.where(core == 0, here, to_other_core(there, (0,)))
+        for here, there in zip(slots[:2], slots[2:])
+    ]
+
+    out_columns = ladder_ints.shape[1]
+    pieces = [own, plane_1, plane_2, plane_12, near, near_1, near_2]
+    last = [near_12, far, far_1, far_2, far_12]
+    sums = ladder_early(pieces, rows_w)
+    turned = cycle_early(width, least, pieces)
+    terms = cycle_late(width, least, last, turned, slots_first, slots[:2])
+    pairs = [(2 * chip + 1, 2 * chip) for chip in (3, 7, 11, 15)]
+    last_group = lax.ppermute(terms[0], AXES, pairs)
+    mine, other = ladder_late(last, rows_w, after(sums, terms[0]))
+    other = to_other_core(other, (0, 1))
+    term = jnp.where(core == 0, jnp.where(plane == 3, last_group, terms[0]), terms[1])
+    term = term.reshape(4, 32, 8 * BS)
+
+    def chunk(chip):
+        return lax.dynamic_index_in_dim(term, chip, 0, False)
+
+    cycle_sum = chunk(plane)
+    for distance, target in ((1, along_x), (2, along_y), (3, across)):
+        cycle_sum = cycle_sum + send(chunk(plane ^ distance), target)
+    ladder_res = ladder_end(block_dims, mine, other)
+    allowed = cycle_allowed(block_dims, core, blk_index, 32, 8 * BS)
+    cycle_res = jnp.where(allowed, cycle_sum, 0.0).astype(jnp.bfloat16)[None]
+    return (ladder_res, cycle_res)
+
+
+WIDTHS = (48, 56, 64)
+
+
+def local(amplitudes, ladder_ints, cycle_ints, block_dims):
+    moved = to_other_core(amplitudes, (0,))
+    moved_ints = ladder_ints.reshape(4, 4, 4 * BS, -1)[:, 3].reshape(GROUP * BS, -1)
+    size = block_dims[0, 1]
+
+    def choose(widths):
+        if len(widths) == 1:
+            return functools.partial(compacted, widths[0], LEAST)
+        half = len(widths) // 2
+        fewer, more = choose(widths[:half]), choose(widths[half:])
+        return lambda *given: lax.cond(size <= widths[half - 1], fewer, more, *given)
+
+    return lax.cond(
+        block_dims[1, 1] <= LEAST,
+        choose(WIDTHS),
+        functools.partial(compacted, BS, BS),
+        amplitudes,
+        ladder_ints,
+        cycle_ints,
+        block_dims,
+        moved,
+        moved_ints,
+    )
 
 
 def solution(mesh):
     in_specs = (P("blk", "slab"), P("slab", "blk"), P("slab", "blk", None, None), P())
     out_specs = (P("slab", "blk"), P("slab", "blk", None))
-    return jax.shard_map(local, mesh=mesh, in_specs=in_specs, out_specs=out_specs, check_vma=False)
+    body = local if dict(mesh.shape) == {"blk": 16, "slab": 2} else plain
+    return jax.shard_map(body, mesh=mesh, in_specs=in_specs, out_specs=out_specs, check_vma=False)

time: 229 us -> 102 us (0.45)
  waiting for transfers between devices: 153 us -> 33.9 us
  starting transfers between devices: 0.12 us -> 32.9 us
  blocking collectives: 30 us -> 0 us
  Pallas kernels: 0 us -> 17.2 us
  between operations: 13.8 us -> 1.29 us
  matrix products: 10.6 us -> 0 us
  other arithmetic: 8.93 us -> 4.6 us
    all_gather x1 -> x0, waiting for transfers between devices: 89.4 us -> none  [local(): gathered = lax.all_gather(masked, 'blk', axis=0, tiled=True)]
    reduce_scatter x2 -> x0, waiting for transfers between devices: 63.5 us -> none  [the longest x1 56.8 us: local(): lax.psum_scatter(cycle_term, 'blk', scatter_dimension=0, tiled=True)]
    ppermute x0 -> x24, waiting for transfers between devices: none -> 33.9 us  [the longest x18 33.9 us: send(): return lax.ppermute(value, AXES, pairs)]
    ppermute x0 -> x24, starting transfers between devices: none -> 32.9 us  [the longest x18 22.9 us: send(): return lax.ppermute(value, AXES, pairs)]
    all_to_all x1 -> x0, blocking collectives: 30 us -> none  [local(): lax.all_to_all(masked, 'blk', split_axis=1, concat_axis=0, tiled=True)]
    pallas_call x0 -> x7, Pallas kernels: none -> 17.2 us  [the longest x1 3.92 us: ladder_early(): pl.pallas_call(ladder_early_kernel, out_shape=jax.ShapeDtypeStruct(shape,...]
    dot_general x2 -> x0, matrix products: 10.6 us -> none  [the longest x1 9.92 us: local(): jnp.dot(gathered, ladder_ints, preferred_element_type=jnp.float32)]
    unnamed x4 -> x0, local copies, waits for them, and re-layouts: 9.38 us -> none
  transfers between devices with their start and end apart: 3 -> 24, of which waited for: 3 -> 9; matrix products, arithmetic and copies ran while one was open for 12% -> 10% of each run, Pallas kernels for 0% -> 6%
where the time goes in v1:
time: 102 us; the launch traced here: 101 us
  waiting for transfers between devices  33.9 us (33%)
  starting transfers between devices  32.9 us (32%)
  Pallas kernels  17.2 us (17%)
  local copies, waits for them, and re-layouts  10.1 us (10%)
  other arithmetic  4.6 us (5%)
  between operations  1.29 us (1%)
  loops' own time  1.23 us (1%)
    ppermute x18, waiting for transfers between devices, send(): return lax.ppermute(value, AXES, pairs)  33.9 us
    ppermute x18, starting transfers between devices, send(): return lax.ppermute(value, AXES, pairs)  22.9 us
    ppermute x5, starting transfers between devices, to_other_core(): return lax.ppermute(value, 'slab', [(core, 1 - core) for core in cores])  9.25 us
    pallas_call x1, Pallas kernels, ladder_early(): pl.pallas_call(ladder_early_kernel, out_shape=jax.ShapeDtypeStruct(shape,...  3.92 us
    pallas_call x1, Pallas kernels, ladder_late(): pl.pallas_call(ladder_late_kernel, out_shape=[half, half], in_specs=[VMEM...  3.41 us
    pallas_call x1, Pallas kernels, cycle_late(): pl.pallas_call(functools.partial(cycle_late_kernel, width, least), out_sh...  3.33 us
    cond x34, local copies, waits for them, and re-layouts  2.94 us
    pallas_call x1, Pallas kernels, prep(): pl.pallas_call(functools.partial(prep_kernel, width, least), out_shape=ja...  2.43 us
  transfers between devices with their start and end apart: 24, of which 9 were waited for; matrix products, arithmetic and copies ran while one was open for 10% of the time, Pallas kernels for 6%

profile of v1, /device:TPU:0, one launch (start us, length us, event | category | flops | bytes accessed | tf_op | source)
XLA Modules:
  0.0 101.2 jit_solution(7613652134194493882)
XLA Ops:
  0.6 2.4 %collective-permute-start.92 = (bf16[60,4096]{1,0:T(8,128)(2,1)}, bf16[60,4096]{1,0:T(8,128)(2,1)S(1)}, u32[]{:S(2)}, u32[]{:S(2)}) collective-permute-start(bf16[60,4096]{1,0:T(8,128)(2,1)} %param.26), channel_id=1, source_target_pairs={{0,1},{2,3},{4,5},{6,7},{8,9},{10,11},{12,13},{14,15},{16,17},{18,... | collective-permute-start | bytes 1474568 | tf_op jit(solution)/shard_map/ppermute | solution.py:107
  3.0 1.3 %slice.67 = s32[1,1]{1,0:T(1,128)} slice(s32[2,2]{1,0:T(2,128)} %param.29), slice={[1:2], [1:2]} | slice | bytes 8 | tf_op jit(solution)/shard_map/slice | solution.py:569
  4.9 2.3 %slice.80 = bf16[4,1,256,512]{3,2,1,0:T(8,128)(2,1)} slice(bf16[4,4,256,512]{3,2,1,0:T(8,128)(2,1)} %bitcast.184), slice={[0:4], [3:4], [0:256], [0:512]} | slice | bytes 2097152 | tf_op jit(solution)/shard_map/slice | solution.py:558
  7.2 0.0 collective-permute-done.92
  7.2 94.0 %conditional.7 = ((bf16[480,512]{1,0:T(8,128)(2,1)}, bf16[1,32,512]{2,1,0:T(8,128)(2,1)})) conditional(s32[]{:T(128)} %bitcast.75, (s32[2,2]{1,0:T(2,128)}, bf16[60,4096]{1,0:T(8,128)(2,1)}, bf16[60,4096]{1,0:T(8,128)(2,1)S(1)}, s32[8,1024]{1,0:T(8,128)}, s32[8,1024]{1,0:T(8,128)}, /*index=5*/bf16[1024,512]{1,0:T(8,128)(2,1)}, ...), branch_computations={%region_0.5_spmd, %region_5.22_spmd} | conditional | flops 11898902 | bytes 145886976 | solution.py:568
  7.2 1.3 %slice.64 = s32[1,1]{1,0:T(1,128)} slice(s32[2,2]{1,0:T(2,128)} %get-tuple-element.256), slice={[0:1], [1:2]} | slice | bytes 8 | tf_op jit(solution)/shard_map/slice | solution.py:559
  9.2 92.0 %conditional.5 = ((bf16[480,512]{1,0:T(8,128)(2,1)}, bf16[1,32,512]{2,1,0:T(8,128)(2,1)})) conditional(s32[]{:T(128)} %convert_element_type.39, (s32[]{:T(128)}, s32[2,2]{1,0:T(2,128)}, bf16[60,4096]{1,0:T(8,128)(2,1)}, bf16[60,4096]{1,0:T(8,128)(2,1)S(1)}, s32[8,1024]{1,0:T(8,128)}, /*index=5*/s32[8,384]{1,0:T(8,128)}, ...), branch_computations={%region_6.16_spmd, %region_17.21_spmd} | conditional | flops 11898900 | bytes 113512232 | solution.py:566
  9.4 0.0 copy-start.56
  9.4 2.4 %prep.7 = bf16[64,2304]{1,0:T(8,128)(2,1)} custom-call(s32[2,2]{1,0:T(2,128)} %get-tuple-element.233.dims, bf16[60,4096]{1,0:T(8,128)(2,1)} %get-tuple-element.234.amp, bf16[60,4096]{1,0:T(8,128)(2,1)S(1)} %get-tuple-element.235.moved, s32[8,768]{1,0:T(8,128)} %constant.373.clone.2.wide, s32[8,384]{1,0:T(8,128)} %get-tuple-element.237.narrow), custom_call_target="tpu_custom_call" | custom-call | tf_op jit(solution)/shard_map/cond/branch_1_fun/cond/branch_1_fun/prep/pallas_call | solution.py:166
  11.9 4.4 %collective-permute-start.70 = (bf16[1,64,2304]{2,1,0:T(8,128)(2,1)}, bf16[1,64,2304]{2,1,0:T(8,128)(2,1)S(1)}, u32[]{:S(2)}, u32[]{:S(2)}) collective-permute-start(bf16[1,64,2304]{2,1,0:T(8,128)(2,1)} %bitcast.177), channel_id=1, source_target_pairs={{0,24},{1,25},{2,26},{3,27},{4,28},{5,29},{6,30},{7,31},{8,0},{9,1... | collective-permute-start | bytes 884744 | tf_op jit(solution)/shard_map/cond/branch_1_fun/cond/branch_1_fun/ppermute | solution.py:79
  16.3 1.5 %collective-permute-start.71 = (bf16[1,64,2304]{2,1,0:T(8,128)(2,1)}, bf16[1,64,2304]{2,1,0:T(8,128)(2,1)S(1)}, u32[]{:S(2)}, u32[]{:S(2)}) collective-permute-start(bf16[1,64,2304]{2,1,0:T(8,128)(2,1)} %bitcast.179), channel_id=1, source_target_pairs={{0,2},{1,5},{2,0},{3,7},{4,6},{5,1},{6,4},{7,3},{8,10},{9,13},{10,... | collective-permute-start | bytes 884744 | tf_op jit(solution)/shard_map/cond/branch_1_fun/cond/branch_1_fun/ppermute | solution.py:79
  17.8 1.5 %collective-permute-start.72 = (bf16[1,64,2304]{2,1,0:T(8,128)(2,1)}, bf16[1,64,2304]{2,1,0:T(8,128)(2,1)S(1)}, u32[]{:S(2)}, u32[]{:S(2)}) collective-permute-start(bf16[1,64,2304]{2,1,0:T(8,128)(2,1)} %bitcast.180), channel_id=1, source_target_pairs={{0,4},{1,3},{2,6},{3,1},{4,0},{5,7},{6,2},{7,5},{8,12},{9,11},{10,... | collective-permute-start | bytes 884744 | tf_op jit(solution)/shard_map/cond/branch_1_fun/cond/branch_1_fun/ppermute | solution.py:79
  19.3 4.8 %collective-permute-done.70 = bf16[1,64,2304]{2,1,0:T(8,128)(2,1)S(1)} collective-permute-done((bf16[1,64,2304]{2,1,0:T(8,128)(2,1)}, bf16[1,64,2304]{2,1,0:T(8,128)(2,1)S(1)}, u32[]{:S(2)}, u32[]{:S(2)}) %collective-permute-start.70) | collective-permute-done | bytes 294944 | tf_op jit(solution)/shard_map/cond/branch_1_fun/cond/branch_1_fun/ppermute | solution.py:79
  24.1 5.5 %collective-permute-done.69 = bf16[1,64,2304]{2,1,0:T(8,128)(2,1)S(1)} collective-permute-done((bf16[1,64,2304]{2,1,0:T(8,128)(2,1)}, bf16[1,64,2304]{2,1,0:T(8,128)(2,1)S(1)}, u32[]{:S(2)}, u32[]{:S(2)}) %collective-permute-start.69) | collective-permute-done | bytes 294944 | tf_op jit(solution)/shard_map/cond/branch_1_fun/cond/branch_1_fun/ppermute | solution.py:79
  29.6 0.1 pad_maximum_fusion.5.refs_4_
  29.7 0.0 collective-permute-done.71.refs_1_
  29.7 0.0 collective-permute-done.72.refs_2_
  29.7 0.8 collective-permute-start.75
  30.5 1.5 %collective-permute-start.73 = (bf16[2,64,2304]{2,1,0:T(8,128)(2,1)S(1)}, bf16[2,64,2304]{2,1,0:T(8,128)(2,1)S(1)}, u32[]{:S(2)}, u32[]{:S(2)}) collective-permute-start(bf16[2,64,2304]{2,1,0:T(8,128)(2,1)S(1)} %pad_maximum_fusion.5.refs_4_), channel_id=1, source_target_pairs={{0,2},{1,5},{2,0},{3,7},{4,6},{5,1},{6,4},{7,3},{8,10},{9,13},{10,... | collective-permute-start | bytes 1769480 | tf_op jit(solution)/shard_map/cond/branch_1_fun/cond/branch_1_fun/ppermute | solution.py:79
  32.0 1.5 %collective-permute-start.81 = (bf16[2,64,2304]{2,1,0:T(8,128)(2,1)S(1)}, bf16[2,64,2304]{2,1,0:T(8,128)(2,1)S(1)}, u32[]{:S(2)}, u32[]{:S(2)}) collective-permute-start(bf16[2,64,2304]{2,1,0:T(8,128)(2,1)S(1)} %pad_maximum_fusion.5.refs_4_), channel_id=1, source_target_pairs={{0,4},{1,3},{2,6},{3,1},{4,0},{5,7},{6,2},{7,5},{8,12},{9,11},{10,... | collective-permute-start | bytes 1769480 | tf_op jit(solution)/shard_map/cond/branch_1_fun/cond/branch_1_fun/ppermute | solution.py:79
  33.5 11.2 %collective-permute-done.75.refs_1_ = bf16[1,64,2304]{2,1,0:T(8,128)(2,1)} collective-permute-done((bf16[1,64,2304]{2,1,0:T(8,128)(2,1)}, bf16[1,64,2304]{2,1,0:T(8,128)(2,1)}, u32[]{:S(2)}, u32[]{:S(2)}) %collective-permute-start.75) | collective-permute-done | bytes 294944 | tf_op jit(solution)/shard_map/cond/branch_1_fun/cond/branch_1_fun/ppermute | solution.py:79
  44.7 0.1 constant_dynamic-slice_fusion.12
  44.8 0.1 collective-permute-start.82
  44.9 1.6 %collective-permute-start.80 = (bf16[1,64,2304]{2,1,0:T(8,128)(2,1)S(1)}, bf16[1,64,2304]{2,1,0:T(8,128)(2,1)S(1)}, u32[]{:S(2)}, u32[]{:S(2)}) collective-permute-start(bf16[1,64,2304]{2,1,0:T(8,128)(2,1)S(1)} %collective-permute-done.71.refs_1_), channel_id=1, source_target_pairs={{0,4},{1,3},{2,6},{3,1},{4,0},{5,7},{6,2},{7,5},{8,12},{9,11},{10,... | collective-permute-start | bytes 884744 | tf_op jit(solution)/shard_map/cond/branch_1_fun/cond/branch_1_fun/ppermute | solution.py:79
  46.5 1.9 %collective-permute-start.83 = (bf16[4,120,128]{2,1,0:T(8,128)(2,1)S(1)}, bf16[4,120,128]{2,1,0:T(8,128)(2,1)S(1)}, u32[]{:S(2)}, u32[]{:S(2)}) collective-permute-start(bf16[4,120,128]{2,1,0:T(8,128)(2,1)S(1)} %get-tuple-element.316), channel_id=1, source_target_pairs={{0,16},{1,17},{2,18},{3,19},{4,20},{5,21},{6,22},{7,23},{8,24},{9,... | collective-permute-start | bytes 368648 | tf_op jit(solution)/shard_map/cond/branch_1_fun/cond/branch_1_fun/ppermute | solution.py:79
  48.3 4.4 %collective-permute-done.82.part_1 = bf16[4,120,128]{2,1,0:T(8,128)(2,1)S(1)} collective-permute-done((bf16[4,120,128]{2,1,0:T(8,128)(2,1)S(1)}, bf16[4,120,128]{2,1,0:T(8,128)(2,1)S(1)}, u32[]{:S(2)}, u32[]{:S(2)}) %collective-permute-start.82) | collective-permute-done | bytes 122912 | tf_op jit(solution)/shard_map/cond/branch_1_fun/cond/branch_1_fun/ppermute | solution.py:79
  52.8 3.4 %collective-permute-done.83.part_2 = bf16[4,120,128]{2,1,0:T(8,128)(2,1)S(1)} collective-permute-done((bf16[4,120,128]{2,1,0:T(8,128)(2,1)S(1)}, bf16[4,120,128]{2,1,0:T(8,128)(2,1)S(1)}, u32[]{:S(2)}, u32[]{:S(2)}) %collective-permute-start.83) | collective-permute-done | bytes 122912 | tf_op jit(solution)/shard_map/cond/branch_1_fun/cond/branch_1_fun/ppermute | solution.py:79
  56.1 2.8 %collective-permute-start.79 = (bf16[1024,512]{1,0:T(8,128)(2,1)}, bf16[1024,512]{1,0:T(8,128)(2,1)}, u32[]{:S(2)}, u32[]{:S(2)}) collective-permute-start(bf16[1024,512]{1,0:T(8,128)(2,1)} %get-tuple-element.241), channel_id=1, source_target_pairs={{0,1},{2,3},{4,5},{6,7},{8,9},{10,11},{12,13},{14,15},{16,17},{18,... | collective-permute-start | bytes 3145736 | tf_op jit(solution)/shard_map/cond/branch_1_fun/cond/branch_1_fun/ppermute | solution.py:107
  58.9 1.0 %collective-permute-start.76 = (bf16[1,64,2304]{2,1,0:T(8,128)(2,1)}, bf16[1,64,2304]{2,1,0:T(8,128)(2,1)}, u32[]{:S(2)}, u32[]{:S(2)}) collective-permute-start(bf16[1,64,2304]{2,1,0:T(8,128)(2,1)} %collective-permute-done.75.refs_1_), channel_id=1, source_target_pairs={{0,2},{1,5},{2,0},{3,7},{4,6},{5,1},{6,4},{7,3},{8,10},{9,13},{10,... | collective-permute-start | bytes 884744 | tf_op jit(solution)/shard_map/cond/branch_1_fun/cond/branch_1_fun/ppermute | solution.py:79
  59.9 1.2 %slots.7 = (bf16[1280,128]{1,0:T(8,128)(2,1)S(1)}, bf16[768,128]{1,0:T(8,128)(2,1)S(1)}, bf16[1280,128]{1,0:T(8,128)(2,1)}, bf16[768,128]{1,0:T(8,128)(2,1)}) custom-call(bf16[4,120,128]{2,1,0:T(8,128)(2,1)S(1)} %get-tuple-element.318.part_0, bf16[4,120,128]{2,1,0:T(8,128)(2,1)S(1)} %collective-permute-done.82.part_1, ...), custom_call_target="tpu_custom_call" | custom-call | tf_op jit(solution)/shard_map/cond/branch_1_fun/cond/branch_1_fun/slots/pallas_call | solution.py:248
  61.2 2.0 %collective-permute-start.86 = (bf16[768,128]{1,0:T(8,128)(2,1)}, bf16[768,128]{1,0:T(8,128)(2,1)}, u32[]{:S(2)}, u32[]{:S(2)}) collective-permute-start(bf16[768,128]{1,0:T(8,128)(2,1)} %get-tuple-element.250), channel_id=1, source_target_pairs={{0,1},{2,3},{4,5},{6,7},{8,9},{10,11},{12,13},{14,15},{16,17},{18,... | collective-permute-start | bytes 589832 | tf_op jit(solution)/shard_map/cond/branch_1_fun/cond/branch_1_fun/ppermute | solution.py:107
  63.1 0.0 collective-permute-done.73.refs_5_
  63.2 2.0 %collective-permute-start.85 = (bf16[1280,128]{1,0:T(8,128)(2,1)}, bf16[1280,128]{1,0:T(8,128)(2,1)}, u32[]{:S(2)}, u32[]{:S(2)}) collective-permute-start(bf16[1280,128]{1,0:T(8,128)(2,1)} %get-tuple-element.248), channel_id=1, source_target_pairs={{0,1},{2,3},{4,5},{6,7},{8,9},{10,11},{12,13},{14,15},{16,17},{18,... | collective-permute-start | bytes 983048 | tf_op jit(solution)/shard_map/cond/branch_1_fun/cond/branch_1_fun/ppermute | solution.py:107
  65.2 1.5 %collective-permute-start.77 = (bf16[1,64,2304]{2,1,0:T(8,128)(2,1)}, bf16[1,64,2304]{2,1,0:T(8,128)(2,1)}, u32[]{:S(2)}, u32[]{:S(2)}) collective-permute-start(bf16[1,64,2304]{2,1,0:T(8,128)(2,1)} %collective-permute-done.75.refs_1_), channel_id=1, source_target_pairs={{0,4},{1,3},{2,6},{3,1},{4,0},{5,7},{6,2},{7,5},{8,12},{9,11},{10,... | collective-permute-start | bytes 884744 | tf_op jit(solution)/shard_map/cond/branch_1_fun/cond/branch_1_fun/ppermute | solution.py:79
  66.7 1.4 %cycle_early.7 = (bf16[1280,512]{1,0:T(8,128)(2,1)S(1)}, bf16[1280,512]{1,0:T(8,128)(2,1)S(1)}) custom-call(bf16[1,64,2304]{2,1,0:T(8,128)(2,1)S(1)} %bitcast.182, bf16[1,64,2304]{2,1,0:T(8,128)(2,1)S(1)} %collective-permute-done.71.refs_1_, bf16[1,64,2304]{2,1,0:T(8,128)(2,1)S(1)} %collective-permute-done.72.refs_2_, ...), custom_call_target="tpu_custom_call" | custom-call | tf_op jit(solution)/shard_map/cond/branch_1_fun/cond/branch_1_fun/cycle_early/pallas_call | solution.py:431
  68.1 0.8 collective-permute-start.74
  68.9 1.3 %collective-permute-start.78 = (bf16[1,64,2304]{2,1,0:T(8,128)(2,1)}, bf16[1,64,2304]{2,1,0:T(8,128)(2,1)}, u32[]{:S(2)}, u32[]{:S(2)}) collective-permute-start(bf16[1,64,2304]{2,1,0:T(8,128)(2,1)} %collective-permute-done.76.refs_2_), channel_id=1, source_target_pairs={{0,4},{1,3},{2,6},{3,1},{4,0},{5,7},{6,2},{7,5},{8,12},{9,11},{10,... | collective-permute-start | bytes 884744 | tf_op jit(solution)/shard_map/cond/branch_1_fun/cond/branch_1_fun/ppermute | solution.py:79
  70.2 0.7 broadcast_select_fusion.7.refs_8_
  71.0 2.1 %conditional.4 = (bf16[2304,512]{1,0:T(8,128)(2,1)}) conditional(s32[]{:T(128)} %convert_element_type.37, (bf16[1024,512]{1,0:T(8,128)(2,1)}, bf16[4096,512]{1,0:T(8,128)(2,1)S(1)}) %tuple.135, bf16[4096,512]{1,0:T(8,128)(2,1)S(1)} %copy-done.48), branch_computations={%region_18.17_spmd, %region_19.18_spmd} | conditional | flops 4718592 | bytes 17301512 | solution.py:199
  71.0 0.2 slice.78
  71.2 0.2 copy.37
  71.5 1.6 %slice.79 = bf16[4,3,4,48,512]{4,3,2,0,1:T(8,128)(2,1)} slice(bf16[4,3,4,64,512]{4,3,2,0,1:T(8,128)(2,1)S(1)} %bitcast.199), slice={[0:4], [0:3], [0:4], [0:48], [0:512]} | slice | bytes 4718592 | tf_op jit(solution)/shard_map/cond/branch_1_fun/cond/branch_1_fun/cond/branch_1_fun/slice | solution.py:189
  73.1 1.0 copy-done.35
  74.0 1.0 copy-done.37
  75.0 1.0 copy-done.39
  76.0 3.9 %ladder_early.7.refs_6_ = f32[640,512]{1,0:T(8,128)S(1)} custom-call(bf16[1,64,2304]{2,1,0:T(8,128)(2,1)S(1)} %bitcast.183, bf16[1,64,2304]{2,1,0:T(8,128)(2,1)S(1)} %copy-done.35, bf16[1,64,2304]{2,1,0:T(8,128)(2,1)S(1)} %copy-done.37, bf16[1,64,2304]{2,1,0:T(8,128)(2,1)S(1)} %copy-done.39, bf16[2,64,2304]{2,1,0:T(8,128)(2,1)S(1)} %pad_maximum_fusion.5.refs_4_, ...), custom_call_target="tpu_custom_call" | custom-call | tf_op jit(solution)/shard_map/cond/branch_1_fun/cond/branch_1_fun/ladder_early/pallas_call | solution.py:280
  79.9 1.8 %collective-permute-done.78.refs_4_ = bf16[1,64,2304]{2,1,0:T(8,128)(2,1)} collective-permute-done((bf16[1,64,2304]{2,1,0:T(8,128)(2,1)}, bf16[1,64,2304]{2,1,0:T(8,128)(2,1)}, u32[]{:S(2)}, u32[]{:S(2)}) %collective-permute-start.78) | collective-permute-done | bytes 294944 | tf_op jit(solution)/shard_map/cond/branch_1_fun/cond/branch_1_fun/ppermute | solution.py:79
  81.7 3.3 %cycle_late.7 = (f32[128,512]{1,0:T(8,128)}, f32[128,512]{1,0:T(8,128)S(1)}) custom-call(bf16[2,64,2304]{2,1,0:T(8,128)(2,1)S(1)} %collective-permute-done.74.refs_0_, bf16[1,64,2304]{2,1,0:T(8,128)(2,1)} %collective-permute-done.75.refs_1_, bf16[1,64,2304]{2,1,0:T(8,128)(2,1)} %collective-permute-done.76.refs_2_, ...), custom_call_target="tpu_custom_call" | custom-call | tf_op jit(solution)/shard_map/cond/branch_1_fun/cond/branch_1_fun/cycle_late/pallas_call | solution.py:476
  85.1 3.4 %ladder_late.7 = (f32[8,64,512]{2,1,0:T(8,128)S(1)}, f32[8,64,512]{2,1,0:T(8,128)S(1)}) custom-call(bf16[2,64,2304]{2,1,0:T(8,128)(2,1)S(1)} %collective-permute-done.74.refs_0_, bf16[1,64,2304]{2,1,0:T(8,128)(2,1)} %collective-permute-done.75.refs_1_, bf16[1,64,2304]{2,1,0:T(8,128)(2,1)} %collective-permute-done.76.refs_2_, ...), custom_call_target="tpu_custom_call" | custom-call | tf_op jit(solution)/shard_map/cond/branch_1_fun/cond/branch_1_fun/ladder_late/pallas_call | solution.py:322
  88.5 0.1 collective-permute-start.87
  88.6 0.7 collective-permute-start.88
  89.3 0.2 slice_reduce_fusion.7
  89.5 0.7 fusion.54
  90.2 0.7 fusion.50
  90.9 1.0 %select_select_fusion.3 = f32[128,512]{1,0:T(8,128)S(1)} fusion(f32[128,512]{1,0:T(8,128)} %copy-done.47, f32[128,512]{1,0:T(8,128)S(1)} %collective-permute-done.88, f32[128,512]{1,0:T(8,128)} %get-tuple-element.251, pred[]{:T(512)S(6)} %eq.146, pred[]{:T(512)S(6)} %eq.143), kind=kLoop, calls=%fused_computation.114 | loop fusion | flops 131072 | bytes 1048578 | tf_op jit(solution)/shard_map/cond/branch_1_fun/cond/branch_1_fun/jit(_where)/select_n | solution.py:538
  92.0 1.4 %collective-permute-start.91 = (f32[32,512]{1,0:T(8,128)S(1)}, f32[32,512]{1,0:T(8,128)S(1)}, u32[]{:S(2)}, u32[]{:S(2)}) collective-permute-start(f32[32,512]{1,0:T(8,128)S(1)} %get-tuple-element.320), channel_id=1, source_target_pairs={{0,6},{1,7},{2,4},{3,5},{4,2},{5,3},{6,0},{7,1},{8,14},{9,15},{10,... | collective-permute-start | bytes 196616 | tf_op jit(solution)/shard_map/cond/branch_1_fun/cond/branch_1_fun/ppermute | solution.py:79
  93.4 1.1 %collective-permute-start.90 = (f32[32,512]{1,0:T(8,128)S(1)}, f32[32,512]{1,0:T(8,128)S(1)}, u32[]{:S(2)}, u32[]{:S(2)}) collective-permute-start(f32[32,512]{1,0:T(8,128)S(1)} %get-tuple-element.321), channel_id=1, source_target_pairs={{0,4},{1,5},{2,6},{3,7},{4,0},{5,1},{6,2},{7,3},{8,12},{9,13},{10,... | collective-permute-start | bytes 196616 | tf_op jit(solution)/shard_map/cond/branch_1_fun/cond/branch_1_fun/ppermute | solution.py:79
  94.5 1.0 %collective-permute-start.89 = (f32[32,512]{1,0:T(8,128)S(1)}, f32[32,512]{1,0:T(8,128)S(1)}, u32[]{:S(2)}, u32[]{:S(2)}) collective-permute-start(f32[32,512]{1,0:T(8,128)S(1)} %get-tuple-element.319), channel_id=1, source_target_pairs={{0,2},{1,3},{2,0},{3,1},{4,6},{5,7},{6,4},{7,5},{8,10},{9,11},{10,... | collective-permute-start | bytes 196616 | tf_op jit(solution)/shard_map/cond/branch_1_fun/cond/branch_1_fun/ppermute | solution.py:79
  95.5 0.7 fusion.56
  96.2 1.4 %collective-permute-done.91 = f32[32,512]{1,0:T(8,128)S(1)} collective-permute-done((f32[32,512]{1,0:T(8,128)S(1)}, f32[32,512]{1,0:T(8,128)S(1)}, u32[]{:S(2)}, u32[]{:S(2)}) %collective-permute-start.91) | collective-permute-done | bytes 65568 | tf_op jit(solution)/shard_map/cond/branch_1_fun/cond/branch_1_fun/ppermute | solution.py:79
  97.5 1.3 %collective-permute-done.90 = f32[32,512]{1,0:T(8,128)S(1)} collective-permute-done((f32[32,512]{1,0:T(8,128)S(1)}, f32[32,512]{1,0:T(8,128)S(1)}, u32[]{:S(2)}, u32[]{:S(2)}) %collective-permute-start.90) | collective-permute-done | bytes 65568 | tf_op jit(solution)/shard_map/cond/branch_1_fun/cond/branch_1_fun/ppermute | solution.py:79
  98.9 0.1 collective-permute-done.89
  99.0 0.7 fusion.49
  99.7 1.5 %ladder_end.7 = bf16[480,512]{1,0:T(8,128)(2,1)} custom-call(s32[2,2]{1,0:T(2,128)S(1)} %copy-done.60, f32[8,64,512]{2,1,0:T(8,128)S(1)} %get-tuple-element.253.mine, f32[8,64,512]{2,1,0:T(8,128)S(1)} %collective-permute-done.87.other), custom_call_target="tpu_custom_call" | custom-call | tf_op jit(solution)/shard_map/cond/branch_1_fun/cond/branch_1_fun/ladder_end/pallas_call | solution.py:355
  (45 shorter events, 0.2 us)
Async XLA Ops:
  0.6 6.6 %collective-permute-start.92 = (bf16[60,4096]{1,0:T(8,128)(2,1)}, bf16[60,4096]{1,0:T(8,128)(2,1)S(1)}, u32[]{:S(2)}, u32[]{:S(2)}) collective-permute-start(bf16[60,4096]{1,0:T(8,128)(2,1)} %param.26), channel_id=1, source_target_pairs={{0,1},{2,3},{4,5},{6,7},{8,9},{10,11},{12,13},{14,15},{16,17},{18,... | collective-permute-start | bytes 1474568 | tf_op jit(solution)/shard_map/ppermute | solution.py:107
  9.4 35.3 %copy-start.56 = (bf16[1,4,120,512]{3,2,1,0:T(8,128)(2,1)S(1)}, bf16[1,4,120,512]{3,2,1,0:T(8,128)(2,1)}, u32[]{:S(2)}) copy-start(bf16[1,4,120,512]{3,2,1,0:T(8,128)(2,1)} %get-tuple-element.245) | copy-start | bytes 1474564 | tf_op jit(solution)/shard_map/cond/branch_1_fun/cond
  11.9 54.8 %copy-start.6 = (bf16[64,2304]{1,0:T(8,128)(2,1)S(1)}, bf16[64,2304]{1,0:T(8,128)(2,1)}, u32[]{:S(2)}) copy-start(bf16[64,2304]{1,0:T(8,128)(2,1)} %prep.7) | copy-start | bytes 884740 | tf_op jit(solution)/shard_map/cond/branch_1_fun/cond
  11.9 12.2 %collective-permute-start.70 = (bf16[1,64,2304]{2,1,0:T(8,128)(2,1)}, bf16[1,64,2304]{2,1,0:T(8,128)(2,1)S(1)}, u32[]{:S(2)}, u32[]{:S(2)}) collective-permute-start(bf16[1,64,2304]{2,1,0:T(8,128)(2,1)} %bitcast.177), channel_id=1, source_target_pairs={{0,24},{1,25},{2,26},{3,27},{4,28},{5,29},{6,30},{7,31},{8,0},{9,1... | collective-permute-start | bytes 884744 | tf_op jit(solution)/shard_map/cond/branch_1_fun/cond/branch_1_fun/ppermute | solution.py:79
  16.3 13.3 %collective-permute-start.69 = (bf16[1,64,2304]{2,1,0:T(8,128)(2,1)}, bf16[1,64,2304]{2,1,0:T(8,128)(2,1)S(1)}, u32[]{:S(2)}, u32[]{:S(2)}) collective-permute-start(bf16[1,64,2304]{2,1,0:T(8,128)(2,1)} %bitcast.178), channel_id=1, source_target_pairs={{0,8},{1,9},{2,10},{3,11},{4,12},{5,13},{6,14},{7,15},{8,16},{9,17... | collective-permute-start | bytes 884744 | tf_op jit(solution)/shard_map/cond/branch_1_fun/cond/branch_1_fun/ppermute | solution.py:79
  16.3 13.4 %collective-permute-start.71 = (bf16[1,64,2304]{2,1,0:T(8,128)(2,1)}, bf16[1,64,2304]{2,1,0:T(8,128)(2,1)S(1)}, u32[]{:S(2)}, u32[]{:S(2)}) collective-permute-start(bf16[1,64,2304]{2,1,0:T(8,128)(2,1)} %bitcast.179), channel_id=1, source_target_pairs={{0,2},{1,5},{2,0},{3,7},{4,6},{5,1},{6,4},{7,3},{8,10},{9,13},{10,... | collective-permute-start | bytes 884744 | tf_op jit(solution)/shard_map/cond/branch_1_fun/cond/branch_1_fun/ppermute | solution.py:79
  17.8 11.9 %collective-permute-start.72 = (bf16[1,64,2304]{2,1,0:T(8,128)(2,1)}, bf16[1,64,2304]{2,1,0:T(8,128)(2,1)S(1)}, u32[]{:S(2)}, u32[]{:S(2)}) collective-permute-start(bf16[1,64,2304]{2,1,0:T(8,128)(2,1)} %bitcast.180), channel_id=1, source_target_pairs={{0,4},{1,3},{2,6},{3,1},{4,0},{5,7},{6,2},{7,5},{8,12},{9,11},{10,... | collective-permute-start | bytes 884744 | tf_op jit(solution)/shard_map/cond/branch_1_fun/cond/branch_1_fun/ppermute | solution.py:79
  29.7 38.4 %copy-start.34 = (bf16[1,64,2304]{2,1,0:T(8,128)(2,1)}, bf16[1,64,2304]{2,1,0:T(8,128)(2,1)S(1)}, u32[]{:S(2)}) copy-start(bf16[1,64,2304]{2,1,0:T(8,128)(2,1)S(1)} %collective-permute-done.71.refs_1_) | copy-start | bytes 884740 | tf_op jit(solution)/shard_map/cond/branch_1_fun/cond
  29.7 38.4 %copy-start.36 = (bf16[1,64,2304]{2,1,0:T(8,128)(2,1)}, bf16[1,64,2304]{2,1,0:T(8,128)(2,1)S(1)}, u32[]{:S(2)}) copy-start(bf16[1,64,2304]{2,1,0:T(8,128)(2,1)S(1)} %collective-permute-done.72.refs_2_) | copy-start | bytes 884740 | tf_op jit(solution)/shard_map/cond/branch_1_fun/cond
  29.7 15.0 %collective-permute-start.75 = (bf16[1,64,2304]{2,1,0:T(8,128)(2,1)}, bf16[1,64,2304]{2,1,0:T(8,128)(2,1)}, u32[]{:S(2)}, u32[]{:S(2)}) collective-permute-start(bf16[1,64,2304]{2,1,0:T(8,128)(2,1)} %bitcast.181), channel_id=1, source_target_pairs={{0,16},{1,17},{2,18},{3,19},{4,20},{5,21},{6,22},{7,23},{8,24},{9,... | collective-permute-start | bytes 884744 | tf_op jit(solution)/shard_map/cond/branch_1_fun/cond/branch_1_fun/ppermute | solution.py:79
  30.5 32.6 %collective-permute-start.73 = (bf16[2,64,2304]{2,1,0:T(8,128)(2,1)S(1)}, bf16[2,64,2304]{2,1,0:T(8,128)(2,1)S(1)}, u32[]{:S(2)}, u32[]{:S(2)}) collective-permute-start(bf16[2,64,2304]{2,1,0:T(8,128)(2,1)S(1)} %pad_maximum_fusion.5.refs_4_), channel_id=1, source_target_pairs={{0,2},{1,5},{2,0},{3,7},{4,6},{5,1},{6,4},{7,3},{8,10},{9,13},{10,... | collective-permute-start | bytes 1769480 | tf_op jit(solution)/shard_map/cond/branch_1_fun/cond/branch_1_fun/ppermute | solution.py:79
  32.0 33.2 %collective-permute-start.81 = (bf16[2,64,2304]{2,1,0:T(8,128)(2,1)S(1)}, bf16[2,64,2304]{2,1,0:T(8,128)(2,1)S(1)}, u32[]{:S(2)}, u32[]{:S(2)}) collective-permute-start(bf16[2,64,2304]{2,1,0:T(8,128)(2,1)S(1)} %pad_maximum_fusion.5.refs_4_), channel_id=1, source_target_pairs={{0,4},{1,3},{2,6},{3,1},{4,0},{5,7},{6,2},{7,5},{8,12},{9,11},{10,... | collective-permute-start | bytes 1769480 | tf_op jit(solution)/shard_map/cond/branch_1_fun/cond/branch_1_fun/ppermute | solution.py:79
  44.8 7.9 %collective-permute-start.82 = (bf16[4,120,128]{2,1,0:T(8,128)(2,1)S(1)}, bf16[4,120,128]{2,1,0:T(8,128)(2,1)S(1)}, u32[]{:S(2)}, u32[]{:S(2)}) collective-permute-start(bf16[4,120,128]{2,1,0:T(8,128)(2,1)S(1)} %get-tuple-element.317), channel_id=1, source_target_pairs={{0,8},{1,9},{2,10},{3,11},{4,12},{5,13},{6,14},{7,15},{8,16},{9,17... | collective-permute-start | bytes 368648 | tf_op jit(solution)/shard_map/cond/branch_1_fun/cond/branch_1_fun/ppermute | solution.py:79
  44.9 16.3 %collective-permute-start.80 = (bf16[1,64,2304]{2,1,0:T(8,128)(2,1)S(1)}, bf16[1,64,2304]{2,1,0:T(8,128)(2,1)S(1)}, u32[]{:S(2)}, u32[]{:S(2)}) collective-permute-start(bf16[1,64,2304]{2,1,0:T(8,128)(2,1)S(1)} %collective-permute-done.71.refs_1_), channel_id=1, source_target_pairs={{0,4},{1,3},{2,6},{3,1},{4,0},{5,7},{6,2},{7,5},{8,12},{9,11},{10,... | collective-permute-start | bytes 884744 | tf_op jit(solution)/shard_map/cond/branch_1_fun/cond/branch_1_fun/ppermute | solution.py:79
  46.5 9.6 %collective-permute-start.83 = (bf16[4,120,128]{2,1,0:T(8,128)(2,1)S(1)}, bf16[4,120,128]{2,1,0:T(8,128)(2,1)S(1)}, u32[]{:S(2)}, u32[]{:S(2)}) collective-permute-start(bf16[4,120,128]{2,1,0:T(8,128)(2,1)S(1)} %get-tuple-element.316), channel_id=1, source_target_pairs={{0,16},{1,17},{2,18},{3,19},{4,20},{5,21},{6,22},{7,23},{8,24},{9,... | collective-permute-start | bytes 368648 | tf_op jit(solution)/shard_map/cond/branch_1_fun/cond/branch_1_fun/ppermute | solution.py:79
  52.8 6.2 %collective-permute-start.84 = (bf16[4,120,128]{2,1,0:T(8,128)(2,1)S(1)}, bf16[4,120,128]{2,1,0:T(8,128)(2,1)S(1)}, u32[]{:S(2)}, u32[]{:S(2)}) collective-permute-start(bf16[4,120,128]{2,1,0:T(8,128)(2,1)S(1)} %get-tuple-element.315), channel_id=1, source_target_pairs={{0,24},{1,25},{2,26},{3,27},{4,28},{5,29},{6,30},{7,31},{8,0},{9,1... | collective-permute-start | bytes 368648 | tf_op jit(solution)/shard_map/cond/branch_1_fun/cond/branch_1_fun/ppermute | solution.py:79
  56.1 14.9 %collective-permute-start.79 = (bf16[1024,512]{1,0:T(8,128)(2,1)}, bf16[1024,512]{1,0:T(8,128)(2,1)}, u32[]{:S(2)}, u32[]{:S(2)}) collective-permute-start(bf16[1024,512]{1,0:T(8,128)(2,1)} %get-tuple-element.241), channel_id=1, source_target_pairs={{0,1},{2,3},{4,5},{6,7},{8,9},{10,11},{12,13},{14,15},{16,17},{18,... | collective-permute-start | bytes 3145736 | tf_op jit(solution)/shard_map/cond/branch_1_fun/cond/branch_1_fun/ppermute | solution.py:107
  58.9 9.2 %collective-permute-start.76 = (bf16[1,64,2304]{2,1,0:T(8,128)(2,1)}, bf16[1,64,2304]{2,1,0:T(8,128)(2,1)}, u32[]{:S(2)}, u32[]{:S(2)}) collective-permute-start(bf16[1,64,2304]{2,1,0:T(8,128)(2,1)} %collective-permute-done.75.refs_1_), channel_id=1, source_target_pairs={{0,2},{1,5},{2,0},{3,7},{4,6},{5,1},{6,4},{7,3},{8,10},{9,13},{10,... | collective-permute-start | bytes 884744 | tf_op jit(solution)/shard_map/cond/branch_1_fun/cond/branch_1_fun/ppermute | solution.py:79
  61.2 9.7 %copy-start.38 = (bf16[1,64,2304]{2,1,0:T(8,128)(2,1)}, bf16[1,64,2304]{2,1,0:T(8,128)(2,1)S(1)}, u32[]{:S(2)}) copy-start(bf16[1,64,2304]{2,1,0:T(8,128)(2,1)S(1)} %collective-permute-done.80.refs_3_) | copy-start | bytes 884740 | tf_op jit(solution)/shard_map/cond/branch_1_fun/cond
  61.2 7.7 %collective-permute-start.86 = (bf16[768,128]{1,0:T(8,128)(2,1)}, bf16[768,128]{1,0:T(8,128)(2,1)}, u32[]{:S(2)}, u32[]{:S(2)}) collective-permute-start(bf16[768,128]{1,0:T(8,128)(2,1)} %get-tuple-element.250), channel_id=1, source_target_pairs={{0,1},{2,3},{4,5},{6,7},{8,9},{10,11},{12,13},{14,15},{16,17},{18,... | collective-permute-start | bytes 589832 | tf_op jit(solution)/shard_map/cond/branch_1_fun/cond/branch_1_fun/ppermute | solution.py:107
  63.2 7.8 %collective-permute-start.85 = (bf16[1280,128]{1,0:T(8,128)(2,1)}, bf16[1280,128]{1,0:T(8,128)(2,1)}, u32[]{:S(2)}, u32[]{:S(2)}) collective-permute-start(bf16[1280,128]{1,0:T(8,128)(2,1)} %get-tuple-element.248), channel_id=1, source_target_pairs={{0,1},{2,3},{4,5},{6,7},{8,9},{10,11},{12,13},{14,15},{16,17},{18,... | collective-permute-start | bytes 983048 | tf_op jit(solution)/shard_map/cond/branch_1_fun/cond/branch_1_fun/ppermute | solution.py:107
  65.2 5.8 %copy-start.48 = (bf16[4096,512]{1,0:T(8,128)(2,1)S(1)}, bf16[4096,512]{1,0:T(8,128)(2,1)}, u32[]{:S(2)}) copy-start(bf16[4096,512]{1,0:T(8,128)(2,1)} %get-tuple-element.242) | copy-start | bytes 12582916 | tf_op jit(solution)/shard_map/cond/branch_1_fun/cond
  65.2 14.7 %collective-permute-start.77 = (bf16[1,64,2304]{2,1,0:T(8,128)(2,1)}, bf16[1,64,2304]{2,1,0:T(8,128)(2,1)}, u32[]{:S(2)}, u32[]{:S(2)}) collective-permute-start(bf16[1,64,2304]{2,1,0:T(8,128)(2,1)} %collective-permute-done.75.refs_1_), channel_id=1, source_target_pairs={{0,4},{1,3},{2,6},{3,1},{4,0},{5,7},{6,2},{7,5},{8,12},{9,11},{10,... | collective-permute-start | bytes 884744 | tf_op jit(solution)/shard_map/cond/branch_1_fun/cond/branch_1_fun/ppermute | solution.py:79
  68.1 2.9 %copy-start.23 = (bf16[1280,512]{1,0:T(8,128)(2,1)}, bf16[1280,512]{1,0:T(8,128)(2,1)S(1)}, u32[]{:S(2)}) copy-start(bf16[1280,512]{1,0:T(8,128)(2,1)S(1)} %get-tuple-element.243.refs_5_) | copy-start | bytes 3932164 | tf_op jit(solution)/shard_map/cond/branch_1_fun/cond
  68.1 2.9 %copy-start.25 = (bf16[1280,512]{1,0:T(8,128)(2,1)}, bf16[1280,512]{1,0:T(8,128)(2,1)S(1)}, u32[]{:S(2)}) copy-start(bf16[1280,512]{1,0:T(8,128)(2,1)S(1)} %get-tuple-element.244.refs_6_) | copy-start | bytes 3932164 | tf_op jit(solution)/shard_map/cond/branch_1_fun/cond
  68.1 13.6 %collective-permute-start.74 = (bf16[2,64,2304]{2,1,0:T(8,128)(2,1)S(1)}, bf16[2,64,2304]{2,1,0:T(8,128)(2,1)S(1)}, u32[]{:S(2)}, u32[]{:S(2)}) collective-permute-start(bf16[2,64,2304]{2,1,0:T(8,128)(2,1)S(1)} %collective-permute-done.73.refs_5_), channel_id=1, source_target_pairs={{0,4},{1,3},{2,6},{3,1},{4,0},{5,7},{6,2},{7,5},{8,12},{9,11},{10,... | collective-permute-start | bytes 1769480 | tf_op jit(solution)/shard_map/cond/branch_1_fun/cond/branch_1_fun/ppermute | solution.py:79
  68.9 12.8 %collective-permute-start.78 = (bf16[1,64,2304]{2,1,0:T(8,128)(2,1)}, bf16[1,64,2304]{2,1,0:T(8,128)(2,1)}, u32[]{:S(2)}, u32[]{:S(2)}) collective-permute-start(bf16[1,64,2304]{2,1,0:T(8,128)(2,1)} %collective-permute-done.76.refs_2_), channel_id=1, source_target_pairs={{0,4},{1,3},{2,6},{3,1},{4,0},{5,7},{6,2},{7,5},{8,12},{9,11},{10,... | collective-permute-start | bytes 884744 | tf_op jit(solution)/shard_map/cond/branch_1_fun/cond/branch_1_fun/ppermute | solution.py:79
  73.1 1.0 copy-start.35
  74.0 1.0 copy-start.37
  75.0 1.0 copy-start.39
  76.0 5.7 %copy-start.24 = (bf16[1280,512]{1,0:T(8,128)(2,1)S(1)}, bf16[1280,512]{1,0:T(8,128)(2,1)}, u32[]{:S(2)}) copy-start(bf16[1280,512]{1,0:T(8,128)(2,1)} %copy-done.23) | copy-start | bytes 3932164 | tf_op jit(solution)/shard_map/cond/branch_1_fun/cond
  76.0 5.7 %copy-start.26 = (bf16[1280,512]{1,0:T(8,128)(2,1)S(1)}, bf16[1280,512]{1,0:T(8,128)(2,1)}, u32[]{:S(2)}) copy-start(bf16[1280,512]{1,0:T(8,128)(2,1)} %copy-done.25) | copy-start | bytes 3932164 | tf_op jit(solution)/shard_map/cond/branch_1_fun/cond
  76.0 5.7 %copy-start.45 = (bf16[768,128]{1,0:T(8,128)(2,1)S(1)}, bf16[768,128]{1,0:T(8,128)(2,1)}, u32[]{:S(2)}) copy-start(bf16[768,128]{1,0:T(8,128)(2,1)} %broadcast_select_fusion.7.refs_8_) | copy-start | bytes 589828 | tf_op jit(solution)/shard_map/cond/branch_1_fun/cond
  79.9 5.1 %copy-start.52 = (bf16[2304,512]{1,0:T(8,128)(2,1)S(1)}, bf16[2304,512]{1,0:T(8,128)(2,1)}, u32[]{:S(2)}) copy-start(bf16[2304,512]{1,0:T(8,128)(2,1)} %get-tuple-element.339.refs_7_.refs_5_) | copy-start | bytes 7077892 | tf_op jit(solution)/shard_map/cond/branch_1_fun/cond
  85.0 3.4 %copy-start.47 = (f32[128,512]{1,0:T(8,128)}, f32[128,512]{1,0:T(8,128)S(1)}, u32[]{:S(2)}) copy-start(f32[128,512]{1,0:T(8,128)S(1)} %get-tuple-element.255) | copy-start | bytes 786436 | tf_op jit(solution)/shard_map/cond/branch_1_fun/cond
  85.0 4.2 %copy-start.60 = (s32[2,2]{1,0:T(2,128)S(1)}, s32[2,2]{1,0:T(2,128)}, u32[]{:S(2)}) copy-start(s32[2,2]{1,0:T(2,128)} %get-tuple-element.233.dims) | copy-start | bytes 52 | tf_op jit(solution)/shard_map/cond/branch_1_fun/cond
  88.5 11.2 %collective-permute-start.87 = (f32[8,64,512]{2,1,0:T(8,128)S(1)}, f32[8,64,512]{2,1,0:T(8,128)S(1)}, u32[]{:S(2)}, u32[]{:S(2)}) collective-permute-start(f32[8,64,512]{2,1,0:T(8,128)S(1)} %get-tuple-element.254), channel_id=1, source_target_pairs={{0,1},{1,0},{2,3},{3,2},{4,5},{5,4},{6,7},{7,6},{8,9},{9,8},{10,11... | collective-permute-start | bytes 3145736 | tf_op jit(solution)/shard_map/cond/branch_1_fun/cond/branch_1_fun/ppermute | solution.py:107
  88.6 2.3 %collective-permute-start.88 = (f32[128,512]{1,0:T(8,128)}, f32[128,512]{1,0:T(8,128)S(1)}, u32[]{:S(2)}, u32[]{:S(2)}) collective-permute-start(f32[128,512]{1,0:T(8,128)} %get-tuple-element.251), channel_id=1, source_target_pairs={{7,6},{15,14},{23,22},{31,30}} | collective-permute-start | bytes 786440 | tf_op jit(solution)/shard_map/cond/branch_1_fun/cond/branch_1_fun/ppermute | solution.py:535
  92.0 5.6 %collective-permute-start.91 = (f32[32,512]{1,0:T(8,128)S(1)}, f32[32,512]{1,0:T(8,128)S(1)}, u32[]{:S(2)}, u32[]{:S(2)}) collective-permute-start(f32[32,512]{1,0:T(8,128)S(1)} %get-tuple-element.320), channel_id=1, source_target_pairs={{0,6},{1,7},{2,4},{3,5},{4,2},{5,3},{6,0},{7,1},{8,14},{9,15},{10,... | collective-permute-start | bytes 196616 | tf_op jit(solution)/shard_map/cond/branch_1_fun/cond/branch_1_fun/ppermute | solution.py:79
  93.4 5.5 %collective-permute-start.90 = (f32[32,512]{1,0:T(8,128)S(1)}, f32[32,512]{1,0:T(8,128)S(1)}, u32[]{:S(2)}, u32[]{:S(2)}) collective-permute-start(f32[32,512]{1,0:T(8,128)S(1)} %get-tuple-element.321), channel_id=1, source_target_pairs={{0,4},{1,5},{2,6},{3,7},{4,0},{5,1},{6,2},{7,3},{8,12},{9,13},{10,... | collective-permute-start | bytes 196616 | tf_op jit(solution)/shard_map/cond/branch_1_fun/cond/branch_1_fun/ppermute | solution.py:79
  94.5 4.5 %collective-permute-start.89 = (f32[32,512]{1,0:T(8,128)S(1)}, f32[32,512]{1,0:T(8,128)S(1)}, u32[]{:S(2)}, u32[]{:S(2)}) collective-permute-start(f32[32,512]{1,0:T(8,128)S(1)} %get-tuple-element.319), channel_id=1, source_target_pairs={{0,2},{1,3},{2,0},{3,1},{4,6},{5,7},{6,4},{7,5},{8,10},{9,11},{10,... | collective-permute-start | bytes 196616 | tf_op jit(solution)/shard_map/cond/branch_1_fun/cond/branch_1_fun/ppermute | solution.py:79

commit v2 on v1

--- a/solution.py
+++ b/solution.py
@@ -215,17 +215,15 @@
 VMEM = pl.BlockSpec(memory_space=pltpu.VMEM)
 SMEM = pl.BlockSpec(memory_space=pltpu.SMEM)
 ROOM = pltpu.CompilerParams(vmem_limit_bytes=48 * 1024 * 1024)
-EARLY_PIECES = 10
-
-
-def slots_kernel(part_0, part_1, part_2, part_3, early, late, other_early, other_late):
+STAGES = (10, 4, 2)
+
+
+def slots_kernel(part_0, part_1, part_2, part_3, here, there):
     core, blk_index = lax.axis_index("slab"), lax.axis_index("blk")
     occupied = part_0.shape[1]
     slot = lax.broadcasted_iota(jnp.int32, (128, 1), 0)
     at = lax.broadcasted_iota(jnp.int32, (128, occupied), 1)
-    cut = 8 * EARLY_PIECES
-    rest = 128 - cut
-    for order, first_pieces, last_pieces in ((core, early, late), (1 - core, other_early, other_late)):
+    for order, out in ((core, here), (1 - core, there)):
         chip = chip_of(slot >> 3, order, blk_index)
         k = 15 * (chip >> 1) + 7 * (chip & 1) + (slot & 7)
         pick = jnp.where(at == k, 1.0, 0.0).astype(jnp.bfloat16)
@@ -234,22 +232,21 @@
             part = jnp.concatenate([part[c] for c in range(4)], 1)
             rows = jnp.dot(pick, part, preferred_element_type=jnp.float32).astype(jnp.bfloat16)
             for c in range(4):
-                of_c = rows[:, 128 * c : 128 * c + 128]
-                first_pieces[pl.ds(pl.multiple_of((first + c) * cut, 16), cut), :] = of_c[:cut]
-                last_pieces[pl.ds(pl.multiple_of((first + c) * rest, 16), rest), :] = of_c[cut:]
+                lo = 0
+                for stage in STAGES:
+                    each = 8 * stage
+                    to = pl.multiple_of(GROUP * lo + (first + c) * each, 16)
+                    out[pl.ds(to, each), :] = rows[lo : lo + each, 128 * c : 128 * c + 128]
+                    lo += each
 
 
 def slots_of_pieces(parts):
-    rows = 8 * EARLY_PIECES
-    shapes = [
-        jax.ShapeDtypeStruct((GROUP * rows, 128), jnp.bfloat16),
-        jax.ShapeDtypeStruct((GROUP * (128 - rows), 128), jnp.bfloat16),
-    ]
+    shape = jax.ShapeDtypeStruct((GROUP * 128, 128), jnp.bfloat16)
     return pl.pallas_call(
         slots_kernel,
-        out_shape=shapes * 2,
+        out_shape=[shape, shape],
         in_specs=[VMEM] * 4,
-        out_specs=[VMEM] * 4,
+        out_specs=[VMEM] * 2,
         compiler_params=ROOM,
         name="slots",
     )(*parts)
@@ -271,63 +268,63 @@
     lax.fori_loop(0, depth // step, body, 0)
 
 
-def ladder_early_kernel(*refs):
+def ladder_part_kernel(*refs):
     products(refs[:-2], refs[-2], refs[-1])
 
 
-def ladder_early(pieces, rows_w):
-    shape = (EARLY_PIECES * PIECE, rows_w.shape[1])
-    return pl.pallas_call(
-        ladder_early_kernel,
+def ladder_part(pieces, rows_w):
+    count = sum(piece.shape[0] for piece in pieces)
+    shape = (count * PIECE, rows_w.shape[1])
+    return pl.pallas_call(
+        ladder_part_kernel,
         out_shape=jax.ShapeDtypeStruct(shape, jnp.float32),
         in_specs=[VMEM] * (len(pieces) + 1),
         out_specs=VMEM,
         compiler_params=ROOM,
-        name="ladder_early",
+        name="ladder_part",
     )(*pieces, rows_w)
 
 
 def ladder_late_kernel(*refs):
-    pieces = refs[:-5]
-    rows_w, early, mine, other, total = refs[-5:]
+    pieces = refs[:-6]
+    rows_w, early, middle, mine, other, total = refs[-6:]
     core, blk_index = lax.axis_index("slab"), lax.axis_index("blk")
     products(pieces, rows_w, total)
 
-    def place(n, value):
-        chip = chip_of(n, core, blk_index)
-
-        @pl.when(chip // 8 == core)
-        def _():
-            mine[chip & 7] = value
-
-        @pl.when(chip // 8 != core)
-        def _():
-            other[chip & 7] = value
-
-    def of_early(n, carry):
-        place(n, early[pl.ds(pl.multiple_of(n * PIECE, PIECE), PIECE), :])
-        return carry
-
-    def of_late(n, carry):
-        place(n + EARLY_PIECES, total[pl.ds(pl.multiple_of(n * PIECE, PIECE), PIECE), :])
-        return carry
-
-    lax.fori_loop(0, EARLY_PIECES, of_early, 0)
-    lax.fori_loop(0, 16 - EARLY_PIECES, of_late, 0)
-
-
-def ladder_late(pieces, rows_w, early):
+    def place(first, sums):
+        def body(n, carry):
+            chip = chip_of(first + n, core, blk_index)
+            value = sums[pl.ds(pl.multiple_of(n * PIECE, PIECE), PIECE), :]
+
+            @pl.when(chip // 8 == core)
+            def _():
+                mine[chip & 7] = value
+
+            @pl.when(chip // 8 != core)
+            def _():
+                other[chip & 7] = value
+
+            return carry
+
+        lax.fori_loop(0, sums.shape[0] // PIECE, body, 0)
+
+    place(0, early)
+    place(STAGES[0], middle)
+    place(STAGES[0] + STAGES[1], total)
+
+
+def ladder_late(pieces, rows_w, early, middle):
     out_columns = rows_w.shape[1]
     half = jax.ShapeDtypeStruct((8, PIECE, out_columns), jnp.float32)
     return pl.pallas_call(
         ladder_late_kernel,
         out_shape=[half, half],
-        in_specs=[VMEM] * (len(pieces) + 2),
+        in_specs=[VMEM] * (len(pieces) + 3),
         out_specs=[VMEM, VMEM],
-        scratch_shapes=[pltpu.VMEM(((16 - EARLY_PIECES) * PIECE, out_columns), jnp.float32)],
+        scratch_shapes=[pltpu.VMEM((STAGES[2] * PIECE, out_columns), jnp.float32)],
         compiler_params=ROOM,
         name="ladder_late",
-    )(*pieces, rows_w, early)
+    )(*pieces, rows_w, early, middle)
 
 
 def ladder_end_kernel(dims, mine, other, out, rows):
@@ -439,59 +436,68 @@
     )(*pieces)
 
 
-def cycle_late_kernel(width, least, *refs):
-    pieces, refs = refs[:-10], refs[-10:]
-    turned_first, turned_own, slots_first, late_first, slots_own, late_own, first, own = refs[:8]
-    spread, turned = refs[8:]
+def cycle_sum_kernel(width, least, row, turned_before, *refs):
+    pieces, refs = refs[:-8], refs[-8:]
+    before_first, before_own, slots_first, slots_own, first, own, spread, turned = refs
     core, plane = lax.axis_index("slab"), lax.axis_index("blk") & 3
     first_start, own_start = group_starts(width, least, core, plane)
 
-    def total(slots, early, slots_late, out):
-        pairs = ((slots, early), (slots_late, turned))
-        out[...] = sum(
-            lax.dot_general(
-                left[...], right[...], (((0,), (0,)), ((), ())), preferred_element_type=jnp.float32
-            )
-            for left, right in pairs
+    def add(slots, row, right):
+        return lax.dot_general(
+            slots[row : row + right.shape[0], :],
+            right[...],
+            (((0,), (0,)), ((), ())),
+            preferred_element_type=jnp.float32,
         )
+
+    def total(group_width, start, slots, before, out):
+        turn(pieces, group_width, start, spread, turned)
+        if turned_before:
+            out[...] = add(slots, 0, before) + add(slots, row, turned)
+        else:
+            out[...] = before[...] + add(slots, row, turned)
 
     first[...] = jnp.zeros_like(first)
     own[...] = jnp.zeros_like(own)
 
     @pl.when(first_part(core, plane))
     def _():
-        turn(pieces, width, first_start, spread, turned)
-        total(slots_first, turned_first, late_first, first)
+        total(width, first_start, slots_first, before_first, first)
 
     @pl.when(core == 1)
     def _():
-        turn(pieces, least, own_start, spread, turned)
-        total(slots_own, turned_own, late_own, own)
-
-
-def cycle_late(width, least, pieces, turned, slots_first, slots_own):
-    count = sum(p.shape[0] for p in pieces)
+        total(least, own_start, slots_own, before_own, own)
+
+
+def cycle_add(width, least, stage, pieces, before, slots_first, slots_own):
+    count = STAGES[stage]
     shape = jax.ShapeDtypeStruct((128, 8 * BS), jnp.float32)
     blocks = GROUP * max(width, least) // 128 + 1
-    return pl.pallas_call(
-        functools.partial(cycle_late_kernel, width, least),
+    row = GROUP * 8 * sum(STAGES[:stage])
+    turned_before = before[0].dtype == jnp.bfloat16
+    return pl.pallas_call(
+        functools.partial(cycle_sum_kernel, width, least, row, turned_before),
         out_shape=[shape, shape],
-        in_specs=[VMEM] * (6 + len(pieces)),
+        in_specs=[VMEM] * (4 + len(pieces)),
         out_specs=[VMEM, VMEM],
         scratch_shapes=[
             pltpu.VMEM((blocks * count * PIECE, 128), jnp.float32),
             pltpu.VMEM((GROUP * 8 * count, 8 * BS), jnp.bfloat16),
         ],
         compiler_params=ROOM,
-        name="cycle_late",
-    )(*pieces, *turned, *slots_first, *slots_own)
+        name="cycle_sum",
+    )(*pieces, *before, slots_first, slots_own)
+
+
+def together(*values):
+    return lax.optimization_barrier(values)
 
 
 def after(value, *others):
-    return lax.optimization_barrier((value,) + others)[0]
-
-
-def compacted(width, least, amplitudes, ladder_ints, cycle_ints, block_dims, moved, moved_ints):
+    return together(value, *others)[0]
+
+
+def compacted(width, least, amplitudes, ladder_ints, cycle_ints, block_dims, moved):
     core = lax.axis_index("slab")
     blk_index = lax.axis_index("blk")
     plane, z = blk_index % 4, blk_index // 4
@@ -502,38 +508,43 @@
     near = [send(own, up(step)) for step in (1, 3)]
     plane_1 = send(own, first_axis)
     plane_2 = send(own, second_axis)
-    moved_ints = to_other_core(after(moved_ints, own), (0,))
     plane_12 = send(plane_1, second_axis)
-    rows_w = compact_rows(ladder_ints, moved_ints, width, least, columns, core)
-    near = after(jnp.concatenate(near), plane_1, plane_2)
-    far = send(after(own, near), up(2))
+    ints, shares = together(ladder_ints, cycle_ints[0], own)[:2]
+    moved_ints = ints.reshape(4, 4, 4 * BS, -1)[:, 3].reshape(GROUP * BS, -1)
+    shares = [lax.dynamic_slice_in_dim(shares, (z + step) % 4 * 128, 128, 2) for step in range(4)]
+    near, far, moved_ints, ints, *shares = together(
+        jnp.concatenate(near), own, moved_ints, ints, *shares, plane_1, plane_2, plane_12
+    )[:8]
+    far = send(far, up(2))
     near_1 = send(near, first_axis)
     near_2 = send(near, second_axis)
-    near_12 = send(near_1, second_axis)
+    moved_ints = to_other_core(moved_ints, (0,))
+    far, near_1, near_2, moved_ints, *shares = together(far, near_1, near_2, moved_ints, *shares)
     far_1 = send(far, first_axis)
     far_2 = send(far, second_axis)
+    near_12 = send(near_1, second_axis)
+    shares[3] = send(shares[3], up(3))
+    shares[2] = send(shares[2], up(2))
+    shares[1] = send(after(shares[1], shares[3]), up(1))
+    rows_w = compact_rows(ints, moved_ints, width, least, columns, core)
+    early = [own, plane_1, plane_2, plane_12, near, near_1, near_2]
+    sums = ladder_part(early, rows_w)
+    turned = cycle_early(width, least, early)
+    far_1, far_2, near_12, sums, turned, *shares = together(
+        far_1, far_2, near_12, sums, turned, *shares
+    )
     far_12 = send(far_1, second_axis)
-    shares = after(cycle_ints[0], far)
-
-    def share(step):
-        part = lax.dynamic_slice_in_dim(shares, (z + step) % 4 * 128, 128, 2)
-        return send(part, up(step)) if step else part
-
-    slots = slots_of_pieces([share(step) for step in range(4)])
-    slots_first = [
-        jnp.where(core == 0, here, to_other_core(there, (0,)))
-        for here, there in zip(slots[:2], slots[2:])
-    ]
-
-    out_columns = ladder_ints.shape[1]
-    pieces = [own, plane_1, plane_2, plane_12, near, near_1, near_2]
-    last = [near_12, far, far_1, far_2, far_12]
-    sums = ladder_early(pieces, rows_w)
-    turned = cycle_early(width, least, pieces)
-    terms = cycle_late(width, least, last, turned, slots_first, slots[:2])
+    slots, there = slots_of_pieces(shares)
+    slots_first = jnp.where(core == 0, slots, to_other_core(there, (0,)))
+    middle = [near_12, far, far_1]
+    sums_middle = ladder_part(middle, rows_w)
+    terms = cycle_add(width, least, 1, middle, turned, slots_first, slots)
+
+    late = [far_2, far_12]
+    terms = cycle_add(width, least, 2, late, terms, slots_first, slots)
     pairs = [(2 * chip + 1, 2 * chip) for chip in (3, 7, 11, 15)]
     last_group = lax.ppermute(terms[0], AXES, pairs)
-    mine, other = ladder_late(last, rows_w, after(sums, terms[0]))
+    mine, other = ladder_late(late, rows_w, after(sums, terms[0]), sums_middle)
     other = to_other_core(other, (0, 1))
     term = jnp.where(core == 0, jnp.where(plane == 3, last_group, terms[0]), terms[1])
     term = term.reshape(4, 32, 8 * BS)
@@ -555,26 +566,13 @@
 
 def local(amplitudes, ladder_ints, cycle_ints, block_dims):
     moved = to_other_core(amplitudes, (0,))
-    moved_ints = ladder_ints.reshape(4, 4, 4 * BS, -1)[:, 3].reshape(GROUP * BS, -1)
-    size = block_dims[0, 1]
-
-    def choose(widths):
-        if len(widths) == 1:
-            return functools.partial(compacted, widths[0], LEAST)
-        half = len(widths) // 2
-        fewer, more = choose(widths[:half]), choose(widths[half:])
-        return lambda *given: lax.cond(size <= widths[half - 1], fewer, more, *given)
-
-    return lax.cond(
-        block_dims[1, 1] <= LEAST,
-        choose(WIDTHS),
-        functools.partial(compacted, BS, BS),
-        amplitudes,
-        ladder_ints,
-        cycle_ints,
-        block_dims,
-        moved,
-        moved_ints,
+    fits = [block_dims[0, 1] > width for width in WIDTHS[:-1]]
+    choice = sum(fit.astype(jnp.int32) for fit in fits)
+    choice = jnp.where(block_dims[1, 1] <= LEAST, choice, len(WIDTHS))
+    branches = [functools.partial(compacted, width, LEAST) for width in WIDTHS]
+    branches.append(functools.partial(compacted, BS, BS))
+    return lax.switch(
+        choice, branches, amplitudes, ladder_ints, cycle_ints, block_dims, moved
     )
 
 

time: 102 us -> 91.8 us (0.900)
  waiting for transfers between devices: 33.9 us -> 26.4 us
  other arithmetic: 4.6 us -> 2.81 us
  starting transfers between devices: 32.9 us -> 31.5 us
  between operations: 1.29 us -> 2.6 us
  Pallas kernels: 17.2 us -> 18.3 us
    ppermute x18, waiting for transfers between devices: 33.9 us -> 26.4 us  [send(): return lax.ppermute(value, AXES, pairs)]
    ppermute x5 -> x4, starting transfers between devices: 9.25 us -> 5.07 us  [to_other_core(): return lax.ppermute(value, 'slab', [(core, 1 - core) for core in cores])]
    ppermute x18, starting transfers between devices: 22.9 us -> 25.7 us  [send(): return lax.ppermute(value, AXES, pairs)]
    cond x34 -> x16, local copies, waits for them, and re-layouts: 2.94 us -> 0.98 us
    slice x2, local copies, waits for them, and re-layouts: 0.41 us -> 2.3 us  [of_first(): return pad(cut(groups[:, :3], width))]
    slice x3 -> x2, local copies, waits for them, and re-layouts: 4.88 us -> 3.6 us  [the longest x1 2.26 us: compacted(): moved_ints = ints.reshape(4, 4, 4 * BS, -1)[:, 3].reshape(GROUP * BS, -1)]
    pallas_call x3 -> x5, Pallas kernels: 8.49 us -> 9.6 us  [the longest x2 4.29 us: ladder_part(): pl.pallas_call(ladder_part_kernel, out_shape=jax.ShapeDtypeStruct(shape,...]
  transfers between devices with their start and end apart: 24 -> 23, of which waited for: 9 -> 8; matrix products, arithmetic and copies ran while one was open for 10% -> 12% of each run, Pallas kernels for 6% -> 9%
where the time goes in v2:
time: 91.8 us; the launch traced here: 91.3 us
  starting transfers between devices  31.5 us (34%)
  waiting for transfers between devices  26.4 us (29%)
  Pallas kernels  18.3 us (20%)
  local copies, waits for them, and re-layouts  9.47 us (10%)
  other arithmetic  2.81 us (3%)
  between operations  2.6 us (3%)
    ppermute x18, waiting for transfers between devices, send(): return lax.ppermute(value, AXES, pairs)  26.4 us
    ppermute x18, starting transfers between devices, send(): return lax.ppermute(value, AXES, pairs)  25.7 us
    ppermute x4, starting transfers between devices, to_other_core(): return lax.ppermute(value, 'slab', [(core, 1 - core) for core in cores])  5.07 us
    pallas_call x2, Pallas kernels, ladder_part(): pl.pallas_call(ladder_part_kernel, out_shape=jax.ShapeDtypeStruct(shape,...  4.29 us
    pallas_call x2, Pallas kernels, cycle_add(): pl.pallas_call(functools.partial(cycle_sum_kernel, width, least, row, tur...  3.89 us
    pallas_call x1, Pallas kernels, ladder_late(): pl.pallas_call(ladder_late_kernel, out_shape=[half, half], in_specs=[VMEM...  3.38 us
    pallas_call x1, Pallas kernels, prep(): pl.pallas_call(functools.partial(prep_kernel, width, least), out_shape=ja...  2.43 us
    slice x2, local copies, waits for them, and re-layouts, of_first(): return pad(cut(groups[:, :3], width))  2.3 us
  transfers between devices with their start and end apart: 23, of which 8 were waited for; matrix products, arithmetic and copies ran while one was open for 12% of the time, Pallas kernels for 9%

profile of v2, /device:TPU:0, one launch (start us, length us, event | category | flops | bytes accessed | tf_op | source)
XLA Modules:
  0.0 91.3 jit_solution(13892496934565531221)
XLA Ops:
  0.6 2.4 %collective-permute-start.88 = (bf16[60,4096]{1,0:T(8,128)(2,1)}, bf16[60,4096]{1,0:T(8,128)(2,1)S(1)}, u32[]{:S(2)}, u32[]{:S(2)}) collective-permute-start(bf16[60,4096]{1,0:T(8,128)(2,1)} %param.24), channel_id=1, source_target_pairs={{0,1},{2,3},{4,5},{6,7},{8,9},{10,11},{12,13},{14,15},{16,17},{18,... | collective-permute-start | bytes 1474568 | tf_op jit(solution)/shard_map/ppermute | solution.py:107
  3.0 1.3 %fusion.58 = (s32[1,1]{1,0:T(1,128)}, s32[1,1]{1,0:T(1,128)}) fusion(s32[2,2]{1,0:T(2,128)} %param.27), kind=kLoop, calls=%fused_computation.142 | loop fusion | bytes 16 | tf_op jit(solution)/shard_map/slice | solution.py:569
  6.3 0.0 collective-permute-done.88
  6.3 85.0 %conditional.5 = (bf16[480,512]{1,0:T(8,128)(2,1)}, bf16[1,32,512]{2,1,0:T(8,128)(2,1)}) conditional(s32[]{:T(128)} %bitcast.82, (s32[2,2]{1,0:T(2,128)}, bf16[60,4096]{1,0:T(8,128)(2,1)}, bf16[60,4096]{1,0:T(8,128)(2,1)S(1)}, (), s32[8,384]{1,0:T(8,128)}, /*index=5*/bf16[1,4,120,512]{3,2,1,0:T(8,128)(2,1)}, ...), branch_computations={%region_0.5_spmd, %region_5.10_spmd, %region_10.15_spmd, %region_1... | conditional | flops 11898898 | bytes 147066768 | solution.py:574
  6.3 0.0 copy-start.37
  6.4 2.4 %prep.4 = bf16[64,2304]{1,0:T(8,128)(2,1)} custom-call(s32[2,2]{1,0:T(2,128)} %get-tuple-element.90.dims, bf16[60,4096]{1,0:T(8,128)(2,1)} %get-tuple-element.91.amp, bf16[60,4096]{1,0:T(8,128)(2,1)S(1)} %get-tuple-element.92.moved, s32[8,768]{1,0:T(8,128)} %constant.381.clone.1.wide, s32[8,384]{1,0:T(8,128)} %get-tuple-element.94.narrow), custom_call_target="tpu_custom_call" | custom-call | tf_op jit(solution)/shard_map/cond/branch_0_fun/prep/pallas_call | solution.py:166
  8.8 2.3 %collective-permute-start.2 = (bf16[1,64,2304]{2,1,0:T(8,128)(2,1)}, bf16[1,64,2304]{2,1,0:T(8,128)(2,1)S(1)}, u32[]{:S(2)}, u32[]{:S(2)}) collective-permute-start(bf16[1,64,2304]{2,1,0:T(8,128)(2,1)} %bitcast.188), channel_id=1, source_target_pairs={{0,2},{1,5},{2,0},{3,7},{4,6},{5,1},{6,4},{7,3},{8,10},{9,13},{10,... | collective-permute-start | bytes 884744 | tf_op jit(solution)/shard_map/cond/branch_0_fun/ppermute | solution.py:79
  11.1 1.6 %collective-permute-start = (bf16[1,64,2304]{2,1,0:T(8,128)(2,1)}, bf16[1,64,2304]{2,1,0:T(8,128)(2,1)S(1)}, u32[]{:S(2)}, u32[]{:S(2)}) collective-permute-start(bf16[1,64,2304]{2,1,0:T(8,128)(2,1)} %bitcast.189), channel_id=1, source_target_pairs={{0,8},{1,9},{2,10},{3,11},{4,12},{5,13},{6,14},{7,15},{8,16},{9,17... | collective-permute-start | bytes 884744 | tf_op jit(solution)/shard_map/cond/branch_0_fun/ppermute | solution.py:79
  12.7 2.2 %collective-permute-start.1 = (bf16[1,64,2304]{2,1,0:T(8,128)(2,1)}, bf16[1,64,2304]{2,1,0:T(8,128)(2,1)S(1)}, u32[]{:S(2)}, u32[]{:S(2)}) collective-permute-start(bf16[1,64,2304]{2,1,0:T(8,128)(2,1)} %bitcast.190), channel_id=1, source_target_pairs={{0,24},{1,25},{2,26},{3,27},{4,28},{5,29},{6,30},{7,31},{8,0},{9,1... | collective-permute-start | bytes 884744 | tf_op jit(solution)/shard_map/cond/branch_0_fun/ppermute | solution.py:79
  14.9 1.5 %collective-permute-start.3 = (bf16[1,64,2304]{2,1,0:T(8,128)(2,1)}, bf16[1,64,2304]{2,1,0:T(8,128)(2,1)S(1)}, u32[]{:S(2)}, u32[]{:S(2)}) collective-permute-start(bf16[1,64,2304]{2,1,0:T(8,128)(2,1)} %bitcast.191), channel_id=1, source_target_pairs={{0,4},{1,3},{2,6},{3,1},{4,0},{5,7},{6,2},{7,5},{8,12},{9,11},{10,... | collective-permute-start | bytes 884744 | tf_op jit(solution)/shard_map/cond/branch_0_fun/ppermute | solution.py:79
  16.5 2.3 %slice.89 = bf16[4,1,256,512]{3,2,1,0:T(8,128)(2,1)} slice(bf16[4,4,256,512]{3,2,1,0:T(8,128)(2,1)} %bitcast.195), slice={[0:4], [3:4], [0:256], [0:512]} | slice | bytes 2097152 | tf_op jit(solution)/shard_map/cond/branch_0_fun/slice | solution.py:513
  18.7 0.8 constant_dynamic-slice_fusion
  19.5 0.5 collective-permute-start.4
  20.0 3.1 %collective-permute-done = bf16[1,64,2304]{2,1,0:T(8,128)(2,1)S(1)} collective-permute-done((bf16[1,64,2304]{2,1,0:T(8,128)(2,1)}, bf16[1,64,2304]{2,1,0:T(8,128)(2,1)S(1)}, u32[]{:S(2)}, u32[]{:S(2)}) %collective-permute-start) | collective-permute-done | bytes 294944 | tf_op jit(solution)/shard_map/cond/branch_0_fun/ppermute | solution.py:79
  23.1 3.9 %collective-permute-done.1 = bf16[1,64,2304]{2,1,0:T(8,128)(2,1)S(1)} collective-permute-done((bf16[1,64,2304]{2,1,0:T(8,128)(2,1)}, bf16[1,64,2304]{2,1,0:T(8,128)(2,1)S(1)}, u32[]{:S(2)}, u32[]{:S(2)}) %collective-permute-start.1) | collective-permute-done | bytes 294944 | tf_op jit(solution)/shard_map/cond/branch_0_fun/ppermute | solution.py:79
  27.0 0.1 pad_maximum_fusion.2.refs_4_
  27.1 0.0 collective-permute-done.4.refs_3_
  27.1 1.4 %collective-permute-start.8 = (bf16[1024,512]{1,0:T(8,128)(2,1)}, bf16[1024,512]{1,0:T(8,128)(2,1)S(1)}, u32[]{:S(2)}, u32[]{:S(2)}) collective-permute-start(bf16[1024,512]{1,0:T(8,128)(2,1)} %bitcast.14), channel_id=1, source_target_pairs={{0,1},{2,3},{4,5},{6,7},{8,9},{10,11},{12,13},{14,15},{16,17},{18,... | collective-permute-start | bytes 3145736 | tf_op jit(solution)/shard_map/cond/branch_0_fun/ppermute | solution.py:107
  28.5 1.6 %collective-permute-start.6 = (bf16[2,64,2304]{2,1,0:T(8,128)(2,1)S(1)}, bf16[2,64,2304]{2,1,0:T(8,128)(2,1)S(1)}, u32[]{:S(2)}, u32[]{:S(2)}) collective-permute-start(bf16[2,64,2304]{2,1,0:T(8,128)(2,1)S(1)} %pad_maximum_fusion.2.refs_4_), channel_id=1, source_target_pairs={{0,2},{1,5},{2,0},{3,7},{4,6},{5,1},{6,4},{7,3},{8,10},{9,13},{10,... | collective-permute-start | bytes 1769480 | tf_op jit(solution)/shard_map/cond/branch_0_fun/ppermute | solution.py:79
  30.1 0.5 collective-permute-start.7
  30.5 2.7 %collective-permute-start.5 = (bf16[1,64,2304]{2,1,0:T(8,128)(2,1)S(1)}, bf16[1,64,2304]{2,1,0:T(8,128)(2,1)}, u32[]{:S(2)}, u32[]{:S(2)}) collective-permute-start(bf16[1,64,2304]{2,1,0:T(8,128)(2,1)S(1)} %bitcast.192), channel_id=1, source_target_pairs={{0,16},{1,17},{2,18},{3,19},{4,20},{5,21},{6,22},{7,23},{8,24},{9,... | collective-permute-start | bytes 884744 | tf_op jit(solution)/shard_map/cond/branch_0_fun/ppermute | solution.py:79
  33.3 12.2 %collective-permute-done.5.refs_1_ = bf16[1,64,2304]{2,1,0:T(8,128)(2,1)} collective-permute-done((bf16[1,64,2304]{2,1,0:T(8,128)(2,1)S(1)}, bf16[1,64,2304]{2,1,0:T(8,128)(2,1)}, u32[]{:S(2)}, u32[]{:S(2)}) %collective-permute-start.5) | collective-permute-done | bytes 294944 | tf_op jit(solution)/shard_map/cond/branch_0_fun/ppermute | solution.py:79
  45.5 0.0 collective-permute-done.6.refs_5_
  45.5 1.7 %collective-permute-start.11 = (bf16[2,64,2304]{2,1,0:T(8,128)(2,1)S(1)}, bf16[2,64,2304]{2,1,0:T(8,128)(2,1)S(1)}, u32[]{:S(2)}, u32[]{:S(2)}) collective-permute-start(bf16[2,64,2304]{2,1,0:T(8,128)(2,1)S(1)} %collective-permute-done.6.refs_5_), channel_id=1, source_target_pairs={{0,4},{1,3},{2,6},{3,1},{4,0},{5,7},{6,2},{7,5},{8,12},{9,11},{10,... | collective-permute-start | bytes 1769480 | tf_op jit(solution)/shard_map/cond/branch_0_fun/ppermute | solution.py:79
  47.2 0.4 collective-permute-start.10
  47.6 0.5 collective-permute-start.9
  48.1 1.8 %collective-permute-start.12 = (bf16[4,120,128]{2,1,0:T(8,128)(2,1)S(1)}, bf16[4,120,128]{2,1,0:T(8,128)(2,1)S(1)}, u32[]{:S(2)}, u32[]{:S(2)}) collective-permute-start(bf16[4,120,128]{2,1,0:T(8,128)(2,1)S(1)} %get-tuple-element.115), channel_id=1, source_target_pairs={{0,24},{1,25},{2,26},{3,27},{4,28},{5,29},{6,30},{7,31},{8,0},{9,1... | collective-permute-start | bytes 368648 | tf_op jit(solution)/shard_map/cond/branch_0_fun/ppermute | solution.py:79
  49.9 0.2 collective-permute-start.14
  50.2 3.5 %collective-permute-done.12.part_3 = bf16[4,120,128]{2,1,0:T(8,128)(2,1)S(1)} collective-permute-done((bf16[4,120,128]{2,1,0:T(8,128)(2,1)S(1)}, bf16[4,120,128]{2,1,0:T(8,128)(2,1)S(1)}, u32[]{:S(2)}, u32[]{:S(2)}) %collective-permute-start.12) | collective-permute-done | bytes 122912 | tf_op jit(solution)/shard_map/cond/branch_0_fun/ppermute | solution.py:79
  53.7 0.6 copy-done.27
  54.3 3.9 %conditional = (bf16[2304,512]{1,0:T(8,128)(2,1)}) conditional(s32[]{:T(128)} %convert_element_type.28, (bf16[1024,512]{1,0:T(8,128)(2,1)}, bf16[4096,512]{1,0:T(8,128)(2,1)}) %tuple.129, bf16[4096,512]{1,0:T(8,128)(2,1)} %get-tuple-element.110), branch_computations={%region_1.1_spmd, %region_2.2_spmd} | conditional | flops 4718592 | bytes 17301512 | solution.py:199
  54.3 2.1 %slice.80 = bf16[4,3,256,512]{3,2,1,0:T(8,128)(2,1)S(1)} slice(bf16[4,4,256,512]{3,2,1,0:T(8,128)(2,1)} %bitcast.197), slice={[0:4], [0:3], [0:256], [0:512]} | slice | bytes 6291456 | tf_op jit(solution)/shard_map/cond/branch_0_fun/cond/branch_1_fun/slice | solution.py:194
  56.4 0.2 copy.37
  56.6 1.6 %slice.81 = bf16[4,3,4,48,512]{4,3,2,0,1:T(8,128)(2,1)} slice(bf16[4,3,4,64,512]{4,3,2,0,1:T(8,128)(2,1)S(1)} %bitcast.213), slice={[0:4], [0:3], [0:4], [0:48], [0:512]} | slice | bytes 4718592 | tf_op jit(solution)/shard_map/cond/branch_0_fun/cond/branch_1_fun/slice | solution.py:189
  58.3 1.4 %cycle_early.4 = (bf16[1280,512]{1,0:T(8,128)(2,1)S(1)}, bf16[1280,512]{1,0:T(8,128)(2,1)S(1)}) custom-call(bf16[1,64,2304]{2,1,0:T(8,128)(2,1)S(1)} %bitcast.193, bf16[1,64,2304]{2,1,0:T(8,128)(2,1)S(1)} %collective-permute-done.2.refs_1_, bf16[1,64,2304]{2,1,0:T(8,128)(2,1)S(1)} %collective-permute-done.3.refs_2_, ...), custom_call_target="tpu_custom_call" | custom-call | tf_op jit(solution)/shard_map/cond/branch_0_fun/cycle_early/pallas_call | solution.py:428
  59.6 0.3 copy-done.36
  59.9 2.1 %ladder_part.8.refs_3_ = f32[640,512]{1,0:T(8,128)S(1)} custom-call(bf16[1,64,2304]{2,1,0:T(8,128)(2,1)S(1)} %bitcast.194, bf16[1,64,2304]{2,1,0:T(8,128)(2,1)S(1)} %collective-permute-done.2.refs_1_, bf16[1,64,2304]{2,1,0:T(8,128)(2,1)S(1)} %collective-permute-done.3.refs_2_, bf16[1,64,2304]{2,1,0:T(8,128)(2,1)S(1)} %collective-permute-done.4.refs_3_, ...), custom_call_target="tpu_custom_call" | custom-call | tf_op jit(solution)/shard_map/cond/branch_0_fun/ladder_part/pallas_call | solution.py:278
  62.1 0.0 collective-permute-done.10.refs_0_
  62.1 1.4 %slots.4 = (bf16[2048,128]{1,0:T(8,128)(2,1)S(1)}, bf16[2048,128]{1,0:T(8,128)(2,1)S(1)}) custom-call(bf16[4,120,128]{2,1,0:T(8,128)(2,1)S(1)} %copy-done.24, bf16[4,120,128]{2,1,0:T(8,128)(2,1)} %collective-permute-done.13.part_1, bf16[4,120,128]{2,1,0:T(8,128)(2,1)} %collective-permute-done.14.part_2, bf16[4,120,128]{2,1,0:T(8,128)(2,1)S(1)} %copy-done.28), custom_call_target="tpu_custom_call" | custom-call | tf_op jit(solution)/shard_map/cond/branch_0_fun/slots/pallas_call | solution.py:245
  63.5 1.3 %collective-permute-start.16 = (bf16[2048,128]{1,0:T(8,128)(2,1)S(1)}, bf16[2048,128]{1,0:T(8,128)(2,1)S(1)}, u32[]{:S(2)}, u32[]{:S(2)}) collective-permute-start(bf16[2048,128]{1,0:T(8,128)(2,1)S(1)} %get-tuple-element.129), channel_id=1, source_target_pairs={{0,1},{2,3},{4,5},{6,7},{8,9},{10,11},{12,13},{14,15},{16,17},{18,... | collective-permute-start | bytes 1572872 | tf_op jit(solution)/shard_map/cond/branch_0_fun/ppermute | solution.py:107
  64.9 4.5 %collective-permute-start.15 = (bf16[1,64,2304]{2,1,0:T(8,128)(2,1)}, bf16[1,64,2304]{2,1,0:T(8,128)(2,1)S(1)}, u32[]{:S(2)}, u32[]{:S(2)}) collective-permute-start(bf16[1,64,2304]{2,1,0:T(8,128)(2,1)} %collective-permute-done.9.refs_2_), channel_id=1, source_target_pairs={{0,4},{1,3},{2,6},{3,1},{4,0},{5,7},{6,2},{7,5},{8,12},{9,11},{10,... | collective-permute-start | bytes 884744 | tf_op jit(solution)/shard_map/cond/branch_0_fun/ppermute | solution.py:79
  69.4 2.2 %ladder_part.9.refs_4_ = f32[256,512]{1,0:T(8,128)S(1)} custom-call(bf16[2,64,2304]{2,1,0:T(8,128)(2,1)S(1)} %collective-permute-done.11.refs_0_, bf16[1,64,2304]{2,1,0:T(8,128)(2,1)} %collective-permute-done.5.refs_1_, bf16[1,64,2304]{2,1,0:T(8,128)(2,1)} %collective-permute-done.9.refs_2_, bf16[2304,512]{1,0:T(8,128)(2,1)S(1)} %copy-done.36), custom_call_target="tpu_custom_call" | custom-call | tf_op jit(solution)/shard_map/cond/branch_0_fun/ladder_part/pallas_call | solution.py:278
  71.6 0.1 broadcast_select_fusion.refs_5_.refs_4_
  71.7 2.2 %cycle_sum.8 = (f32[128,512]{1,0:T(8,128)S(1)}, f32[128,512]{1,0:T(8,128)S(1)}) custom-call(bf16[2,64,2304]{2,1,0:T(8,128)(2,1)S(1)} %collective-permute-done.11.refs_0_, bf16[1,64,2304]{2,1,0:T(8,128)(2,1)} %collective-permute-done.5.refs_1_, bf16[1,64,2304]{2,1,0:T(8,128)(2,1)} %collective-permute-done.9.refs_2_, ...), custom_call_target="tpu_custom_call" | custom-call | tf_op jit(solution)/shard_map/cond/branch_0_fun/cycle_sum/pallas_call | solution.py:478
  73.9 0.4 collective-permute-done.15.refs_1_
  74.3 1.7 %cycle_sum.9 = (f32[128,512]{1,0:T(8,128)S(1)}, f32[128,512]{1,0:T(8,128)S(1)}) custom-call(bf16[1,64,2304]{2,1,0:T(8,128)(2,1)} %collective-permute-done.10.refs_0_, bf16[1,64,2304]{2,1,0:T(8,128)(2,1)S(1)} %collective-permute-done.15.refs_1_, f32[128,512]{1,0:T(8,128)S(1)} %get-tuple-element.130.refs_2_, f32[128,512]{1,0:T(8,128)S(1)} %get-tuple-element.131.refs_3_, ...), custom_call_target="tpu_custom_call" | custom-call | tf_op jit(solution)/shard_map/cond/branch_0_fun/cycle_sum/pallas_call | solution.py:478
  76.0 0.0 copy-start.48
  76.0 3.4 %ladder_late.4 = (f32[8,64,512]{2,1,0:T(8,128)S(1)}, f32[8,64,512]{2,1,0:T(8,128)}) custom-call(bf16[1,64,2304]{2,1,0:T(8,128)(2,1)} %collective-permute-done.10.refs_0_, bf16[1,64,2304]{2,1,0:T(8,128)(2,1)S(1)} %collective-permute-done.15.refs_1_, bf16[2304,512]{1,0:T(8,128)(2,1)S(1)} %copy-done.36, f32[640,512]{1,0:T(8,128)S(1)} %ladder_part.8.refs_3_, ...), custom_call_target="tpu_custom_call" | custom-call | tf_op jit(solution)/shard_map/cond/branch_0_fun/ladder_late/pallas_call | solution.py:319
  79.4 0.7 collective-permute-start.18
  80.1 0.2 slice_reduce_fusion.1
  80.3 0.6 fusion.15
  80.9 0.7 fusion.11
  81.6 0.0 collective-permute-done.18
  81.6 0.1 select_select_fusion
  81.7 1.8 %collective-permute-start.19 = (f32[32,512]{1,0:T(8,128)S(1)}, f32[32,512]{1,0:T(8,128)S(1)}, u32[]{:S(2)}, u32[]{:S(2)}) collective-permute-start(f32[32,512]{1,0:T(8,128)S(1)} %get-tuple-element.304), channel_id=1, source_target_pairs={{0,2},{1,3},{2,0},{3,1},{4,6},{5,7},{6,4},{7,5},{8,10},{9,11},{10,... | collective-permute-start | bytes 196616 | tf_op jit(solution)/shard_map/cond/branch_0_fun/ppermute | solution.py:79
  83.4 0.5 collective-permute-start.20
  84.0 1.3 %collective-permute-start.21 = (f32[32,512]{1,0:T(8,128)S(1)}, f32[32,512]{1,0:T(8,128)S(1)}, u32[]{:S(2)}, u32[]{:S(2)}) collective-permute-start(f32[32,512]{1,0:T(8,128)S(1)} %get-tuple-element.305), channel_id=1, source_target_pairs={{0,6},{1,7},{2,4},{3,5},{4,2},{5,3},{6,0},{7,1},{8,14},{9,15},{10,... | collective-permute-start | bytes 196616 | tf_op jit(solution)/shard_map/cond/branch_0_fun/ppermute | solution.py:79
  85.2 0.7 fusion.17
  85.9 0.4 collective-permute-done.19
  86.3 1.5 %collective-permute-done.20 = f32[32,512]{1,0:T(8,128)S(1)} collective-permute-done((f32[32,512]{1,0:T(8,128)S(1)}, f32[32,512]{1,0:T(8,128)S(1)}, u32[]{:S(2)}, u32[]{:S(2)}) %collective-permute-start.20) | collective-permute-done | bytes 65568 | tf_op jit(solution)/shard_map/cond/branch_0_fun/ppermute | solution.py:79
  87.7 1.4 %collective-permute-done.21 = f32[32,512]{1,0:T(8,128)S(1)} collective-permute-done((f32[32,512]{1,0:T(8,128)S(1)}, f32[32,512]{1,0:T(8,128)S(1)}, u32[]{:S(2)}, u32[]{:S(2)}) %collective-permute-start.21) | collective-permute-done | bytes 65568 | tf_op jit(solution)/shard_map/cond/branch_0_fun/ppermute | solution.py:79
  89.1 0.7 fusion.10
  89.8 0.0 collective-permute-done.17.other
  89.8 1.5 %ladder_end.4 = bf16[480,512]{1,0:T(8,128)(2,1)} custom-call(s32[2,2]{1,0:T(2,128)S(1)} %copy-done.48, f32[8,64,512]{2,1,0:T(8,128)S(1)} %get-tuple-element.134.mine, f32[8,64,512]{2,1,0:T(8,128)S(1)} %collective-permute-done.17.other), custom_call_target="tpu_custom_call" | custom-call | tf_op jit(solution)/shard_map/cond/branch_0_fun/ladder_end/pallas_call | solution.py:352
  (24 shorter events, 0.1 us)
Async XLA Ops:
  0.6 5.7 %collective-permute-start.88 = (bf16[60,4096]{1,0:T(8,128)(2,1)}, bf16[60,4096]{1,0:T(8,128)(2,1)S(1)}, u32[]{:S(2)}, u32[]{:S(2)}) collective-permute-start(bf16[60,4096]{1,0:T(8,128)(2,1)} %param.24), channel_id=1, source_target_pairs={{0,1},{2,3},{4,5},{6,7},{8,9},{10,11},{12,13},{14,15},{16,17},{18,... | collective-permute-start | bytes 1474568 | tf_op jit(solution)/shard_map/ppermute | solution.py:107
  6.3 12.4 %copy-start.37 = (bf16[1,4,120,512]{3,2,1,0:T(8,128)(2,1)S(1)}, bf16[1,4,120,512]{3,2,1,0:T(8,128)(2,1)}, u32[]{:S(2)}) copy-start(bf16[1,4,120,512]{3,2,1,0:T(8,128)(2,1)} %get-tuple-element.96) | copy-start | bytes 1474564 | tf_op jit(solution)/shard_map/cond
  8.8 21.8 %copy-start.5 = (bf16[64,2304]{1,0:T(8,128)(2,1)S(1)}, bf16[64,2304]{1,0:T(8,128)(2,1)}, u32[]{:S(2)}) copy-start(bf16[64,2304]{1,0:T(8,128)(2,1)} %prep.4) | copy-start | bytes 884740 | tf_op jit(solution)/shard_map/cond
  8.8 10.7 %collective-permute-start.2 = (bf16[1,64,2304]{2,1,0:T(8,128)(2,1)}, bf16[1,64,2304]{2,1,0:T(8,128)(2,1)S(1)}, u32[]{:S(2)}, u32[]{:S(2)}) collective-permute-start(bf16[1,64,2304]{2,1,0:T(8,128)(2,1)} %bitcast.188), channel_id=1, source_target_pairs={{0,2},{1,5},{2,0},{3,7},{4,6},{5,1},{6,4},{7,3},{8,10},{9,13},{10,... | collective-permute-start | bytes 884744 | tf_op jit(solution)/shard_map/cond/branch_0_fun/ppermute | solution.py:79
  11.1 12.0 %collective-permute-start = (bf16[1,64,2304]{2,1,0:T(8,128)(2,1)}, bf16[1,64,2304]{2,1,0:T(8,128)(2,1)S(1)}, u32[]{:S(2)}, u32[]{:S(2)}) collective-permute-start(bf16[1,64,2304]{2,1,0:T(8,128)(2,1)} %bitcast.189), channel_id=1, source_target_pairs={{0,8},{1,9},{2,10},{3,11},{4,12},{5,13},{6,14},{7,15},{8,16},{9,17... | collective-permute-start | bytes 884744 | tf_op jit(solution)/shard_map/cond/branch_0_fun/ppermute | solution.py:79
  12.7 14.3 %collective-permute-start.1 = (bf16[1,64,2304]{2,1,0:T(8,128)(2,1)}, bf16[1,64,2304]{2,1,0:T(8,128)(2,1)S(1)}, u32[]{:S(2)}, u32[]{:S(2)}) collective-permute-start(bf16[1,64,2304]{2,1,0:T(8,128)(2,1)} %bitcast.190), channel_id=1, source_target_pairs={{0,24},{1,25},{2,26},{3,27},{4,28},{5,29},{6,30},{7,31},{8,0},{9,1... | collective-permute-start | bytes 884744 | tf_op jit(solution)/shard_map/cond/branch_0_fun/ppermute | solution.py:79
  14.9 12.2 %collective-permute-start.3 = (bf16[1,64,2304]{2,1,0:T(8,128)(2,1)}, bf16[1,64,2304]{2,1,0:T(8,128)(2,1)S(1)}, u32[]{:S(2)}, u32[]{:S(2)}) collective-permute-start(bf16[1,64,2304]{2,1,0:T(8,128)(2,1)} %bitcast.191), channel_id=1, source_target_pairs={{0,4},{1,3},{2,6},{3,1},{4,0},{5,7},{6,2},{7,5},{8,12},{9,11},{10,... | collective-permute-start | bytes 884744 | tf_op jit(solution)/shard_map/cond/branch_0_fun/ppermute | solution.py:79
  19.5 7.6 %collective-permute-start.4 = (bf16[1,64,2304]{2,1,0:T(8,128)(2,1)S(1)}, bf16[1,64,2304]{2,1,0:T(8,128)(2,1)S(1)}, u32[]{:S(2)}, u32[]{:S(2)}) collective-permute-start(bf16[1,64,2304]{2,1,0:T(8,128)(2,1)S(1)} %collective-permute-done.2.refs_1_), channel_id=1, source_target_pairs={{0,4},{1,3},{2,6},{3,1},{4,0},{5,7},{6,2},{7,5},{8,12},{9,11},{10,... | collective-permute-start | bytes 884744 | tf_op jit(solution)/shard_map/cond/branch_0_fun/ppermute | solution.py:79
  27.1 18.4 %collective-permute-start.8 = (bf16[1024,512]{1,0:T(8,128)(2,1)}, bf16[1024,512]{1,0:T(8,128)(2,1)S(1)}, u32[]{:S(2)}, u32[]{:S(2)}) collective-permute-start(bf16[1024,512]{1,0:T(8,128)(2,1)} %bitcast.14), channel_id=1, source_target_pairs={{0,1},{2,3},{4,5},{6,7},{8,9},{10,11},{12,13},{14,15},{16,17},{18,... | collective-permute-start | bytes 3145736 | tf_op jit(solution)/shard_map/cond/branch_0_fun/ppermute | solution.py:107
  28.5 17.0 %collective-permute-start.6 = (bf16[2,64,2304]{2,1,0:T(8,128)(2,1)S(1)}, bf16[2,64,2304]{2,1,0:T(8,128)(2,1)S(1)}, u32[]{:S(2)}, u32[]{:S(2)}) collective-permute-start(bf16[2,64,2304]{2,1,0:T(8,128)(2,1)S(1)} %pad_maximum_fusion.2.refs_4_), channel_id=1, source_target_pairs={{0,2},{1,5},{2,0},{3,7},{4,6},{5,1},{6,4},{7,3},{8,10},{9,13},{10,... | collective-permute-start | bytes 1769480 | tf_op jit(solution)/shard_map/cond/branch_0_fun/ppermute | solution.py:79
  30.1 15.4 %collective-permute-start.7 = (bf16[2,64,2304]{2,1,0:T(8,128)(2,1)S(1)}, bf16[2,64,2304]{2,1,0:T(8,128)(2,1)S(1)}, u32[]{:S(2)}, u32[]{:S(2)}) collective-permute-start(bf16[2,64,2304]{2,1,0:T(8,128)(2,1)S(1)} %pad_maximum_fusion.2.refs_4_), channel_id=1, source_target_pairs={{0,4},{1,3},{2,6},{3,1},{4,0},{5,7},{6,2},{7,5},{8,12},{9,11},{10,... | collective-permute-start | bytes 1769480 | tf_op jit(solution)/shard_map/cond/branch_0_fun/ppermute | solution.py:79
  30.5 14.9 %collective-permute-start.5 = (bf16[1,64,2304]{2,1,0:T(8,128)(2,1)S(1)}, bf16[1,64,2304]{2,1,0:T(8,128)(2,1)}, u32[]{:S(2)}, u32[]{:S(2)}) collective-permute-start(bf16[1,64,2304]{2,1,0:T(8,128)(2,1)S(1)} %bitcast.192), channel_id=1, source_target_pairs={{0,16},{1,17},{2,18},{3,19},{4,20},{5,21},{6,22},{7,23},{8,24},{9,... | collective-permute-start | bytes 884744 | tf_op jit(solution)/shard_map/cond/branch_0_fun/ppermute | solution.py:79
  45.5 2.1 %copy-start.46 = (bf16[1024,512]{1,0:T(8,128)(2,1)}, bf16[1024,512]{1,0:T(8,128)(2,1)S(1)}, u32[]{:S(2)}) copy-start(bf16[1024,512]{1,0:T(8,128)(2,1)S(1)} %collective-permute-done.8) | copy-start | bytes 3145732 | tf_op jit(solution)/shard_map/cond
  45.5 16.6 %collective-permute-start.11 = (bf16[2,64,2304]{2,1,0:T(8,128)(2,1)S(1)}, bf16[2,64,2304]{2,1,0:T(8,128)(2,1)S(1)}, u32[]{:S(2)}, u32[]{:S(2)}) collective-permute-start(bf16[2,64,2304]{2,1,0:T(8,128)(2,1)S(1)} %collective-permute-done.6.refs_5_), channel_id=1, source_target_pairs={{0,4},{1,3},{2,6},{3,1},{4,0},{5,7},{6,2},{7,5},{8,12},{9,11},{10,... | collective-permute-start | bytes 1769480 | tf_op jit(solution)/shard_map/cond/branch_0_fun/ppermute | solution.py:79
  47.2 14.9 %collective-permute-start.10 = (bf16[1,64,2304]{2,1,0:T(8,128)(2,1)}, bf16[1,64,2304]{2,1,0:T(8,128)(2,1)}, u32[]{:S(2)}, u32[]{:S(2)}) collective-permute-start(bf16[1,64,2304]{2,1,0:T(8,128)(2,1)} %collective-permute-done.5.refs_1_), channel_id=1, source_target_pairs={{0,4},{1,3},{2,6},{3,1},{4,0},{5,7},{6,2},{7,5},{8,12},{9,11},{10,... | collective-permute-start | bytes 884744 | tf_op jit(solution)/shard_map/cond/branch_0_fun/ppermute | solution.py:79
  47.6 14.5 %collective-permute-start.9 = (bf16[1,64,2304]{2,1,0:T(8,128)(2,1)}, bf16[1,64,2304]{2,1,0:T(8,128)(2,1)}, u32[]{:S(2)}, u32[]{:S(2)}) collective-permute-start(bf16[1,64,2304]{2,1,0:T(8,128)(2,1)} %collective-permute-done.5.refs_1_), channel_id=1, source_target_pairs={{0,2},{1,5},{2,0},{3,7},{4,6},{5,1},{6,4},{7,3},{8,10},{9,13},{10,... | collective-permute-start | bytes 884744 | tf_op jit(solution)/shard_map/cond/branch_0_fun/ppermute | solution.py:79
  48.1 5.6 %collective-permute-start.12 = (bf16[4,120,128]{2,1,0:T(8,128)(2,1)S(1)}, bf16[4,120,128]{2,1,0:T(8,128)(2,1)S(1)}, u32[]{:S(2)}, u32[]{:S(2)}) collective-permute-start(bf16[4,120,128]{2,1,0:T(8,128)(2,1)S(1)} %get-tuple-element.115), channel_id=1, source_target_pairs={{0,24},{1,25},{2,26},{3,27},{4,28},{5,29},{6,30},{7,31},{8,0},{9,1... | collective-permute-start | bytes 368648 | tf_op jit(solution)/shard_map/cond/branch_0_fun/ppermute | solution.py:79
  49.9 12.1 %collective-permute-start.14 = (bf16[4,120,128]{2,1,0:T(8,128)(2,1)}, bf16[4,120,128]{2,1,0:T(8,128)(2,1)}, u32[]{:S(2)}, u32[]{:S(2)}) collective-permute-start(bf16[4,120,128]{2,1,0:T(8,128)(2,1)} %get-tuple-element.117), channel_id=1, source_target_pairs={{0,16},{1,17},{2,18},{3,19},{4,20},{5,21},{6,22},{7,23},{8,24},{9,... | collective-permute-start | bytes 368648 | tf_op jit(solution)/shard_map/cond/branch_0_fun/ppermute | solution.py:79
  53.7 0.6 copy-start.27
  54.3 7.7 %collective-permute-start.13 = (bf16[4,120,128]{2,1,0:T(8,128)(2,1)}, bf16[4,120,128]{2,1,0:T(8,128)(2,1)}, u32[]{:S(2)}, u32[]{:S(2)}) collective-permute-start(bf16[4,120,128]{2,1,0:T(8,128)(2,1)} %get-tuple-element.116), channel_id=1, source_target_pairs={{0,8},{1,9},{2,10},{3,11},{4,12},{5,13},{6,14},{7,15},{8,16},{9,17... | collective-permute-start | bytes 368648 | tf_op jit(solution)/shard_map/cond/branch_0_fun/ppermute | solution.py:79
  58.3 1.7 %copy-start.36 = (bf16[2304,512]{1,0:T(8,128)(2,1)S(1)}, bf16[2304,512]{1,0:T(8,128)(2,1)}, u32[]{:S(2)}) copy-start(bf16[2304,512]{1,0:T(8,128)(2,1)} %get-tuple-element.346.refs_7_.refs_3_.refs_2_) | copy-start | bytes 7077892 | tf_op jit(solution)/shard_map/cond
  59.9 2.2 %copy-start.24 = (bf16[4,120,128]{2,1,0:T(8,128)(2,1)S(1)}, bf16[4,120,128]{2,1,0:T(8,128)(2,1)}, u32[]{:S(2)}) copy-start(bf16[4,120,128]{2,1,0:T(8,128)(2,1)} %get-tuple-element.124.part_0) | copy-start | bytes 368644 | tf_op jit(solution)/shard_map/cond
  59.9 2.2 %copy-start.28 = (bf16[4,120,128]{2,1,0:T(8,128)(2,1)S(1)}, bf16[4,120,128]{2,1,0:T(8,128)(2,1)}, u32[]{:S(2)}) copy-start(bf16[4,120,128]{2,1,0:T(8,128)(2,1)} %copy-done.27) | copy-start | bytes 368644 | tf_op jit(solution)/shard_map/cond
  63.5 8.0 %collective-permute-start.16 = (bf16[2048,128]{1,0:T(8,128)(2,1)S(1)}, bf16[2048,128]{1,0:T(8,128)(2,1)S(1)}, u32[]{:S(2)}, u32[]{:S(2)}) collective-permute-start(bf16[2048,128]{1,0:T(8,128)(2,1)S(1)} %get-tuple-element.129), channel_id=1, source_target_pairs={{0,1},{2,3},{4,5},{6,7},{8,9},{10,11},{12,13},{14,15},{16,17},{18,... | collective-permute-start | bytes 1572872 | tf_op jit(solution)/shard_map/cond/branch_0_fun/ppermute | solution.py:107
  64.9 9.4 %collective-permute-start.15 = (bf16[1,64,2304]{2,1,0:T(8,128)(2,1)}, bf16[1,64,2304]{2,1,0:T(8,128)(2,1)S(1)}, u32[]{:S(2)}, u32[]{:S(2)}) collective-permute-start(bf16[1,64,2304]{2,1,0:T(8,128)(2,1)} %collective-permute-done.9.refs_2_), channel_id=1, source_target_pairs={{0,4},{1,3},{2,6},{3,1},{4,0},{5,7},{6,2},{7,5},{8,12},{9,11},{10,... | collective-permute-start | bytes 884744 | tf_op jit(solution)/shard_map/cond/branch_0_fun/ppermute | solution.py:79
  76.0 4.1 %copy-start.48 = (s32[2,2]{1,0:T(2,128)S(1)}, s32[2,2]{1,0:T(2,128)}, u32[]{:S(2)}) copy-start(s32[2,2]{1,0:T(2,128)} %get-tuple-element.90.dims) | copy-start | bytes 52 | tf_op jit(solution)/shard_map/cond
  79.4 10.4 %collective-permute-start.17 = (f32[8,64,512]{2,1,0:T(8,128)}, f32[8,64,512]{2,1,0:T(8,128)S(1)}, u32[]{:S(2)}, u32[]{:S(2)}) collective-permute-start(f32[8,64,512]{2,1,0:T(8,128)} %get-tuple-element.135), channel_id=1, source_target_pairs={{0,1},{1,0},{2,3},{3,2},{4,5},{5,4},{6,7},{7,6},{8,9},{9,8},{10,11... | collective-permute-start | bytes 3145736 | tf_op jit(solution)/shard_map/cond/branch_0_fun/ppermute | solution.py:107
  79.4 2.2 %collective-permute-start.18 = (f32[128,512]{1,0:T(8,128)S(1)}, f32[128,512]{1,0:T(8,128)S(1)}, u32[]{:S(2)}, u32[]{:S(2)}) collective-permute-start(f32[128,512]{1,0:T(8,128)S(1)} %get-tuple-element.132), channel_id=1, source_target_pairs={{7,6},{15,14},{23,22},{31,30}} | collective-permute-start | bytes 786440 | tf_op jit(solution)/shard_map/cond/branch_0_fun/ppermute | solution.py:546
  81.7 4.6 %collective-permute-start.19 = (f32[32,512]{1,0:T(8,128)S(1)}, f32[32,512]{1,0:T(8,128)S(1)}, u32[]{:S(2)}, u32[]{:S(2)}) collective-permute-start(f32[32,512]{1,0:T(8,128)S(1)} %get-tuple-element.304), channel_id=1, source_target_pairs={{0,2},{1,3},{2,0},{3,1},{4,6},{5,7},{6,4},{7,5},{8,10},{9,11},{10,... | collective-permute-start | bytes 196616 | tf_op jit(solution)/shard_map/cond/branch_0_fun/ppermute | solution.py:79
  83.4 4.3 %collective-permute-start.20 = (f32[32,512]{1,0:T(8,128)S(1)}, f32[32,512]{1,0:T(8,128)S(1)}, u32[]{:S(2)}, u32[]{:S(2)}) collective-permute-start(f32[32,512]{1,0:T(8,128)S(1)} %get-tuple-element.306), channel_id=1, source_target_pairs={{0,4},{1,5},{2,6},{3,7},{4,0},{5,1},{6,2},{7,3},{8,12},{9,13},{10,... | collective-permute-start | bytes 196616 | tf_op jit(solution)/shard_map/cond/branch_0_fun/ppermute | solution.py:79
  84.0 5.2 %collective-permute-start.21 = (f32[32,512]{1,0:T(8,128)S(1)}, f32[32,512]{1,0:T(8,128)S(1)}, u32[]{:S(2)}, u32[]{:S(2)}) collective-permute-start(f32[32,512]{1,0:T(8,128)S(1)} %get-tuple-element.305), channel_id=1, source_target_pairs={{0,6},{1,7},{2,4},{3,5},{4,2},{5,3},{6,0},{7,1},{8,14},{9,15},{10,... | collective-permute-start | bytes 196616 | tf_op jit(solution)/shard_map/cond/branch_0_fun/ppermute | solution.py:79

commit v3 on v2

--- a/solution.py
+++ b/solution.py
@@ -28,14 +28,6 @@
     owner = column // (BS * BS)
     size_first, size_second = block_sizes(block_dims, owner)
     return (column // BS % BS < size_first) & (column % BS < size_second)
-
-
-def cycle_allowed(block_dims, slab_index, blk_index, local_rows, columns):
-    own_block = jnp.full((1,), slab_index, jnp.int32)
-    size_first, size_second = block_sizes(block_dims, own_block)
-    row_virtual = (blk_index * local_rows + lax.iota(jnp.int32, local_rows)) % BS
-    column_virtual = lax.iota(jnp.int32, columns) % BS
-    return (row_virtual[:, None] < size_first[0]) & (column_virtual[None, :] < size_second[0])
 
 
 def plain(amplitudes, ladder_ints, cycle_ints, block_dims):
@@ -65,7 +57,12 @@
     )
     cycle_term = cycle_term.reshape(cycle_term.shape[0], j_window * BS)
     cycle_sum = lax.psum_scatter(cycle_term, "blk", scatter_dimension=0, tiled=True)
-    allowed = cycle_allowed(block_dims, slab_index, blk_index, cycle_sum.shape[0], j_window * BS)
+    own_block = jnp.full((1,), slab_index, jnp.int32)
+    size_first, size_second = block_sizes(block_dims, own_block)
+    local_rows = cycle_sum.shape[0]
+    row_virtual = (blk_index * local_rows + lax.iota(jnp.int32, local_rows)) % BS
+    column_virtual = lax.iota(jnp.int32, j_window * BS) % BS
+    allowed = (row_virtual[:, None] < size_first[0]) & (column_virtual[None, :] < size_second[0])
     cycle_res = jnp.where(allowed, cycle_sum, 0.0).astype(jnp.bfloat16)[None]
     return (ladder_res, cycle_res)
 
@@ -149,10 +146,10 @@
 
     @pl.when(core == 1)
     def _():
-        compact(moved, 3, wide, tiles(wide, width), 0, 0)
         picks = tiles(narrow, least)
         for g in range(4):
-            compact(amp, g, narrow, picks, 1, wide_columns + g * narrow_columns)
+            compact(amp, g, narrow, picks, 1, g * narrow_columns)
+        compact(moved, 3, wide, tiles(wide, width), 0, 4 * narrow_columns)
 
     shape = (PIECE, PIECE)
     down = lax.broadcasted_iota(jnp.int32, shape, 0) - lax.broadcasted_iota(jnp.int32, shape, 1)
@@ -179,22 +176,25 @@
     )
 
 
-def compact_rows(ladder_ints, moved_ints, width, least, columns, core):
-    def pad(rows):
-        return jnp.pad(rows, ((0, columns - rows.shape[0]), (0, 0)))
-
+def cut_rows(ints, keep):
+    out_columns = ints.shape[-1]
+    rows = ints.reshape(4, -1, 4, BS, out_columns)[:, :, :, :keep]
+    return rows.transpose(1, 0, 2, 3, 4).reshape(-1, out_columns)
+
+
+def pad_rows(rows, count):
+    return jnp.pad(rows, ((0, count - rows.shape[0]), (0, 0)))
+
+
+def own_rows(ladder_ints, width, least, columns, core):
     out_columns = ladder_ints.shape[1]
-
-    def cut(rows, keep):
-        rows = rows.reshape(4, -1, 4, BS, out_columns)[:, :, :, :keep]
-        return rows.transpose(1, 0, 2, 3, 4).reshape(-1, out_columns)
 
     def of_first():
         groups = ladder_ints.reshape(4, 4, 4 * BS, out_columns)
-        return pad(cut(groups[:, :3], width))
+        return pad_rows(cut_rows(groups[:, :3], width), columns)
 
     def of_second():
-        return pad(jnp.concatenate([cut(moved_ints, width), cut(ladder_ints, least)]))
+        return pad_rows(cut_rows(ladder_ints, least), columns)
 
     return lax.cond(core == 0, of_first, of_second)
 
@@ -215,7 +215,8 @@
 VMEM = pl.BlockSpec(memory_space=pltpu.VMEM)
 SMEM = pl.BlockSpec(memory_space=pltpu.SMEM)
 ROOM = pltpu.CompilerParams(vmem_limit_bytes=48 * 1024 * 1024)
-STAGES = (10, 4, 2)
+SHORT = pl.CostEstimate(flops=1024, bytes_accessed=1024, transcendentals=0)
+STAGES = (10, 6)
 
 
 def slots_kernel(part_0, part_1, part_2, part_3, here, there):
@@ -248,13 +249,14 @@
         in_specs=[VMEM] * 4,
         out_specs=[VMEM] * 2,
         compiler_params=ROOM,
+        cost_estimate=SHORT,
         name="slots",
     )(*parts)
 
 
 def products(pieces, rows_w, total):
     depth = rows_w.shape[0]
-    step = max(n for n in range(128, 1025, 128) if depth % n == 0)
+    step = max(n for n in range(128, 513, 128) if depth % n == 0)
     total[...] = jnp.zeros_like(total)
 
     def body(n, carry):
@@ -281,13 +283,14 @@
         in_specs=[VMEM] * (len(pieces) + 1),
         out_specs=VMEM,
         compiler_params=ROOM,
+        cost_estimate=SHORT,
         name="ladder_part",
     )(*pieces, rows_w)
 
 
 def ladder_late_kernel(*refs):
-    pieces = refs[:-6]
-    rows_w, early, middle, mine, other, total = refs[-6:]
+    pieces = refs[:-5]
+    rows_w, early, mine, other, total = refs[-5:]
     core, blk_index = lax.axis_index("slab"), lax.axis_index("blk")
     products(pieces, rows_w, total)
 
@@ -309,22 +312,22 @@
         lax.fori_loop(0, sums.shape[0] // PIECE, body, 0)
 
     place(0, early)
-    place(STAGES[0], middle)
-    place(STAGES[0] + STAGES[1], total)
-
-
-def ladder_late(pieces, rows_w, early, middle):
+    place(STAGES[0], total)
+
+
+def ladder_late(pieces, rows_w, early):
     out_columns = rows_w.shape[1]
     half = jax.ShapeDtypeStruct((8, PIECE, out_columns), jnp.float32)
     return pl.pallas_call(
         ladder_late_kernel,
         out_shape=[half, half],
-        in_specs=[VMEM] * (len(pieces) + 3),
+        in_specs=[VMEM] * (len(pieces) + 2),
         out_specs=[VMEM, VMEM],
-        scratch_shapes=[pltpu.VMEM((STAGES[2] * PIECE, out_columns), jnp.float32)],
+        scratch_shapes=[pltpu.VMEM((STAGES[1] * PIECE, out_columns), jnp.float32)],
         compiler_params=ROOM,
+        cost_estimate=SHORT,
         name="ladder_late",
-    )(*pieces, rows_w, early, middle)
+    )(*pieces, rows_w, early)
 
 
 def ladder_end_kernel(dims, mine, other, out, rows):
@@ -352,10 +355,11 @@
     return pl.pallas_call(
         ladder_end_kernel,
         out_shape=jax.ShapeDtypeStruct(shape, jnp.bfloat16),
-        in_specs=[SMEM, VMEM, VMEM],
+        in_specs=[SMEM] + [VMEM] * 2,
         out_specs=VMEM,
         scratch_shapes=[pltpu.VMEM(shape, jnp.float32)],
         compiler_params=ROOM,
+        cost_estimate=SHORT,
         name="ladder_end",
     )(block_dims, mine, other)
 
@@ -402,8 +406,8 @@
 
 
 def group_starts(width, least, core, plane):
-    first = jnp.where(core == 0, plane, 0) * (GROUP * width)
-    own = GROUP * width + plane * (GROUP * least)
+    first = jnp.where(core == 0, plane * (GROUP * width), 4 * GROUP * least)
+    own = plane * (GROUP * least)
     return pl.multiple_of(first, 128), pl.multiple_of(own, 128)
 
 
@@ -432,11 +436,12 @@
         out_specs=[VMEM, VMEM],
         scratch_shapes=[pltpu.VMEM((blocks * count * PIECE, 128), jnp.float32)],
         compiler_params=ROOM,
+        cost_estimate=SHORT,
         name="cycle_early",
     )(*pieces)
 
 
-def cycle_sum_kernel(width, least, row, turned_before, *refs):
+def cycle_late_kernel(width, least, row, *refs):
     pieces, refs = refs[:-8], refs[-8:]
     before_first, before_own, slots_first, slots_own, first, own, spread, turned = refs
     core, plane = lax.axis_index("slab"), lax.axis_index("blk") & 3
@@ -452,10 +457,10 @@
 
     def total(group_width, start, slots, before, out):
         turn(pieces, group_width, start, spread, turned)
-        if turned_before:
-            out[...] = add(slots, 0, before) + add(slots, row, turned)
-        else:
-            out[...] = before[...] + add(slots, row, turned)
+        value = add(slots, 0, before) + add(slots, row, turned)
+        for n in range(4):
+            to = pl.multiple_of((plane ^ n) * 32, 32)
+            out[pl.ds(to, 32), :] = value[32 * n : 32 * n + 32]
 
     first[...] = jnp.zeros_like(first)
     own[...] = jnp.zeros_like(own)
@@ -468,15 +473,18 @@
     def _():
         total(least, own_start, slots_own, before_own, own)
 
-
-def cycle_add(width, least, stage, pieces, before, slots_first, slots_own):
-    count = STAGES[stage]
+    @pl.when(core == 0)
+    def _():
+        own[...] = first[...]
+
+
+def cycle_late(width, least, pieces, turned, slots_first, slots_own):
+    count = STAGES[1]
     shape = jax.ShapeDtypeStruct((128, 8 * BS), jnp.float32)
     blocks = GROUP * max(width, least) // 128 + 1
-    row = GROUP * 8 * sum(STAGES[:stage])
-    turned_before = before[0].dtype == jnp.bfloat16
-    return pl.pallas_call(
-        functools.partial(cycle_sum_kernel, width, least, row, turned_before),
+    row = GROUP * 8 * STAGES[0]
+    return pl.pallas_call(
+        functools.partial(cycle_late_kernel, width, least, row),
         out_shape=[shape, shape],
         in_specs=[VMEM] * (4 + len(pieces)),
         out_specs=[VMEM, VMEM],
@@ -485,8 +493,31 @@
             pltpu.VMEM((GROUP * 8 * count, 8 * BS), jnp.bfloat16),
         ],
         compiler_params=ROOM,
-        name="cycle_sum",
-    )(*pieces, *before, slots_first, slots_own)
+        cost_estimate=SHORT,
+        name="cycle_late",
+    )(*pieces, *turned, slots_first, slots_own)
+
+
+def cycle_end_kernel(dims, part_0, part_1, part_2, part_3, out):
+    core, blk_index = lax.axis_index("slab"), lax.axis_index("blk")
+    rows, columns = part_0.shape
+    a = blk_index * rows + lax.broadcasted_iota(jnp.int32, (rows, columns), 0) & (BS - 1)
+    d = lax.broadcasted_iota(jnp.int32, (rows, columns), 1) & (BS - 1)
+    keep = (a < dims[core, 0]) & (d < dims[core, 1])
+    total = part_0[...] + part_1[...] + part_2[...] + part_3[...]
+    out[0] = jnp.where(keep, total, 0.0).astype(jnp.bfloat16)
+
+
+def cycle_end(block_dims, parts):
+    return pl.pallas_call(
+        cycle_end_kernel,
+        out_shape=jax.ShapeDtypeStruct((1,) + parts[0].shape, jnp.bfloat16),
+        in_specs=[SMEM] + [VMEM] * 4,
+        out_specs=VMEM,
+        compiler_params=ROOM,
+        cost_estimate=SHORT,
+        name="cycle_end",
+    )(block_dims, *parts)
 
 
 def together(*values):
@@ -512,21 +543,28 @@
     ints, shares = together(ladder_ints, cycle_ints[0], own)[:2]
     moved_ints = ints.reshape(4, 4, 4 * BS, -1)[:, 3].reshape(GROUP * BS, -1)
     shares = [lax.dynamic_slice_in_dim(shares, (z + step) % 4 * 128, 128, 2) for step in range(4)]
-    near, far, moved_ints, ints, *shares = together(
-        jnp.concatenate(near), own, moved_ints, ints, *shares, plane_1, plane_2, plane_12
+    rows_w = own_rows(ints, width, least, columns, core)
+    near, far, moved_ints, rows_w, *shares = together(
+        jnp.concatenate(near), own, moved_ints, rows_w, *shares, plane_1, plane_2, plane_12
     )[:8]
     far = send(far, up(2))
     near_1 = send(near, first_axis)
     near_2 = send(near, second_axis)
     moved_ints = to_other_core(moved_ints, (0,))
-    far, near_1, near_2, moved_ints, *shares = together(far, near_1, near_2, moved_ints, *shares)
+    far, near_1, near_2, rows_w, moved_ints, *shares = together(
+        far, near_1, near_2, rows_w, moved_ints, *shares
+    )
+    cut = 4 * narrow_columns
+    moved_rows = pad_rows(cut_rows(moved_ints, width), columns - cut)
+    rows_w = lax.dynamic_update_slice(
+        rows_w, jnp.where(core == 0, rows_w[cut:], moved_rows), (cut, 0)
+    )
     far_1 = send(far, first_axis)
     far_2 = send(far, second_axis)
     near_12 = send(near_1, second_axis)
     shares[3] = send(shares[3], up(3))
     shares[2] = send(shares[2], up(2))
     shares[1] = send(after(shares[1], shares[3]), up(1))
-    rows_w = compact_rows(ints, moved_ints, width, least, columns, core)
     early = [own, plane_1, plane_2, plane_12, near, near_1, near_2]
     sums = ladder_part(early, rows_w)
     turned = cycle_early(width, least, early)
@@ -535,29 +573,19 @@
     )
     far_12 = send(far_1, second_axis)
     slots, there = slots_of_pieces(shares)
-    slots_first = jnp.where(core == 0, slots, to_other_core(there, (0,)))
-    middle = [near_12, far, far_1]
-    sums_middle = ladder_part(middle, rows_w)
-    terms = cycle_add(width, least, 1, middle, turned, slots_first, slots)
-
-    late = [far_2, far_12]
-    terms = cycle_add(width, least, 2, late, terms, slots_first, slots)
+    there = to_other_core(there, (0,))
+    near_12, far_12, slots, there = together(near_12, far_12, slots, there)
+    slots_first = jnp.where(core == 0, slots, there)
+    late = [near_12, far, far_1, far_2, far_12]
+    terms = cycle_late(width, least, late, turned, slots_first, slots)
     pairs = [(2 * chip + 1, 2 * chip) for chip in (3, 7, 11, 15)]
     last_group = lax.ppermute(terms[0], AXES, pairs)
-    mine, other = ladder_late(late, rows_w, after(sums, terms[0]), sums_middle)
+    mine, other = ladder_late(late, rows_w, after(sums, terms[1]))
     other = to_other_core(other, (0, 1))
-    term = jnp.where(core == 0, jnp.where(plane == 3, last_group, terms[0]), terms[1])
-    term = term.reshape(4, 32, 8 * BS)
-
-    def chunk(chip):
-        return lax.dynamic_index_in_dim(term, chip, 0, False)
-
-    cycle_sum = chunk(plane)
-    for distance, target in ((1, along_x), (2, along_y), (3, across)):
-        cycle_sum = cycle_sum + send(chunk(plane ^ distance), target)
+    term = (terms[1] + last_group).reshape(4, 32, 8 * BS)
+    parts = [send(term[n], target) for n, target in ((1, along_x), (2, along_y), (3, across))]
     ladder_res = ladder_end(block_dims, mine, other)
-    allowed = cycle_allowed(block_dims, core, blk_index, 32, 8 * BS)
-    cycle_res = jnp.where(allowed, cycle_sum, 0.0).astype(jnp.bfloat16)[None]
+    cycle_res = cycle_end(block_dims, [after(term[0], ladder_res)] + parts)
     return (ladder_res, cycle_res)
 
 

time: 91.8 us -> 100 us (1.089)
  waiting for transfers between devices: 26.4 us -> 38.6 us
  Pallas kernels: 18.3 us -> 16.3 us
  starting transfers between devices: 31.5 us -> 29.9 us
    ppermute x18, waiting for transfers between devices: 26.4 us -> 38.6 us  [send(): return lax.ppermute(value, AXES, pairs)]
    dynamic_update_slice x0 -> x1, other arithmetic: none -> 2.95 us  [compacted(): lax.dynamic_update_slice(rows_w, jnp.where(core == 0, rows_w[cut:], moved...]
    ppermute x18, starting transfers between devices: 25.7 us -> 24.1 us  [send(): return lax.ppermute(value, AXES, pairs)]
    lt x2 -> x0, other arithmetic: 1.31 us -> none  [the longest x1 0.66 us: cycle_allowed(): row_virtual[:, None] < size_first[0]]
    pallas_call x2 -> x1, Pallas kernels: 4.29 us -> 3.11 us  [ladder_part(): pl.pallas_call(ladder_part_kernel, out_shape=jax.ShapeDtypeStruct(shape,...]
    dynamic_slice x1, local copies, waits for them, and re-layouts: 0.78 us -> 1.91 us  [compacted(): lax.dynamic_slice_in_dim(shares, (z + step) % 4 * 128, 128, 2)]
    slice x4 -> x3, local copies, waits for them, and re-layouts: 4.09 us -> 4.04 us  [the longest x2 4.02 us: of_first(): return pad_rows(cut_rows(groups[:, :3], width), columns)]
  transfers between devices with their start and end apart: 23 -> 23, of which waited for: 8 -> 8; matrix products, arithmetic and copies ran while one was open for 12% -> 12% of each run, Pallas kernels for 9% -> 7%
where the time goes in v3:
time: 100 us; the launch traced here: 99.6 us
  waiting for transfers between devices  38.6 us (39%)
  starting transfers between devices  29.9 us (30%)
  Pallas kernels  16.3 us (16%)
  local copies, waits for them, and re-layouts  8.6 us (9%)
  other arithmetic  3.12 us (3%)
  between operations  2.6 us (3%)
    ppermute x18, waiting for transfers between devices, send(): return lax.ppermute(value, AXES, pairs)  38.6 us
    ppermute x18, starting transfers between devices, send(): return lax.ppermute(value, AXES, pairs)  24.1 us
    ppermute x4, starting transfers between devices, to_other_core(): return lax.ppermute(value, 'slab', [(core, 1 - core) for core in cores])  5.14 us
    slice x2, local copies, waits for them, and re-layouts, of_first(): return pad_rows(cut_rows(groups[:, :3], width), columns)  4.02 us
    pallas_call x1, Pallas kernels, ladder_part(): pl.pallas_call(ladder_part_kernel, out_shape=jax.ShapeDtypeStruct(shape,...  3.11 us
    dynamic_update_slice x1, other arithmetic, compacted(): lax.dynamic_update_slice(rows_w, jnp.where(core == 0, rows_w[cut:], moved...  2.95 us
    pallas_call x1, Pallas kernels, ladder_late(): pl.pallas_call(ladder_late_kernel, out_shape=[half, half], in_specs=[VMEM...  2.89 us
    pallas_call x1, Pallas kernels, cycle_late(): pl.pallas_call(functools.partial(cycle_late_kernel, width, least, row), o...  2.51 us
  transfers between devices with their start and end apart: 23, of which 8 were waited for; matrix products, arithmetic and copies ran while one was open for 12% of the time, Pallas kernels for 7%

profile of v3, /device:TPU:0, one launch (start us, length us, event | category | flops | bytes accessed | tf_op | source)
XLA Modules:
  0.0 99.6 jit_solution(10324832474802860510)
XLA Ops:
  0.6 2.4 %collective-permute-start.88 = (bf16[60,4096]{1,0:T(8,128)(2,1)}, bf16[60,4096]{1,0:T(8,128)(2,1)S(1)}, u32[]{:S(2)}, u32[]{:S(2)}) collective-permute-start(bf16[60,4096]{1,0:T(8,128)(2,1)} %param.24), channel_id=1, source_target_pairs={{0,1},{2,3},{4,5},{6,7},{8,9},{10,11},{12,13},{14,15},{16,17},{18,... | collective-permute-start | bytes 1474568 | tf_op jit(solution)/shard_map/ppermute | solution.py:104
  3.0 1.3 %fusion.4 = (s32[1,1]{1,0:T(1,128)}, s32[1,1]{1,0:T(1,128)}) fusion(s32[2,2]{1,0:T(2,128)} %param.27), kind=kLoop, calls=%fused_computation.33 | loop fusion | bytes 16 | tf_op jit(solution)/shard_map/slice | solution.py:597
  6.3 0.0 collective-permute-done.88
  6.3 93.3 %conditional.5 = (bf16[480,512]{1,0:T(8,128)(2,1)}, bf16[1,32,512]{2,1,0:T(8,128)(2,1)}) conditional(s32[]{:T(128)} %bitcast.58, (s32[2,2]{1,0:T(2,128)}, bf16[60,4096]{1,0:T(8,128)(2,1)}, bf16[60,4096]{1,0:T(8,128)(2,1)S(1)}, (), s32[8,384]{1,0:T(8,128)}, /*index=5*/bf16[1,4,120,512]{3,2,1,0:T(8,128)(2,1)}, ...), branch_computations={%region_0.3_spmd, %region_3.6_spmd, %region_6.9_spmd, %region_9.12... | conditional | flops 1514581 | bytes 145073456 | solution.py:602
  6.6 2.5 %prep.6 = bf16[64,3072]{1,0:T(8,128)(2,1)} custom-call(s32[2,2]{1,0:T(2,128)} %get-tuple-element.178.dims, bf16[60,4096]{1,0:T(8,128)(2,1)} %get-tuple-element.179.amp, bf16[60,4096]{1,0:T(8,128)(2,1)S(1)} %get-tuple-element.180.moved, s32[8,1024]{1,0:T(8,128)} %get-tuple-element.181.wide, s32[8,384]{1,0:T(8,128)} %get-tuple-element.182.narrow), custom_call_target="tpu_custom_call" | custom-call | tf_op jit(solution)/shard_map/cond/branch_2_fun/prep/pallas_call | solution.py:163
  9.0 2.3 %collective-permute-start.46 = (bf16[1,64,3072]{2,1,0:T(8,128)(2,1)}, bf16[1,64,3072]{2,1,0:T(8,128)(2,1)S(1)}, u32[]{:S(2)}, u32[]{:S(2)}) collective-permute-start(bf16[1,64,3072]{2,1,0:T(8,128)(2,1)} %bitcast.71), channel_id=1, source_target_pairs={{0,2},{1,5},{2,0},{3,7},{4,6},{5,1},{6,4},{7,3},{8,10},{9,13},{10,... | collective-permute-start | bytes 1179656 | tf_op jit(solution)/shard_map/cond/branch_2_fun/ppermute | solution.py:76
  11.4 3.6 %collective-permute-start.45 = (bf16[1,64,3072]{2,1,0:T(8,128)(2,1)}, bf16[1,64,3072]{2,1,0:T(8,128)(2,1)S(1)}, u32[]{:S(2)}, u32[]{:S(2)}) collective-permute-start(bf16[1,64,3072]{2,1,0:T(8,128)(2,1)} %bitcast.72), channel_id=1, source_target_pairs={{0,24},{1,25},{2,26},{3,27},{4,28},{5,29},{6,30},{7,31},{8,0},{9,1... | collective-permute-start | bytes 1179656 | tf_op jit(solution)/shard_map/cond/branch_2_fun/ppermute | solution.py:76
  15.0 0.0 collective-permute-start.44
  15.0 1.5 %collective-permute-start.47 = (bf16[1,64,3072]{2,1,0:T(8,128)(2,1)}, bf16[1,64,3072]{2,1,0:T(8,128)(2,1)S(1)}, u32[]{:S(2)}, u32[]{:S(2)}) collective-permute-start(bf16[1,64,3072]{2,1,0:T(8,128)(2,1)} %bitcast.74), channel_id=1, source_target_pairs={{0,4},{1,3},{2,6},{3,1},{4,0},{5,7},{6,2},{7,5},{8,12},{9,11},{10,... | collective-permute-start | bytes 1179656 | tf_op jit(solution)/shard_map/cond/branch_2_fun/ppermute | solution.py:76
  16.5 1.6 %collective-permute-done.46.refs_1_ = bf16[1,64,3072]{2,1,0:T(8,128)(2,1)S(1)} collective-permute-done((bf16[1,64,3072]{2,1,0:T(8,128)(2,1)}, bf16[1,64,3072]{2,1,0:T(8,128)(2,1)S(1)}, u32[]{:S(2)}, u32[]{:S(2)}) %collective-permute-start.46) | collective-permute-done | bytes 393248 | tf_op jit(solution)/shard_map/cond/branch_2_fun/ppermute | solution.py:76
  18.1 3.4 %collective-permute-start.48 = (bf16[1,64,3072]{2,1,0:T(8,128)(2,1)S(1)}, bf16[1,64,3072]{2,1,0:T(8,128)(2,1)S(1)}, u32[]{:S(2)}, u32[]{:S(2)}) collective-permute-start(bf16[1,64,3072]{2,1,0:T(8,128)(2,1)S(1)} %collective-permute-done.46.refs_1_), channel_id=1, source_target_pairs={{0,4},{1,3},{2,6},{3,1},{4,0},{5,7},{6,2},{7,5},{8,12},{9,11},{10,... | collective-permute-start | bytes 1179656 | tf_op jit(solution)/shard_map/cond/branch_2_fun/ppermute | solution.py:76
  21.5 1.9 %constant_dynamic-slice_fusion.8 = (bf16[4,120,128]{2,1,0:T(8,128)(2,1)}, bf16[4,120,128]{2,1,0:T(8,128)(2,1)}, bf16[4,120,128]{2,1,0:T(8,128)(2,1)}, bf16[4,120,128]{2,1,0:T(8,128)(2,1)S(1)}) fusion(bf16[4,120,512]{2,1,0:T(8,128)(2,1)} %bitcast.114, s32[]{:T(128)S(6)} %select_n.173, s32[]{:T(128)S(6)} %select_n.171, s32[]{:T(128)S(6)} %select_n.169, ...), kind=kLoop, calls=%fused_computation.18 | loop fusion | bytes 983056 | tf_op jit(solution)/shard_map/cond/branch_2_fun/dynamic_slice | solution.py:545
  23.4 1.3 %slice.150 = bf16[4,1,256,512]{3,2,1,0:T(8,128)(2,1)S(1)} slice(bf16[4,4,256,512]{3,2,1,0:T(8,128)(2,1)} %bitcast.98), slice={[0:4], [3:4], [0:256], [0:512]} | slice | bytes 2097152 | tf_op jit(solution)/shard_map/cond/branch_2_fun/slice | solution.py:544
  24.7 0.0 copy-start.4
  24.8 4.0 %conditional.2 = (bf16[3072,512]{1,0:T(8,128)(2,1)}) conditional(s32[]{:T(128)} %convert_element_type.30, bf16[4096,512]{1,0:T(8,128)(2,1)} %get-tuple-element.185, bf16[4096,512]{1,0:T(8,128)(2,1)} %get-tuple-element.185), branch_computations={%region_7.7_spmd, %region_8.8_spmd} | conditional | bytes 12582920 | solution.py:199
  24.8 2.1 %slice.149 = bf16[4,3,256,512]{3,2,1,0:T(8,128)(2,1)S(1)} slice(bf16[4,4,256,512]{3,2,1,0:T(8,128)(2,1)} %bitcast.100), slice={[0:4], [0:3], [0:256], [0:512]} | slice | bytes 6291456 | tf_op jit(solution)/shard_map/cond/branch_2_fun/cond/branch_1_fun/slice | solution.py:194
  26.9 1.9 %copy.25 = bf16[4,3,256,512]{3,2,0,1:T(8,128)(2,1)} copy(bf16[4,3,256,512]{3,2,1,0:T(8,128)(2,1)S(1)} %slice.149) | data formatting | bytes 6291456 | tf_op jit(solution)/shard_map/cond/branch_2_fun/cond/branch_1_fun/slice | solution.py:194
  28.8 0.0 collective-permute-done.45
  28.8 3.4 %collective-permute-done.44 = bf16[1,64,3072]{2,1,0:T(8,128)(2,1)S(1)} collective-permute-done((bf16[1,64,3072]{2,1,0:T(8,128)(2,1)}, bf16[1,64,3072]{2,1,0:T(8,128)(2,1)S(1)}, u32[]{:S(2)}, u32[]{:S(2)}) %collective-permute-start.44) | collective-permute-done | bytes 393248 | tf_op jit(solution)/shard_map/cond/branch_2_fun/ppermute | solution.py:76
  32.2 0.1 pad_maximum_fusion.2.refs_4_
  32.3 0.0 collective-permute-done.47.refs_2_
  32.3 0.0 collective-permute-done.48.refs_3_
  32.3 1.4 %collective-permute-start.52 = (bf16[1024,512]{1,0:T(8,128)(2,1)S(1)}, bf16[1024,512]{1,0:T(8,128)(2,1)S(1)}, u32[]{:S(2)}, u32[]{:S(2)}) collective-permute-start(bf16[1024,512]{1,0:T(8,128)(2,1)S(1)} %bitcast.122), channel_id=1, source_target_pairs={{0,1},{2,3},{4,5},{6,7},{8,9},{10,11},{12,13},{14,15},{16,17},{18,... | collective-permute-start | bytes 3145736 | tf_op jit(solution)/shard_map/cond/branch_2_fun/ppermute | solution.py:104
  33.7 0.6 collective-permute-start.51
  34.2 1.5 %collective-permute-start.50 = (bf16[2,64,3072]{2,1,0:T(8,128)(2,1)S(1)}, bf16[2,64,3072]{2,1,0:T(8,128)(2,1)S(1)}, u32[]{:S(2)}, u32[]{:S(2)}) collective-permute-start(bf16[2,64,3072]{2,1,0:T(8,128)(2,1)S(1)} %pad_maximum_fusion.2.refs_4_), channel_id=1, source_target_pairs={{0,2},{1,5},{2,0},{3,7},{4,6},{5,1},{6,4},{7,3},{8,10},{9,13},{10,... | collective-permute-start | bytes 2359304 | tf_op jit(solution)/shard_map/cond/branch_2_fun/ppermute | solution.py:76
  35.7 1.0 %collective-permute-start.49 = (bf16[1,64,3072]{2,1,0:T(8,128)(2,1)S(1)}, bf16[1,64,3072]{2,1,0:T(8,128)(2,1)S(1)}, u32[]{:S(2)}, u32[]{:S(2)}) collective-permute-start(bf16[1,64,3072]{2,1,0:T(8,128)(2,1)S(1)} %bitcast.75), channel_id=1, source_target_pairs={{0,16},{1,17},{2,18},{3,19},{4,20},{5,21},{6,22},{7,23},{8,24},{9,... | collective-permute-start | bytes 1179656 | tf_op jit(solution)/shard_map/cond/branch_2_fun/ppermute | solution.py:76
  36.8 17.8 %collective-permute-done.49.refs_1_ = bf16[1,64,3072]{2,1,0:T(8,128)(2,1)S(1)} collective-permute-done((bf16[1,64,3072]{2,1,0:T(8,128)(2,1)S(1)}, bf16[1,64,3072]{2,1,0:T(8,128)(2,1)S(1)}, u32[]{:S(2)}, u32[]{:S(2)}) %collective-permute-start.49) | collective-permute-done | bytes 393248 | tf_op jit(solution)/shard_map/cond/branch_2_fun/ppermute | solution.py:76
  54.5 0.0 collective-permute-done.51.refs_6_
  54.5 0.0 collective-permute-done.50.refs_5_
  54.5 0.0 collective-permute-done.52
  54.5 1.8 %collective-permute-start.55 = (bf16[2,64,3072]{2,1,0:T(8,128)(2,1)S(1)}, bf16[2,64,3072]{2,1,0:T(8,128)(2,1)S(1)}, u32[]{:S(2)}, u32[]{:S(2)}) collective-permute-start(bf16[2,64,3072]{2,1,0:T(8,128)(2,1)S(1)} %collective-permute-done.50.refs_5_), channel_id=1, source_target_pairs={{0,4},{1,3},{2,6},{3,1},{4,0},{5,7},{6,2},{7,5},{8,12},{9,11},{10,... | collective-permute-start | bytes 2359304 | tf_op jit(solution)/shard_map/cond/branch_2_fun/ppermute | solution.py:76
  56.3 1.3 %collective-permute-start.56 = (bf16[4,120,128]{2,1,0:T(8,128)(2,1)}, bf16[4,120,128]{2,1,0:T(8,128)(2,1)S(1)}, u32[]{:S(2)}, u32[]{:S(2)}) collective-permute-start(bf16[4,120,128]{2,1,0:T(8,128)(2,1)} %get-tuple-element.204), channel_id=1, source_target_pairs={{0,24},{1,25},{2,26},{3,27},{4,28},{5,29},{6,30},{7,31},{8,0},{9,1... | collective-permute-start | bytes 368648 | tf_op jit(solution)/shard_map/cond/branch_2_fun/ppermute | solution.py:76
  57.6 0.3 collective-permute-start.54
  57.9 0.4 collective-permute-start.53
  58.4 0.7 collective-permute-start.58
  59.1 2.4 %collective-permute-done.56.part_3 = bf16[4,120,128]{2,1,0:T(8,128)(2,1)S(1)} collective-permute-done((bf16[4,120,128]{2,1,0:T(8,128)(2,1)}, bf16[4,120,128]{2,1,0:T(8,128)(2,1)S(1)}, u32[]{:S(2)}, u32[]{:S(2)}) %collective-permute-start.56) | collective-permute-done | bytes 122912 | tf_op jit(solution)/shard_map/cond/branch_2_fun/ppermute | solution.py:76
  61.5 0.0 collective-permute-start.57
  61.5 3.0 %select_dynamic-update-slice_fusion.1.refs_7_.refs_5_ = bf16[3072,512]{1,0:T(8,128)(2,1)} fusion(bf16[3072,512]{1,0:T(8,128)(2,1)} %get-tuple-element.331, bf16[1024,512]{1,0:T(8,128)(2,1)S(1)} %collective-permute-done.52, pred[]{:T(512)S(6)} %eq.35), kind=kLoop, calls=%fused_computation.15 | loop fusion | flops 786432 | bytes 4194305 | tf_op jit(solution)/shard_map/cond/branch_2_fun/dynamic_update_slice | solution.py:559
  64.4 2.2 %cycle_early.6 = (bf16[1280,512]{1,0:T(8,128)(2,1)S(1)}, bf16[1280,512]{1,0:T(8,128)(2,1)}) custom-call(bf16[1,64,3072]{2,1,0:T(8,128)(2,1)S(1)} %bitcast.76, bf16[1,64,3072]{2,1,0:T(8,128)(2,1)S(1)} %collective-permute-done.46.refs_1_, bf16[1,64,3072]{2,1,0:T(8,128)(2,1)S(1)} %collective-permute-done.47.refs_2_, ...), custom_call_target="tpu_custom_call" | custom-call | flops 1024 | bytes 1024 | tf_op jit(solution)/shard_map/cond/branch_2_fun/cycle_early/pallas_call | solution.py:432
  66.6 3.1 %ladder_part.6.refs_6_ = f32[640,512]{1,0:T(8,128)S(1)} custom-call(bf16[1,64,3072]{2,1,0:T(8,128)(2,1)S(1)} %bitcast.77, bf16[1,64,3072]{2,1,0:T(8,128)(2,1)S(1)} %collective-permute-done.46.refs_1_, bf16[1,64,3072]{2,1,0:T(8,128)(2,1)S(1)} %collective-permute-done.47.refs_2_, bf16[1,64,3072]{2,1,0:T(8,128)(2,1)S(1)} %collective-permute-done.48.refs_3_, ...), custom_call_target="tpu_custom_call" | custom-call | flops 1024 | bytes 1024 | tf_op jit(solution)/shard_map/cond/branch_2_fun/ladder_part/pallas_call | solution.py:280
  69.8 0.0 collective-permute-done.58.part_2
  69.8 0.0 collective-permute-done.57.part_1
  69.8 5.2 %collective-permute-done.54.refs_3_ = bf16[1,64,3072]{2,1,0:T(8,128)(2,1)S(1)} collective-permute-done((bf16[1,64,3072]{2,1,0:T(8,128)(2,1)S(1)}, bf16[1,64,3072]{2,1,0:T(8,128)(2,1)S(1)}, u32[]{:S(2)}, u32[]{:S(2)}) %collective-permute-start.54) | collective-permute-done | bytes 393248 | tf_op jit(solution)/shard_map/cond/branch_2_fun/ppermute | solution.py:76
  75.0 0.0 collective-permute-done.53.refs_2_
  75.0 0.0 collective-permute-done.55.refs_0_
  75.0 0.5 slots.6
  75.5 1.3 %collective-permute-start.60 = (bf16[2048,128]{1,0:T(8,128)(2,1)S(1)}, bf16[2048,128]{1,0:T(8,128)(2,1)S(1)}, u32[]{:S(2)}, u32[]{:S(2)}) collective-permute-start(bf16[2048,128]{1,0:T(8,128)(2,1)S(1)} %get-tuple-element.214), channel_id=1, source_target_pairs={{0,1},{2,3},{4,5},{6,7},{8,9},{10,11},{12,13},{14,15},{16,17},{18,... | collective-permute-start | bytes 1572872 | tf_op jit(solution)/shard_map/cond/branch_2_fun/ppermute | solution.py:104
  76.8 1.8 %collective-permute-start.59 = (bf16[1,64,3072]{2,1,0:T(8,128)(2,1)S(1)}, bf16[1,64,3072]{2,1,0:T(8,128)(2,1)S(1)}, u32[]{:S(2)}, u32[]{:S(2)}) collective-permute-start(bf16[1,64,3072]{2,1,0:T(8,128)(2,1)S(1)} %collective-permute-done.53.refs_2_), channel_id=1, source_target_pairs={{0,4},{1,3},{2,6},{3,1},{4,0},{5,7},{6,2},{7,5},{8,12},{9,11},{10,... | collective-permute-start | bytes 1179656 | tf_op jit(solution)/shard_map/cond/branch_2_fun/ppermute | solution.py:76
  78.6 6.0 %collective-permute-done.59.refs_4_ = bf16[1,64,3072]{2,1,0:T(8,128)(2,1)S(1)} collective-permute-done((bf16[1,64,3072]{2,1,0:T(8,128)(2,1)S(1)}, bf16[1,64,3072]{2,1,0:T(8,128)(2,1)S(1)}, u32[]{:S(2)}, u32[]{:S(2)}) %collective-permute-start.59) | collective-permute-done | bytes 393248 | tf_op jit(solution)/shard_map/cond/branch_2_fun/ppermute | solution.py:76
  84.6 0.0 collective-permute-done.60
  84.7 0.1 broadcast_select_fusion.2.refs_7_
  84.7 2.5 %cycle_late.6 = (f32[128,512]{1,0:T(8,128)S(1)}, f32[128,512]{1,0:T(8,128)S(1)}) custom-call(bf16[2,64,3072]{2,1,0:T(8,128)(2,1)S(1)} %collective-permute-done.55.refs_0_, bf16[1,64,3072]{2,1,0:T(8,128)(2,1)S(1)} %collective-permute-done.49.refs_1_, bf16[1,64,3072]{2,1,0:T(8,128)(2,1)S(1)} %collective-permute-done.53.refs_2_, ...), custom_call_target="tpu_custom_call" | custom-call | flops 1024 | bytes 1024 | tf_op jit(solution)/shard_map/cond/branch_2_fun/cycle_late/pallas_call | solution.py:486
  87.2 0.0 copy-start.18
  87.2 2.9 %ladder_late.6 = (f32[8,64,512]{2,1,0:T(8,128)S(1)}, f32[8,64,512]{2,1,0:T(8,128)S(1)}) custom-call(bf16[2,64,3072]{2,1,0:T(8,128)(2,1)S(1)} %collective-permute-done.55.refs_0_, bf16[1,64,3072]{2,1,0:T(8,128)(2,1)S(1)} %collective-permute-done.49.refs_1_, bf16[1,64,3072]{2,1,0:T(8,128)(2,1)S(1)} %collective-permute-done.53.refs_2_, ...), custom_call_target="tpu_custom_call" | custom-call | flops 1024 | bytes 1024 | tf_op jit(solution)/shard_map/cond/branch_2_fun/ladder_late/pallas_call | solution.py:321
  90.1 0.1 collective-permute-start.61
  90.2 0.7 collective-permute-start.62
  90.9 0.0 collective-permute-done.62
  91.0 3.2 %collective-permute-start.65 = (f32[32,512]{1,0:T(8,128)S(1)}, f32[32,512]{1,0:T(8,128)S(1)}, u32[]{:S(2)}, u32[]{:S(2)}) collective-permute-start(f32[32,512]{1,0:T(8,128)S(1)} %get-tuple-element.307), channel_id=1, source_target_pairs={{0,6},{1,7},{2,4},{3,5},{4,2},{5,3},{6,0},{7,1},{8,14},{9,15},{10,... | collective-permute-start | bytes 196616 | tf_op jit(solution)/shard_map/cond/branch_2_fun/ppermute | solution.py:76
  94.2 0.0 collective-permute-start.64
  94.2 0.6 collective-permute-start.63
  94.8 1.5 %ladder_end.6 = bf16[480,512]{1,0:T(8,128)(2,1)} custom-call(s32[2,2]{1,0:T(2,128)S(1)} %copy-done.18, f32[8,64,512]{2,1,0:T(8,128)S(1)} %get-tuple-element.225.mine, f32[8,64,512]{2,1,0:T(8,128)S(1)} %collective-permute-done.61.other), custom_call_target="tpu_custom_call" | custom-call | flops 1024 | bytes 1024 | tf_op jit(solution)/shard_map/cond/branch_2_fun/ladder_end/pallas_call | solution.py:355
  96.3 0.2 collective-permute-done.65.part_3
  96.6 1.9 %collective-permute-done.64.part_2 = f32[32,512]{1,0:T(8,128)S(1)} collective-permute-done((f32[32,512]{1,0:T(8,128)S(1)}, f32[32,512]{1,0:T(8,128)S(1)}, u32[]{:S(2)}, u32[]{:S(2)}) %collective-permute-start.64) | collective-permute-done | bytes 65568 | tf_op jit(solution)/shard_map/cond/branch_2_fun/ppermute | solution.py:76
  98.5 1.2 %cycle_end.6 = bf16[1,32,512]{2,1,0:T(8,128)(2,1)} custom-call(s32[2,2]{1,0:T(2,128)S(1)} %copy-done.18, f32[32,512]{1,0:T(8,128)S(1)} %get-tuple-element.228.part_0, f32[32,512]{1,0:T(8,128)S(1)} %collective-permute-done.63.part_1, f32[32,512]{1,0:T(8,128)S(1)} %collective-permute-done.64.part_2, f32[32,512]{1,0:T(8,128)S(1)} %collective-permute-done.65.part_3), custom_call_target="tpu_custom_call" | custom-call | flops 1024 | bytes 1024 | tf_op jit(solution)/shard_map/cond/branch_2_fun/cycle_end/pallas_call | solution.py:512
  (8 shorter events, 0.1 us)
Async XLA Ops:
  0.6 5.7 %collective-permute-start.88 = (bf16[60,4096]{1,0:T(8,128)(2,1)}, bf16[60,4096]{1,0:T(8,128)(2,1)S(1)}, u32[]{:S(2)}, u32[]{:S(2)}) collective-permute-start(bf16[60,4096]{1,0:T(8,128)(2,1)} %param.24), channel_id=1, source_target_pairs={{0,1},{2,3},{4,5},{6,7},{8,9},{10,11},{12,13},{14,15},{16,17},{18,... | collective-permute-start | bytes 1474568 | tf_op jit(solution)/shard_map/ppermute | solution.py:104
  9.0 9.1 %collective-permute-start.46 = (bf16[1,64,3072]{2,1,0:T(8,128)(2,1)}, bf16[1,64,3072]{2,1,0:T(8,128)(2,1)S(1)}, u32[]{:S(2)}, u32[]{:S(2)}) collective-permute-start(bf16[1,64,3072]{2,1,0:T(8,128)(2,1)} %bitcast.71), channel_id=1, source_target_pairs={{0,2},{1,5},{2,0},{3,7},{4,6},{5,1},{6,4},{7,3},{8,10},{9,13},{10,... | collective-permute-start | bytes 1179656 | tf_op jit(solution)/shard_map/cond/branch_2_fun/ppermute | solution.py:76
  11.4 17.4 %collective-permute-start.45 = (bf16[1,64,3072]{2,1,0:T(8,128)(2,1)}, bf16[1,64,3072]{2,1,0:T(8,128)(2,1)S(1)}, u32[]{:S(2)}, u32[]{:S(2)}) collective-permute-start(bf16[1,64,3072]{2,1,0:T(8,128)(2,1)} %bitcast.72), channel_id=1, source_target_pairs={{0,24},{1,25},{2,26},{3,27},{4,28},{5,29},{6,30},{7,31},{8,0},{9,1... | collective-permute-start | bytes 1179656 | tf_op jit(solution)/shard_map/cond/branch_2_fun/ppermute | solution.py:76
  15.0 17.3 %collective-permute-start.44 = (bf16[1,64,3072]{2,1,0:T(8,128)(2,1)}, bf16[1,64,3072]{2,1,0:T(8,128)(2,1)S(1)}, u32[]{:S(2)}, u32[]{:S(2)}) collective-permute-start(bf16[1,64,3072]{2,1,0:T(8,128)(2,1)} %bitcast.73), channel_id=1, source_target_pairs={{0,8},{1,9},{2,10},{3,11},{4,12},{5,13},{6,14},{7,15},{8,16},{9,17... | collective-permute-start | bytes 1179656 | tf_op jit(solution)/shard_map/cond/branch_2_fun/ppermute | solution.py:76
  15.0 17.3 %collective-permute-start.47 = (bf16[1,64,3072]{2,1,0:T(8,128)(2,1)}, bf16[1,64,3072]{2,1,0:T(8,128)(2,1)S(1)}, u32[]{:S(2)}, u32[]{:S(2)}) collective-permute-start(bf16[1,64,3072]{2,1,0:T(8,128)(2,1)} %bitcast.74), channel_id=1, source_target_pairs={{0,4},{1,3},{2,6},{3,1},{4,0},{5,7},{6,2},{7,5},{8,12},{9,11},{10,... | collective-permute-start | bytes 1179656 | tf_op jit(solution)/shard_map/cond/branch_2_fun/ppermute | solution.py:76
  18.1 14.2 %collective-permute-start.48 = (bf16[1,64,3072]{2,1,0:T(8,128)(2,1)S(1)}, bf16[1,64,3072]{2,1,0:T(8,128)(2,1)S(1)}, u32[]{:S(2)}, u32[]{:S(2)}) collective-permute-start(bf16[1,64,3072]{2,1,0:T(8,128)(2,1)S(1)} %collective-permute-done.46.refs_1_), channel_id=1, source_target_pairs={{0,4},{1,3},{2,6},{3,1},{4,0},{5,7},{6,2},{7,5},{8,12},{9,11},{10,... | collective-permute-start | bytes 1179656 | tf_op jit(solution)/shard_map/cond/branch_2_fun/ppermute | solution.py:76
  24.7 11.0 %copy-start.4 = (bf16[64,3072]{1,0:T(8,128)(2,1)S(1)}, bf16[64,3072]{1,0:T(8,128)(2,1)}, u32[]{:S(2)}) copy-start(bf16[64,3072]{1,0:T(8,128)(2,1)} %prep.6) | copy-start | bytes 1179652 | tf_op jit(solution)/shard_map/cond
  32.3 22.2 %collective-permute-start.52 = (bf16[1024,512]{1,0:T(8,128)(2,1)S(1)}, bf16[1024,512]{1,0:T(8,128)(2,1)S(1)}, u32[]{:S(2)}, u32[]{:S(2)}) collective-permute-start(bf16[1024,512]{1,0:T(8,128)(2,1)S(1)} %bitcast.122), channel_id=1, source_target_pairs={{0,1},{2,3},{4,5},{6,7},{8,9},{10,11},{12,13},{14,15},{16,17},{18,... | collective-permute-start | bytes 3145736 | tf_op jit(solution)/shard_map/cond/branch_2_fun/ppermute | solution.py:104
  33.7 20.8 %collective-permute-start.51 = (bf16[2,64,3072]{2,1,0:T(8,128)(2,1)S(1)}, bf16[2,64,3072]{2,1,0:T(8,128)(2,1)S(1)}, u32[]{:S(2)}, u32[]{:S(2)}) collective-permute-start(bf16[2,64,3072]{2,1,0:T(8,128)(2,1)S(1)} %pad_maximum_fusion.2.refs_4_), channel_id=1, source_target_pairs={{0,4},{1,3},{2,6},{3,1},{4,0},{5,7},{6,2},{7,5},{8,12},{9,11},{10,... | collective-permute-start | bytes 2359304 | tf_op jit(solution)/shard_map/cond/branch_2_fun/ppermute | solution.py:76
  34.2 20.3 %collective-permute-start.50 = (bf16[2,64,3072]{2,1,0:T(8,128)(2,1)S(1)}, bf16[2,64,3072]{2,1,0:T(8,128)(2,1)S(1)}, u32[]{:S(2)}, u32[]{:S(2)}) collective-permute-start(bf16[2,64,3072]{2,1,0:T(8,128)(2,1)S(1)} %pad_maximum_fusion.2.refs_4_), channel_id=1, source_target_pairs={{0,2},{1,5},{2,0},{3,7},{4,6},{5,1},{6,4},{7,3},{8,10},{9,13},{10,... | collective-permute-start | bytes 2359304 | tf_op jit(solution)/shard_map/cond/branch_2_fun/ppermute | solution.py:76
  35.7 18.8 %collective-permute-start.49 = (bf16[1,64,3072]{2,1,0:T(8,128)(2,1)S(1)}, bf16[1,64,3072]{2,1,0:T(8,128)(2,1)S(1)}, u32[]{:S(2)}, u32[]{:S(2)}) collective-permute-start(bf16[1,64,3072]{2,1,0:T(8,128)(2,1)S(1)} %bitcast.75), channel_id=1, source_target_pairs={{0,16},{1,17},{2,18},{3,19},{4,20},{5,21},{6,22},{7,23},{8,24},{9,... | collective-permute-start | bytes 1179656 | tf_op jit(solution)/shard_map/cond/branch_2_fun/ppermute | solution.py:76
  54.5 20.5 %collective-permute-start.55 = (bf16[2,64,3072]{2,1,0:T(8,128)(2,1)S(1)}, bf16[2,64,3072]{2,1,0:T(8,128)(2,1)S(1)}, u32[]{:S(2)}, u32[]{:S(2)}) collective-permute-start(bf16[2,64,3072]{2,1,0:T(8,128)(2,1)S(1)} %collective-permute-done.50.refs_5_), channel_id=1, source_target_pairs={{0,4},{1,3},{2,6},{3,1},{4,0},{5,7},{6,2},{7,5},{8,12},{9,11},{10,... | collective-permute-start | bytes 2359304 | tf_op jit(solution)/shard_map/cond/branch_2_fun/ppermute | solution.py:76
  56.3 5.1 %collective-permute-start.56 = (bf16[4,120,128]{2,1,0:T(8,128)(2,1)}, bf16[4,120,128]{2,1,0:T(8,128)(2,1)S(1)}, u32[]{:S(2)}, u32[]{:S(2)}) collective-permute-start(bf16[4,120,128]{2,1,0:T(8,128)(2,1)} %get-tuple-element.204), channel_id=1, source_target_pairs={{0,24},{1,25},{2,26},{3,27},{4,28},{5,29},{6,30},{7,31},{8,0},{9,1... | collective-permute-start | bytes 368648 | tf_op jit(solution)/shard_map/cond/branch_2_fun/ppermute | solution.py:76
  57.6 17.4 %collective-permute-start.54 = (bf16[1,64,3072]{2,1,0:T(8,128)(2,1)S(1)}, bf16[1,64,3072]{2,1,0:T(8,128)(2,1)S(1)}, u32[]{:S(2)}, u32[]{:S(2)}) collective-permute-start(bf16[1,64,3072]{2,1,0:T(8,128)(2,1)S(1)} %collective-permute-done.49.refs_1_), channel_id=1, source_target_pairs={{0,4},{1,3},{2,6},{3,1},{4,0},{5,7},{6,2},{7,5},{8,12},{9,11},{10,... | collective-permute-start | bytes 1179656 | tf_op jit(solution)/shard_map/cond/branch_2_fun/ppermute | solution.py:76
  57.9 17.1 %collective-permute-start.53 = (bf16[1,64,3072]{2,1,0:T(8,128)(2,1)S(1)}, bf16[1,64,3072]{2,1,0:T(8,128)(2,1)S(1)}, u32[]{:S(2)}, u32[]{:S(2)}) collective-permute-start(bf16[1,64,3072]{2,1,0:T(8,128)(2,1)S(1)} %collective-permute-done.49.refs_1_), channel_id=1, source_target_pairs={{0,2},{1,5},{2,0},{3,7},{4,6},{5,1},{6,4},{7,3},{8,10},{9,13},{10,... | collective-permute-start | bytes 1179656 | tf_op jit(solution)/shard_map/cond/branch_2_fun/ppermute | solution.py:76
  58.4 11.4 %collective-permute-start.58 = (bf16[4,120,128]{2,1,0:T(8,128)(2,1)}, bf16[4,120,128]{2,1,0:T(8,128)(2,1)S(1)}, u32[]{:S(2)}, u32[]{:S(2)}) collective-permute-start(bf16[4,120,128]{2,1,0:T(8,128)(2,1)} %get-tuple-element.206), channel_id=1, source_target_pairs={{0,16},{1,17},{2,18},{3,19},{4,20},{5,21},{6,22},{7,23},{8,24},{9,... | collective-permute-start | bytes 368648 | tf_op jit(solution)/shard_map/cond/branch_2_fun/ppermute | solution.py:76
  61.5 8.3 %collective-permute-start.57 = (bf16[4,120,128]{2,1,0:T(8,128)(2,1)}, bf16[4,120,128]{2,1,0:T(8,128)(2,1)S(1)}, u32[]{:S(2)}, u32[]{:S(2)}) collective-permute-start(bf16[4,120,128]{2,1,0:T(8,128)(2,1)} %get-tuple-element.205), channel_id=1, source_target_pairs={{0,8},{1,9},{2,10},{3,11},{4,12},{5,13},{6,14},{7,15},{8,16},{9,17... | collective-permute-start | bytes 368648 | tf_op jit(solution)/shard_map/cond/branch_2_fun/ppermute | solution.py:76
  64.4 2.2 %copy-start.10 = (bf16[3072,512]{1,0:T(8,128)(2,1)S(1)}, bf16[3072,512]{1,0:T(8,128)(2,1)}, u32[]{:S(2)}) copy-start(bf16[3072,512]{1,0:T(8,128)(2,1)} %select_dynamic-update-slice_fusion.1.refs_7_.refs_5_) | copy-start | bytes 9437188 | tf_op jit(solution)/shard_map/cond
  75.5 9.2 %collective-permute-start.60 = (bf16[2048,128]{1,0:T(8,128)(2,1)S(1)}, bf16[2048,128]{1,0:T(8,128)(2,1)S(1)}, u32[]{:S(2)}, u32[]{:S(2)}) collective-permute-start(bf16[2048,128]{1,0:T(8,128)(2,1)S(1)} %get-tuple-element.214), channel_id=1, source_target_pairs={{0,1},{2,3},{4,5},{6,7},{8,9},{10,11},{12,13},{14,15},{16,17},{18,... | collective-permute-start | bytes 1572872 | tf_op jit(solution)/shard_map/cond/branch_2_fun/ppermute | solution.py:104
  76.8 7.8 %collective-permute-start.59 = (bf16[1,64,3072]{2,1,0:T(8,128)(2,1)S(1)}, bf16[1,64,3072]{2,1,0:T(8,128)(2,1)S(1)}, u32[]{:S(2)}, u32[]{:S(2)}) collective-permute-start(bf16[1,64,3072]{2,1,0:T(8,128)(2,1)S(1)} %collective-permute-done.53.refs_2_), channel_id=1, source_target_pairs={{0,4},{1,3},{2,6},{3,1},{4,0},{5,7},{6,2},{7,5},{8,12},{9,11},{10,... | collective-permute-start | bytes 1179656 | tf_op jit(solution)/shard_map/cond/branch_2_fun/ppermute | solution.py:76
  87.2 7.6 %copy-start.18 = (s32[2,2]{1,0:T(2,128)S(1)}, s32[2,2]{1,0:T(2,128)}, u32[]{:S(2)}) copy-start(s32[2,2]{1,0:T(2,128)} %get-tuple-element.178.dims) | copy-start | bytes 52 | tf_op jit(solution)/shard_map/cond
  90.1 4.7 %collective-permute-start.61 = (f32[8,64,512]{2,1,0:T(8,128)S(1)}, f32[8,64,512]{2,1,0:T(8,128)S(1)}, u32[]{:S(2)}, u32[]{:S(2)}) collective-permute-start(f32[8,64,512]{2,1,0:T(8,128)S(1)} %get-tuple-element.226), channel_id=1, source_target_pairs={{0,1},{1,0},{2,3},{3,2},{4,5},{5,4},{6,7},{7,6},{8,9},{9,8},{10,11... | collective-permute-start | bytes 3145736 | tf_op jit(solution)/shard_map/cond/branch_2_fun/ppermute | solution.py:104
  90.2 0.7 collective-permute-start.62
  91.0 5.6 %collective-permute-start.65 = (f32[32,512]{1,0:T(8,128)S(1)}, f32[32,512]{1,0:T(8,128)S(1)}, u32[]{:S(2)}, u32[]{:S(2)}) collective-permute-start(f32[32,512]{1,0:T(8,128)S(1)} %get-tuple-element.307), channel_id=1, source_target_pairs={{0,6},{1,7},{2,4},{3,5},{4,2},{5,3},{6,0},{7,1},{8,14},{9,15},{10,... | collective-permute-start | bytes 196616 | tf_op jit(solution)/shard_map/cond/branch_2_fun/ppermute | solution.py:76
  94.2 4.3 %collective-permute-start.64 = (f32[32,512]{1,0:T(8,128)S(1)}, f32[32,512]{1,0:T(8,128)S(1)}, u32[]{:S(2)}, u32[]{:S(2)}) collective-permute-start(f32[32,512]{1,0:T(8,128)S(1)} %get-tuple-element.308), channel_id=1, source_target_pairs={{0,4},{1,5},{2,6},{3,7},{4,0},{5,1},{6,2},{7,3},{8,12},{9,13},{10,... | collective-permute-start | bytes 196616 | tf_op jit(solution)/shard_map/cond/branch_2_fun/ppermute | solution.py:76
  94.2 4.3 %collective-permute-start.63 = (f32[32,512]{1,0:T(8,128)S(1)}, f32[32,512]{1,0:T(8,128)S(1)}, u32[]{:S(2)}, u32[]{:S(2)}) collective-permute-start(f32[32,512]{1,0:T(8,128)S(1)} %get-tuple-element.309), channel_id=1, source_target_pairs={{0,2},{1,3},{2,0},{3,1},{4,6},{5,7},{6,4},{7,5},{8,10},{9,11},{10,... | collective-permute-start | bytes 196616 | tf_op jit(solution)/shard_map/cond/branch_2_fun/ppermute | solution.py:76

commit v4 on v3

--- a/solution.py
+++ b/solution.py
@@ -13,6 +13,7 @@
 GROUP = 16
 PIECE = 64
 AXES = ("blk", "slab")
+LAST_CHIPS = (3, 7, 11, 15)
 
 
 def block_sizes(block_dims, owner):
@@ -28,6 +29,14 @@
     owner = column // (BS * BS)
     size_first, size_second = block_sizes(block_dims, owner)
     return (column // BS % BS < size_first) & (column % BS < size_second)
+
+
+def cycle_allowed(block_dims, slab_index, blk_index, local_rows, columns):
+    own_block = jnp.full((1,), slab_index, jnp.int32)
+    size_first, size_second = block_sizes(block_dims, own_block)
+    row_virtual = (blk_index * local_rows + lax.iota(jnp.int32, local_rows)) % BS
+    column_virtual = lax.iota(jnp.int32, columns) % BS
+    return (row_virtual[:, None] < size_first[0]) & (column_virtual[None, :] < size_second[0])
 
 
 def plain(amplitudes, ladder_ints, cycle_ints, block_dims):
@@ -57,12 +66,7 @@
     )
     cycle_term = cycle_term.reshape(cycle_term.shape[0], j_window * BS)
     cycle_sum = lax.psum_scatter(cycle_term, "blk", scatter_dimension=0, tiled=True)
-    own_block = jnp.full((1,), slab_index, jnp.int32)
-    size_first, size_second = block_sizes(block_dims, own_block)
-    local_rows = cycle_sum.shape[0]
-    row_virtual = (blk_index * local_rows + lax.iota(jnp.int32, local_rows)) % BS
-    column_virtual = lax.iota(jnp.int32, j_window * BS) % BS
-    allowed = (row_virtual[:, None] < size_first[0]) & (column_virtual[None, :] < size_second[0])
+    allowed = cycle_allowed(block_dims, slab_index, blk_index, cycle_sum.shape[0], j_window * BS)
     cycle_res = jnp.where(allowed, cycle_sum, 0.0).astype(jnp.bfloat16)[None]
     return (ladder_res, cycle_res)
 
@@ -270,64 +274,50 @@
     lax.fori_loop(0, depth // step, body, 0)
 
 
-def ladder_part_kernel(*refs):
-    products(refs[:-2], refs[-2], refs[-1])
-
-
-def ladder_part(pieces, rows_w):
-    count = sum(piece.shape[0] for piece in pieces)
-    shape = (count * PIECE, rows_w.shape[1])
+def ladder_kernel(first, pieces, rows_w, mine, other, total):
+    core, blk_index = lax.axis_index("slab"), lax.axis_index("blk")
+    products(pieces, rows_w, total)
+
+    def body(n, carry):
+        chip = chip_of(first + n, core, blk_index)
+        value = total[pl.ds(pl.multiple_of(n * PIECE, PIECE), PIECE), :]
+
+        @pl.when(chip // 8 == core)
+        def _():
+            mine[chip & 7] = value
+
+        @pl.when(chip // 8 != core)
+        def _():
+            other[chip & 7] = value
+
+        return carry
+
+    lax.fori_loop(0, total.shape[0] // PIECE, body, 0)
+
+
+def ladder_early_kernel(*refs):
+    ladder_kernel(0, refs[:-4], *refs[-4:])
+
+
+def ladder_late_kernel(*refs):
+    ladder_kernel(STAGES[0], refs[:-6], refs[-6], *refs[-3:])
+
+
+def ladder(stage, pieces, rows_w, before=()):
+    out_columns = rows_w.shape[1]
+    half = jax.ShapeDtypeStruct((8, PIECE, out_columns), jnp.float32)
+    given = len(pieces) + 1
     return pl.pallas_call(
-        ladder_part_kernel,
-        out_shape=jax.ShapeDtypeStruct(shape, jnp.float32),
-        in_specs=[VMEM] * (len(pieces) + 1),
-        out_specs=VMEM,
+        ladder_late_kernel if stage else ladder_early_kernel,
+        out_shape=[half, half],
+        in_specs=[VMEM] * (given + len(before)),
+        out_specs=[VMEM, VMEM],
+        scratch_shapes=[pltpu.VMEM((STAGES[stage] * PIECE, out_columns), jnp.float32)],
+        input_output_aliases={given + n: n for n in range(len(before))},
         compiler_params=ROOM,
         cost_estimate=SHORT,
-        name="ladder_part",
-    )(*pieces, rows_w)
-
-
-def ladder_late_kernel(*refs):
-    pieces = refs[:-5]
-    rows_w, early, mine, other, total = refs[-5:]
-    core, blk_index = lax.axis_index("slab"), lax.axis_index("blk")
-    products(pieces, rows_w, total)
-
-    def place(first, sums):
-        def body(n, carry):
-            chip = chip_of(first + n, core, blk_index)
-            value = sums[pl.ds(pl.multiple_of(n * PIECE, PIECE), PIECE), :]
-
-            @pl.when(chip // 8 == core)
-            def _():
-                mine[chip & 7] = value
-
-            @pl.when(chip // 8 != core)
-            def _():
-                other[chip & 7] = value
-
-            return carry
-
-        lax.fori_loop(0, sums.shape[0] // PIECE, body, 0)
-
-    place(0, early)
-    place(STAGES[0], total)
-
-
-def ladder_late(pieces, rows_w, early):
-    out_columns = rows_w.shape[1]
-    half = jax.ShapeDtypeStruct((8, PIECE, out_columns), jnp.float32)
-    return pl.pallas_call(
-        ladder_late_kernel,
-        out_shape=[half, half],
-        in_specs=[VMEM] * (len(pieces) + 2),
-        out_specs=[VMEM, VMEM],
-        scratch_shapes=[pltpu.VMEM((STAGES[1] * PIECE, out_columns), jnp.float32)],
-        compiler_params=ROOM,
-        cost_estimate=SHORT,
-        name="ladder_late",
-    )(*pieces, rows_w, early)
+        name="ladder_late" if stage else "ladder_early",
+    )(*pieces, rows_w, *before)
 
 
 def ladder_end_kernel(dims, mine, other, out, rows):
@@ -498,28 +488,6 @@
     )(*pieces, *turned, slots_first, slots_own)
 
 
-def cycle_end_kernel(dims, part_0, part_1, part_2, part_3, out):
-    core, blk_index = lax.axis_index("slab"), lax.axis_index("blk")
-    rows, columns = part_0.shape
-    a = blk_index * rows + lax.broadcasted_iota(jnp.int32, (rows, columns), 0) & (BS - 1)
-    d = lax.broadcasted_iota(jnp.int32, (rows, columns), 1) & (BS - 1)
-    keep = (a < dims[core, 0]) & (d < dims[core, 1])
-    total = part_0[...] + part_1[...] + part_2[...] + part_3[...]
-    out[0] = jnp.where(keep, total, 0.0).astype(jnp.bfloat16)
-
-
-def cycle_end(block_dims, parts):
-    return pl.pallas_call(
-        cycle_end_kernel,
-        out_shape=jax.ShapeDtypeStruct((1,) + parts[0].shape, jnp.bfloat16),
-        in_specs=[SMEM] + [VMEM] * 4,
-        out_specs=VMEM,
-        compiler_params=ROOM,
-        cost_estimate=SHORT,
-        name="cycle_end",
-    )(block_dims, *parts)
-
-
 def together(*values):
     return lax.optimization_barrier(values)
 
@@ -544,15 +512,17 @@
     moved_ints = ints.reshape(4, 4, 4 * BS, -1)[:, 3].reshape(GROUP * BS, -1)
     shares = [lax.dynamic_slice_in_dim(shares, (z + step) % 4 * 128, 128, 2) for step in range(4)]
     rows_w = own_rows(ints, width, least, columns, core)
-    near, far, moved_ints, rows_w, *shares = together(
-        jnp.concatenate(near), own, moved_ints, rows_w, *shares, plane_1, plane_2, plane_12
+    far = send(after(own, *near), up(2))
+    dims = after(block_dims, own)
+    allowed = cycle_allowed(dims, core, blk_index, 32, 8 * BS).astype(jnp.float32)
+    near, moved_ints, rows_w, allowed, *shares = together(
+        jnp.concatenate(near), moved_ints, rows_w, allowed, *shares, plane_1, plane_2, plane_12
     )[:8]
-    far = send(far, up(2))
     near_1 = send(near, first_axis)
     near_2 = send(near, second_axis)
     moved_ints = to_other_core(moved_ints, (0,))
-    far, near_1, near_2, rows_w, moved_ints, *shares = together(
-        far, near_1, near_2, rows_w, moved_ints, *shares
+    *shares, rows_w, moved_ints, near_2, near_1, far = together(
+        *shares, rows_w, moved_ints, near_2, near_1, far
     )
     cut = 4 * narrow_columns
     moved_rows = pad_rows(cut_rows(moved_ints, width), columns - cut)
@@ -566,26 +536,31 @@
     shares[2] = send(shares[2], up(2))
     shares[1] = send(after(shares[1], shares[3]), up(1))
     early = [own, plane_1, plane_2, plane_12, near, near_1, near_2]
-    sums = ladder_part(early, rows_w)
+    sums = ladder(0, early, rows_w)
     turned = cycle_early(width, least, early)
     far_1, far_2, near_12, sums, turned, *shares = together(
         far_1, far_2, near_12, sums, turned, *shares
     )
     far_12 = send(far_1, second_axis)
     slots, there = slots_of_pieces(shares)
-    there = to_other_core(there, (0,))
-    near_12, far_12, slots, there = together(near_12, far_12, slots, there)
-    slots_first = jnp.where(core == 0, slots, there)
+    there = [
+        lax.ppermute(part, AXES, [(2 * chip, 2 * chip + 1) for chip in LAST_CHIPS])
+        for part in jnp.split(there, 2)
+    ]
+    near_12, slots, far_12, *there = together(near_12, slots, far_12, *there)
+    slots_first = jnp.where(core == 0, slots, jnp.concatenate(there))
     late = [near_12, far, far_1, far_2, far_12]
     terms = cycle_late(width, least, late, turned, slots_first, slots)
-    pairs = [(2 * chip + 1, 2 * chip) for chip in (3, 7, 11, 15)]
+    pairs = [(2 * chip + 1, 2 * chip) for chip in LAST_CHIPS]
     last_group = lax.ppermute(terms[0], AXES, pairs)
-    mine, other = ladder_late(late, rows_w, after(sums, terms[1]))
+    mine, other = ladder(1, late, rows_w, after(sums, terms[1]))
     other = to_other_core(other, (0, 1))
     term = (terms[1] + last_group).reshape(4, 32, 8 * BS)
     parts = [send(term[n], target) for n, target in ((1, along_x), (2, along_y), (3, across))]
     ladder_res = ladder_end(block_dims, mine, other)
-    cycle_res = cycle_end(block_dims, [after(term[0], ladder_res)] + parts)
+    parts = together(term[0], *parts, ladder_res)[:4]
+    cycle_sum = parts[0] + parts[1] + parts[2] + parts[3]
+    cycle_res = (cycle_sum * allowed).astype(jnp.bfloat16)[None]
     return (ladder_res, cycle_res)
 
 

time: 100 us -> 85.8 us (0.86)
  waiting for transfers between devices: 38.6 us -> 27.9 us
  Pallas kernels: 16.3 us -> 13.1 us
  starting transfers between devices: 29.9 us -> 28.7 us
  other arithmetic: 3.12 us -> 4.28 us
    ppermute x18, waiting for transfers between devices: 38.6 us -> 27.9 us  [send(): return lax.ppermute(value, AXES, pairs)]
    dynamic_update_slice x1, other arithmetic: 2.95 us -> 0.4 us  [compacted(): lax.dynamic_update_slice(rows_w, jnp.where(core == 0, rows_w[cut:], moved...]
    slice x2, local copies, waits for them, and re-layouts: 4.02 us -> 2.34 us  [of_first(): return pad_rows(cut_rows(groups[:, :3], width), columns)]
    ppermute x0 -> x2, starting transfers between devices: none -> 1.35 us  [compacted(): lax.ppermute(part, AXES, [(2 * chip, 2 * chip + 1) for chip in LAST_CHIPS])]
    ppermute x4 -> x3, starting transfers between devices: 5.14 us -> 3.81 us  [to_other_core(): return lax.ppermute(value, 'slab', [(core, 1 - core) for core in cores])]
    lt x0 -> x2, other arithmetic: none -> 1.28 us  [the longest x1 0.64 us: cycle_allowed(): column_virtual[None, :] < size_second[0]]
    ppermute x18, starting transfers between devices: 24.1 us -> 22.9 us  [send(): return lax.ppermute(value, AXES, pairs)]
    slice x0 -> x3, local copies, waits for them, and re-layouts: none -> 1.22 us  [the longest x1 0.96 us: block_sizes(): size_first = jnp.sum(jnp.where(select, block_dims[None, :, 0], 0), 1)]
  transfers between devices with their start and end apart: 23 -> 24, of which waited for: 8 -> 10; matrix products, arithmetic and copies ran while one was open for 12% -> 14% of each run, Pallas kernels for 7% -> 8%
where the time goes in v4:
time: 85.8 us; the launch traced here: 85.4 us
  starting transfers between devices  28.7 us (33%)
  waiting for transfers between devices  27.9 us (33%)
  Pallas kernels  13.1 us (15%)
  local copies, waits for them, and re-layouts  8.37 us (10%)
  other arithmetic  4.28 us (5%)
  between operations  2.74 us (3%)
    ppermute x18, waiting for transfers between devices, send(): return lax.ppermute(value, AXES, pairs)  27.9 us
    ppermute x18, starting transfers between devices, send(): return lax.ppermute(value, AXES, pairs)  22.9 us
    pallas_call x2, Pallas kernels, ladder(): pl.pallas_call(ladder_late_kernel if stage else ladder_early_kernel, out_...  6.02 us
    ppermute x3, starting transfers between devices, to_other_core(): return lax.ppermute(value, 'slab', [(core, 1 - core) for core in cores])  3.81 us
    pallas_call x1, Pallas kernels, prep(): pl.pallas_call(functools.partial(prep_kernel, width, least), out_shape=ja...  2.37 us
    slice x2, local copies, waits for them, and re-layouts, of_first(): return pad_rows(cut_rows(groups[:, :3], width), columns)  2.34 us
    slice x1, local copies, waits for them, and re-layouts, compacted(): moved_ints = ints.reshape(4, 4, 4 * BS, -1)[:, 3].reshape(GROUP * BS, -1)  2.27 us
  transfers between devices with their start and end apart: 24, of which 10 were waited for; matrix products, arithmetic and copies ran while one was open for 14% of the time, Pallas kernels for 8%

profile of v4, /device:TPU:0, one launch (start us, length us, event | category | flops | bytes accessed | tf_op | source)
XLA Modules:
  0.0 85.4 jit_solution(1875221037178021208)
XLA Ops:
  0.6 2.4 %collective-permute-start.92 = (bf16[60,4096]{1,0:T(8,128)(2,1)}, bf16[60,4096]{1,0:T(8,128)(2,1)S(1)}, u32[]{:S(2)}, u32[]{:S(2)}) collective-permute-start(bf16[60,4096]{1,0:T(8,128)(2,1)} %param.24), channel_id=1, source_target_pairs={{0,1},{2,3},{4,5},{6,7},{8,9},{10,11},{12,13},{14,15},{16,17},{18,... | collective-permute-start | bytes 1474568 | tf_op jit(solution)/shard_map/ppermute | solution.py:108
  3.0 1.3 %fusion.44 = (s32[1,1]{1,0:T(1,128)}, s32[1,1]{1,0:T(1,128)}) fusion(s32[2,2]{1,0:T(2,128)} %param.27), kind=kLoop, calls=%fused_computation.117 | loop fusion | bytes 16 | tf_op jit(solution)/shard_map/slice | solution.py:572
  6.3 0.0 collective-permute-done.92
  6.3 79.0 %conditional.5 = (bf16[480,512]{1,0:T(8,128)(2,1)}, bf16[1,32,512]{2,1,0:T(8,128)(2,1)}) conditional(s32[]{:T(128)} %bitcast.62, (s32[2,2]{1,0:T(2,128)}, bf16[60,4096]{1,0:T(8,128)(2,1)}, bf16[60,4096]{1,0:T(8,128)(2,1)S(1)}, (), s32[8,384]{1,0:T(8,128)}, /*index=5*/bf16[1,4,120,512]{3,2,1,0:T(8,128)(2,1)}, ...), branch_computations={%region_0.5_spmd, %region_5.10_spmd, %region_10.15_spmd, %region_1... | conditional | flops 2680830 | bytes 143762768 | solution.py:577
  6.3 2.4 %prep.4 = bf16[64,2304]{1,0:T(8,128)(2,1)} custom-call(s32[2,2]{1,0:T(2,128)} %get-tuple-element.84.dims, bf16[60,4096]{1,0:T(8,128)(2,1)} %get-tuple-element.77.amp, bf16[60,4096]{1,0:T(8,128)(2,1)S(1)} %get-tuple-element.78.moved, s32[8,768]{1,0:T(8,128)} %constant.339.clone.1.wide, s32[8,384]{1,0:T(8,128)} %get-tuple-element.80.narrow), custom_call_target="tpu_custom_call" | custom-call | tf_op jit(solution)/shard_map/cond/branch_0_fun/prep/pallas_call | solution.py:167
  8.7 2.3 %collective-permute-start.3 = (bf16[1,64,2304]{2,1,0:T(8,128)(2,1)}, bf16[1,64,2304]{2,1,0:T(8,128)(2,1)S(1)}, u32[]{:S(2)}, u32[]{:S(2)}) collective-permute-start(bf16[1,64,2304]{2,1,0:T(8,128)(2,1)} %bitcast.109), channel_id=1, source_target_pairs={{0,4},{1,3},{2,6},{3,1},{4,0},{5,7},{6,2},{7,5},{8,12},{9,11},{10,... | collective-permute-start | bytes 884744 | tf_op jit(solution)/shard_map/cond/branch_0_fun/ppermute | solution.py:80
  11.1 1.5 %collective-permute-start.2 = (bf16[1,64,2304]{2,1,0:T(8,128)(2,1)}, bf16[1,64,2304]{2,1,0:T(8,128)(2,1)S(1)}, u32[]{:S(2)}, u32[]{:S(2)}) collective-permute-start(bf16[1,64,2304]{2,1,0:T(8,128)(2,1)} %bitcast.110), channel_id=1, source_target_pairs={{0,2},{1,5},{2,0},{3,7},{4,6},{5,1},{6,4},{7,3},{8,10},{9,13},{10,... | collective-permute-start | bytes 884744 | tf_op jit(solution)/shard_map/cond/branch_0_fun/ppermute | solution.py:80
  12.6 3.6 %collective-permute-start.1 = (bf16[1,64,2304]{2,1,0:T(8,128)(2,1)}, bf16[1,64,2304]{2,1,0:T(8,128)(2,1)S(1)}, u32[]{:S(2)}, u32[]{:S(2)}) collective-permute-start(bf16[1,64,2304]{2,1,0:T(8,128)(2,1)} %bitcast.111), channel_id=1, source_target_pairs={{0,24},{1,25},{2,26},{3,27},{4,28},{5,29},{6,30},{7,31},{8,0},{9,1... | collective-permute-start | bytes 884744 | tf_op jit(solution)/shard_map/cond/branch_0_fun/ppermute | solution.py:80
  16.2 0.0 collective-permute-start
  16.2 1.0 %slice_reduce_fusion.1 = (s32[2]{0:T(128)S(1)}, s32[2]{0:T(128)S(1)}) fusion(s32[2,2]{1,0:T(2,128)} %get-tuple-element.84.dims), kind=kLoop, calls=%fused_computation.23 | loop fusion | bytes 32 | tf_op jit(solution)/shard_map/cond/branch_0_fun/slice | solution.py:22
  17.1 0.7 fusion.5
  17.8 0.6 fusion.1
  18.5 2.3 %slice.163 = bf16[4,1,256,512]{3,2,1,0:T(8,128)(2,1)} slice(bf16[4,4,256,512]{3,2,1,0:T(8,128)(2,1)} %bitcast.116), slice={[0:4], [3:4], [0:256], [0:512]} | slice | bytes 2097152 | tf_op jit(solution)/shard_map/cond/branch_0_fun/slice | solution.py:512
  20.7 2.5 %conditional = (bf16[2304,512]{1,0:T(8,128)(2,1)S(1)}) conditional(s32[]{:T(128)} %convert_element_type.44, bf16[4096,512]{1,0:T(8,128)(2,1)} %get-tuple-element.83, bf16[4096,512]{1,0:T(8,128)(2,1)} %get-tuple-element.83), branch_computations={%region_1.1_spmd, %region_2.2_spmd} | conditional | bytes 17301512 | solution.py:203
  20.7 2.1 %slice.155 = bf16[4,3,256,512]{3,2,1,0:T(8,128)(2,1)S(1)} slice(bf16[4,4,256,512]{3,2,1,0:T(8,128)(2,1)} %bitcast.118), slice={[0:4], [0:3], [0:256], [0:512]} | slice | bytes 6291456 | tf_op jit(solution)/shard_map/cond/branch_0_fun/cond/branch_1_fun/slice | solution.py:198
  22.9 0.2 copy.39
  23.1 0.2 slice.156
  23.3 1.1 %constant_dynamic-slice_fusion = (bf16[4,120,128]{2,1,0:T(8,128)(2,1)S(1)}, bf16[4,120,128]{2,1,0:T(8,128)(2,1)S(1)}, bf16[4,120,128]{2,1,0:T(8,128)(2,1)S(1)}, bf16[4,120,128]{2,1,0:T(8,128)(2,1)S(1)}) fusion(bf16[4,120,512]{2,1,0:T(8,128)(2,1)} %bitcast.137, s32[]{:T(128)S(6)} %select_n.292, s32[]{:T(128)S(6)} %select_n.290, s32[]{:T(128)S(6)} %select_n.288, ...), kind=kLoop, calls=%fused_computation.16 | loop fusion | bytes 983056 | tf_op jit(solution)/shard_map/cond/branch_0_fun/dynamic_slice | solution.py:513
  24.5 0.6 fusion.7
  25.1 0.1 and_convert_fusion
  25.2 0.6 collective-permute-start.4
  25.8 3.3 %collective-permute-done = bf16[1,64,2304]{2,1,0:T(8,128)(2,1)} collective-permute-done((bf16[1,64,2304]{2,1,0:T(8,128)(2,1)}, bf16[1,64,2304]{2,1,0:T(8,128)(2,1)}, u32[]{:S(2)}, u32[]{:S(2)}) %collective-permute-start) | collective-permute-done | bytes 294944 | tf_op jit(solution)/shard_map/cond/branch_0_fun/ppermute | solution.py:80
  29.1 1.0 %pad_maximum_fusion.refs_4_ = bf16[2,64,2304]{2,1,0:T(8,128)(2,1)S(1)} fusion(bf16[1,64,2304]{2,1,0:T(8,128)(2,1)S(1)} %collective-permute-done.1, bf16[1,64,2304]{2,1,0:T(8,128)(2,1)} %collective-permute-done), kind=kLoop, calls=%fused_computation.1 | loop fusion | flops 294912 | bytes 1179648 | tf_op jit(solution)/shard_map/cond/branch_0_fun/concatenate | solution.py:519
  30.1 1.8 %collective-permute-done.4.refs_3_ = bf16[1,64,2304]{2,1,0:T(8,128)(2,1)S(1)} collective-permute-done((bf16[1,64,2304]{2,1,0:T(8,128)(2,1)S(1)}, bf16[1,64,2304]{2,1,0:T(8,128)(2,1)S(1)}, u32[]{:S(2)}, u32[]{:S(2)}) %collective-permute-start.4) | collective-permute-done | bytes 294944 | tf_op jit(solution)/shard_map/cond/branch_0_fun/ppermute | solution.py:80
  32.0 1.3 %collective-permute-start.5 = (bf16[1024,512]{1,0:T(8,128)(2,1)}, bf16[1024,512]{1,0:T(8,128)(2,1)S(1)}, u32[]{:S(2)}, u32[]{:S(2)}) collective-permute-start(bf16[1024,512]{1,0:T(8,128)(2,1)} %bitcast.145), channel_id=1, source_target_pairs={{0,1},{2,3},{4,5},{6,7},{8,9},{10,11},{12,13},{14,15},{16,17},{18,... | collective-permute-start | bytes 3145736 | tf_op jit(solution)/shard_map/cond/branch_0_fun/ppermute | solution.py:108
  33.3 0.6 collective-permute-start.7
  33.9 0.5 collective-permute-start.6
  34.4 1.0 %collective-permute-start.8 = (bf16[1,64,2304]{2,1,0:T(8,128)(2,1)S(1)}, bf16[1,64,2304]{2,1,0:T(8,128)(2,1)S(1)}, u32[]{:S(2)}, u32[]{:S(2)}) collective-permute-start(bf16[1,64,2304]{2,1,0:T(8,128)(2,1)S(1)} %bitcast.113), channel_id=1, source_target_pairs={{0,16},{1,17},{2,18},{3,19},{4,20},{5,21},{6,22},{7,23},{8,24},{9,... | collective-permute-start | bytes 884744 | tf_op jit(solution)/shard_map/cond/branch_0_fun/ppermute | solution.py:80
  35.4 11.7 %collective-permute-done.8.refs_1_ = bf16[1,64,2304]{2,1,0:T(8,128)(2,1)S(1)} collective-permute-done((bf16[1,64,2304]{2,1,0:T(8,128)(2,1)S(1)}, bf16[1,64,2304]{2,1,0:T(8,128)(2,1)S(1)}, u32[]{:S(2)}, u32[]{:S(2)}) %collective-permute-start.8) | collective-permute-done | bytes 294944 | tf_op jit(solution)/shard_map/cond/branch_0_fun/ppermute | solution.py:80
  47.2 0.0 collective-permute-done.7.refs_5_
  47.2 0.0 collective-permute-done.6.refs_6_
  47.2 0.0 collective-permute-done.5
  47.2 1.6 %collective-permute-start.11 = (bf16[2,64,2304]{2,1,0:T(8,128)(2,1)S(1)}, bf16[2,64,2304]{2,1,0:T(8,128)(2,1)S(1)}, u32[]{:S(2)}, u32[]{:S(2)}) collective-permute-start(bf16[2,64,2304]{2,1,0:T(8,128)(2,1)S(1)} %collective-permute-done.7.refs_5_), channel_id=1, source_target_pairs={{0,4},{1,3},{2,6},{3,1},{4,0},{5,7},{6,2},{7,5},{8,12},{9,11},{10,... | collective-permute-start | bytes 1769480 | tf_op jit(solution)/shard_map/cond/branch_0_fun/ppermute | solution.py:80
  48.8 1.9 %collective-permute-start.12 = (bf16[4,120,128]{2,1,0:T(8,128)(2,1)S(1)}, bf16[4,120,128]{2,1,0:T(8,128)(2,1)S(1)}, u32[]{:S(2)}, u32[]{:S(2)}) collective-permute-start(bf16[4,120,128]{2,1,0:T(8,128)(2,1)S(1)} %get-tuple-element.105), channel_id=1, source_target_pairs={{0,24},{1,25},{2,26},{3,27},{4,28},{5,29},{6,30},{7,31},{8,0},{9,1... | collective-permute-start | bytes 368648 | tf_op jit(solution)/shard_map/cond/branch_0_fun/ppermute | solution.py:80
  50.7 0.5 collective-permute-start.10
  51.2 1.2 %collective-permute-start.9 = (bf16[1,64,2304]{2,1,0:T(8,128)(2,1)S(1)}, bf16[1,64,2304]{2,1,0:T(8,128)(2,1)S(1)}, u32[]{:S(2)}, u32[]{:S(2)}) collective-permute-start(bf16[1,64,2304]{2,1,0:T(8,128)(2,1)S(1)} %collective-permute-done.8.refs_1_), channel_id=1, source_target_pairs={{0,2},{1,5},{2,0},{3,7},{4,6},{5,1},{6,4},{7,3},{8,10},{9,13},{10,... | collective-permute-start | bytes 884744 | tf_op jit(solution)/shard_map/cond/branch_0_fun/ppermute | solution.py:80
  52.4 0.1 slice.164
  52.5 0.1 collective-permute-start.14
  52.6 1.8 %collective-permute-done.12.part_3 = bf16[4,120,128]{2,1,0:T(8,128)(2,1)S(1)} collective-permute-done((bf16[4,120,128]{2,1,0:T(8,128)(2,1)S(1)}, bf16[4,120,128]{2,1,0:T(8,128)(2,1)S(1)}, u32[]{:S(2)}, u32[]{:S(2)}) %collective-permute-start.12) | collective-permute-done | bytes 122912 | tf_op jit(solution)/shard_map/cond/branch_0_fun/ppermute | solution.py:80
  54.4 0.0 collective-permute-start.13
  54.4 0.4 constant_dynamic-update-slice_fusion.refs_7_.refs_5_
  54.8 1.4 %cycle_early.4 = (bf16[1280,512]{1,0:T(8,128)(2,1)S(1)}, bf16[1280,512]{1,0:T(8,128)(2,1)S(1)}) custom-call(bf16[1,64,2304]{2,1,0:T(8,128)(2,1)S(1)} %bitcast.114, bf16[1,64,2304]{2,1,0:T(8,128)(2,1)S(1)} %collective-permute-done.2.refs_1_, bf16[1,64,2304]{2,1,0:T(8,128)(2,1)S(1)} %collective-permute-done.3.refs_2_, ...), custom_call_target="tpu_custom_call" | custom-call | flops 1024 | bytes 1024 | tf_op jit(solution)/shard_map/cond/branch_0_fun/cycle_early/pallas_call | solution.py:422
  56.2 3.5 %ladder_early.4 = (f32[8,64,512]{2,1,0:T(8,128)S(1)}, f32[8,64,512]{2,1,0:T(8,128)S(1)}) custom-call(bf16[1,64,2304]{2,1,0:T(8,128)(2,1)S(1)} %bitcast.115, bf16[1,64,2304]{2,1,0:T(8,128)(2,1)S(1)} %collective-permute-done.2.refs_1_, bf16[1,64,2304]{2,1,0:T(8,128)(2,1)S(1)} %collective-permute-done.3.refs_2_, ...), custom_call_target="tpu_custom_call" | custom-call | flops 1024 | bytes 1024 | tf_op jit(solution)/shard_map/cond/branch_0_fun/ladder_early/pallas_call | solution.py:310
  59.7 0.3 collective-permute-done.14.part_2
  60.0 1.5 %collective-permute-done.13.part_1 = bf16[4,120,128]{2,1,0:T(8,128)(2,1)S(1)} collective-permute-done((bf16[4,120,128]{2,1,0:T(8,128)(2,1)S(1)}, bf16[4,120,128]{2,1,0:T(8,128)(2,1)S(1)}, u32[]{:S(2)}, u32[]{:S(2)}) %collective-permute-start.13) | collective-permute-done | bytes 122912 | tf_op jit(solution)/shard_map/cond/branch_0_fun/ppermute | solution.py:80
  61.5 1.9 %collective-permute-done.10.refs_3_ = bf16[1,64,2304]{2,1,0:T(8,128)(2,1)S(1)} collective-permute-done((bf16[1,64,2304]{2,1,0:T(8,128)(2,1)S(1)}, bf16[1,64,2304]{2,1,0:T(8,128)(2,1)S(1)}, u32[]{:S(2)}, u32[]{:S(2)}) %collective-permute-start.10) | collective-permute-done | bytes 294944 | tf_op jit(solution)/shard_map/cond/branch_0_fun/ppermute | solution.py:80
  63.5 0.0 collective-permute-done.9.refs_2_
  63.5 1.5 %collective-permute-start.15 = (bf16[1,64,2304]{2,1,0:T(8,128)(2,1)S(1)}, bf16[1,64,2304]{2,1,0:T(8,128)(2,1)S(1)}, u32[]{:S(2)}, u32[]{:S(2)}) collective-permute-start(bf16[1,64,2304]{2,1,0:T(8,128)(2,1)S(1)} %collective-permute-done.9.refs_2_), channel_id=1, source_target_pairs={{0,4},{1,3},{2,6},{3,1},{4,0},{5,7},{6,2},{7,5},{8,12},{9,11},{10,... | collective-permute-start | bytes 884744 | tf_op jit(solution)/shard_map/cond/branch_0_fun/ppermute | solution.py:80
  65.0 0.5 slots.4
  65.5 0.7 collective-permute-start.17
  66.2 0.7 collective-permute-start.16
  66.9 3.3 %collective-permute-done.15.refs_4_ = bf16[1,64,2304]{2,1,0:T(8,128)(2,1)S(1)} collective-permute-done((bf16[1,64,2304]{2,1,0:T(8,128)(2,1)S(1)}, bf16[1,64,2304]{2,1,0:T(8,128)(2,1)S(1)}, u32[]{:S(2)}, u32[]{:S(2)}) %collective-permute-start.15) | collective-permute-done | bytes 294944 | tf_op jit(solution)/shard_map/cond/branch_0_fun/ppermute | solution.py:80
  70.2 0.1 maximum_select_fusion.refs_7_
  70.3 1.4 %cycle_late.4 = (f32[128,512]{1,0:T(8,128)S(1)}, f32[128,512]{1,0:T(8,128)S(1)}) custom-call(bf16[2,64,2304]{2,1,0:T(8,128)(2,1)S(1)} %collective-permute-done.11.refs_0_, bf16[1,64,2304]{2,1,0:T(8,128)(2,1)S(1)} %collective-permute-done.8.refs_1_, bf16[1,64,2304]{2,1,0:T(8,128)(2,1)S(1)} %collective-permute-done.9.refs_2_, ...), custom_call_target="tpu_custom_call" | custom-call | flops 1024 | bytes 1024 | tf_op jit(solution)/shard_map/cond/branch_0_fun/cycle_late/pallas_call | solution.py:476
  71.8 0.0 copy-start.15
  71.8 2.5 %ladder_late.4 = (f32[8,64,512]{2,1,0:T(8,128)S(1)}, f32[8,64,512]{2,1,0:T(8,128)S(1)}) custom-call(bf16[2,64,2304]{2,1,0:T(8,128)(2,1)S(1)} %collective-permute-done.11.refs_0_, bf16[1,64,2304]{2,1,0:T(8,128)(2,1)S(1)} %collective-permute-done.8.refs_1_, ...), custom_call_target="tpu_custom_call", output_to_operand_aliasing={{0}: (6, {}), {1}: (7, {})} | custom-call | flops 1024 | bytes 1024 | tf_op jit(solution)/shard_map/cond/branch_0_fun/ladder_late/pallas_call | solution.py:310
  74.3 0.1 collective-permute-start.18
  74.4 0.7 collective-permute-start.19
  75.1 5.3 %collective-permute-start.22 = (f32[32,512]{1,0:T(8,128)S(1)}, f32[32,512]{1,0:T(8,128)S(1)}, u32[]{:S(2)}, u32[]{:S(2)}) collective-permute-start(f32[32,512]{1,0:T(8,128)S(1)} %get-tuple-element.341), channel_id=1, source_target_pairs={{0,6},{1,7},{2,4},{3,5},{4,2},{5,3},{6,0},{7,1},{8,14},{9,15},{10,... | collective-permute-start | bytes 196616 | tf_op jit(solution)/shard_map/cond/branch_0_fun/ppermute | solution.py:80
  80.4 0.6 collective-permute-start.20
  81.0 1.5 %ladder_end.4 = bf16[480,512]{1,0:T(8,128)(2,1)} custom-call(s32[2,2]{1,0:T(2,128)S(1)} %copy-done.15, f32[8,64,512]{2,1,0:T(8,128)S(1)} %get-tuple-element.129.mine, f32[8,64,512]{2,1,0:T(8,128)S(1)} %collective-permute-done.18.other), custom_call_target="tpu_custom_call" | custom-call | flops 1024 | bytes 1024 | tf_op jit(solution)/shard_map/cond/branch_0_fun/ladder_end/pallas_call | solution.py:345
  82.6 0.2 collective-permute-done.22
  82.8 1.9 %collective-permute-done.21 = f32[32,512]{1,0:T(8,128)S(1)} collective-permute-done((f32[32,512]{1,0:T(8,128)S(1)}, f32[32,512]{1,0:T(8,128)S(1)}, u32[]{:S(2)}, u32[]{:S(2)}) %collective-permute-start.21) | collective-permute-done | bytes 65568 | tf_op jit(solution)/shard_map/cond/branch_0_fun/ppermute | solution.py:80
  84.7 0.6 fusion
  (16 shorter events, 0.1 us)
Async XLA Ops:
  0.6 5.7 %collective-permute-start.92 = (bf16[60,4096]{1,0:T(8,128)(2,1)}, bf16[60,4096]{1,0:T(8,128)(2,1)S(1)}, u32[]{:S(2)}, u32[]{:S(2)}) collective-permute-start(bf16[60,4096]{1,0:T(8,128)(2,1)} %param.24), channel_id=1, source_target_pairs={{0,1},{2,3},{4,5},{6,7},{8,9},{10,11},{12,13},{14,15},{16,17},{18,... | collective-permute-start | bytes 1474568 | tf_op jit(solution)/shard_map/ppermute | solution.py:108
  8.7 21.4 %collective-permute-start.3 = (bf16[1,64,2304]{2,1,0:T(8,128)(2,1)}, bf16[1,64,2304]{2,1,0:T(8,128)(2,1)S(1)}, u32[]{:S(2)}, u32[]{:S(2)}) collective-permute-start(bf16[1,64,2304]{2,1,0:T(8,128)(2,1)} %bitcast.109), channel_id=1, source_target_pairs={{0,4},{1,3},{2,6},{3,1},{4,0},{5,7},{6,2},{7,5},{8,12},{9,11},{10,... | collective-permute-start | bytes 884744 | tf_op jit(solution)/shard_map/cond/branch_0_fun/ppermute | solution.py:80
  11.1 14.1 %collective-permute-start.2 = (bf16[1,64,2304]{2,1,0:T(8,128)(2,1)}, bf16[1,64,2304]{2,1,0:T(8,128)(2,1)S(1)}, u32[]{:S(2)}, u32[]{:S(2)}) collective-permute-start(bf16[1,64,2304]{2,1,0:T(8,128)(2,1)} %bitcast.110), channel_id=1, source_target_pairs={{0,2},{1,5},{2,0},{3,7},{4,6},{5,1},{6,4},{7,3},{8,10},{9,13},{10,... | collective-permute-start | bytes 884744 | tf_op jit(solution)/shard_map/cond/branch_0_fun/ppermute | solution.py:80
  12.6 13.2 %collective-permute-start.1 = (bf16[1,64,2304]{2,1,0:T(8,128)(2,1)}, bf16[1,64,2304]{2,1,0:T(8,128)(2,1)S(1)}, u32[]{:S(2)}, u32[]{:S(2)}) collective-permute-start(bf16[1,64,2304]{2,1,0:T(8,128)(2,1)} %bitcast.111), channel_id=1, source_target_pairs={{0,24},{1,25},{2,26},{3,27},{4,28},{5,29},{6,30},{7,31},{8,0},{9,1... | collective-permute-start | bytes 884744 | tf_op jit(solution)/shard_map/cond/branch_0_fun/ppermute | solution.py:80
  16.2 12.9 %collective-permute-start = (bf16[1,64,2304]{2,1,0:T(8,128)(2,1)}, bf16[1,64,2304]{2,1,0:T(8,128)(2,1)}, u32[]{:S(2)}, u32[]{:S(2)}) collective-permute-start(bf16[1,64,2304]{2,1,0:T(8,128)(2,1)} %bitcast.112), channel_id=1, source_target_pairs={{0,8},{1,9},{2,10},{3,11},{4,12},{5,13},{6,14},{7,15},{8,16},{9,17... | collective-permute-start | bytes 884744 | tf_op jit(solution)/shard_map/cond/branch_0_fun/ppermute | solution.py:80
  20.7 13.7 %copy-start.5 = (bf16[64,2304]{1,0:T(8,128)(2,1)S(1)}, bf16[64,2304]{1,0:T(8,128)(2,1)}, u32[]{:S(2)}) copy-start(bf16[64,2304]{1,0:T(8,128)(2,1)} %prep.4) | copy-start | bytes 884740 | tf_op jit(solution)/shard_map/cond
  25.2 6.8 %collective-permute-start.4 = (bf16[1,64,2304]{2,1,0:T(8,128)(2,1)S(1)}, bf16[1,64,2304]{2,1,0:T(8,128)(2,1)S(1)}, u32[]{:S(2)}, u32[]{:S(2)}) collective-permute-start(bf16[1,64,2304]{2,1,0:T(8,128)(2,1)S(1)} %collective-permute-done.2.refs_1_), channel_id=1, source_target_pairs={{0,4},{1,3},{2,6},{3,1},{4,0},{5,7},{6,2},{7,5},{8,12},{9,11},{10,... | collective-permute-start | bytes 884744 | tf_op jit(solution)/shard_map/cond/branch_0_fun/ppermute | solution.py:80
  32.0 15.2 %collective-permute-start.5 = (bf16[1024,512]{1,0:T(8,128)(2,1)}, bf16[1024,512]{1,0:T(8,128)(2,1)S(1)}, u32[]{:S(2)}, u32[]{:S(2)}) collective-permute-start(bf16[1024,512]{1,0:T(8,128)(2,1)} %bitcast.145), channel_id=1, source_target_pairs={{0,1},{2,3},{4,5},{6,7},{8,9},{10,11},{12,13},{14,15},{16,17},{18,... | collective-permute-start | bytes 3145736 | tf_op jit(solution)/shard_map/cond/branch_0_fun/ppermute | solution.py:108
  33.3 13.9 %collective-permute-start.7 = (bf16[2,64,2304]{2,1,0:T(8,128)(2,1)S(1)}, bf16[2,64,2304]{2,1,0:T(8,128)(2,1)S(1)}, u32[]{:S(2)}, u32[]{:S(2)}) collective-permute-start(bf16[2,64,2304]{2,1,0:T(8,128)(2,1)S(1)} %pad_maximum_fusion.refs_4_), channel_id=1, source_target_pairs={{0,2},{1,5},{2,0},{3,7},{4,6},{5,1},{6,4},{7,3},{8,10},{9,13},{10,... | collective-permute-start | bytes 1769480 | tf_op jit(solution)/shard_map/cond/branch_0_fun/ppermute | solution.py:80
  33.9 13.3 %collective-permute-start.6 = (bf16[2,64,2304]{2,1,0:T(8,128)(2,1)S(1)}, bf16[2,64,2304]{2,1,0:T(8,128)(2,1)S(1)}, u32[]{:S(2)}, u32[]{:S(2)}) collective-permute-start(bf16[2,64,2304]{2,1,0:T(8,128)(2,1)S(1)} %pad_maximum_fusion.refs_4_), channel_id=1, source_target_pairs={{0,4},{1,3},{2,6},{3,1},{4,0},{5,7},{6,2},{7,5},{8,12},{9,11},{10,... | collective-permute-start | bytes 1769480 | tf_op jit(solution)/shard_map/cond/branch_0_fun/ppermute | solution.py:80
  34.4 12.7 %collective-permute-start.8 = (bf16[1,64,2304]{2,1,0:T(8,128)(2,1)S(1)}, bf16[1,64,2304]{2,1,0:T(8,128)(2,1)S(1)}, u32[]{:S(2)}, u32[]{:S(2)}) collective-permute-start(bf16[1,64,2304]{2,1,0:T(8,128)(2,1)S(1)} %bitcast.113), channel_id=1, source_target_pairs={{0,16},{1,17},{2,18},{3,19},{4,20},{5,21},{6,22},{7,23},{8,24},{9,... | collective-permute-start | bytes 884744 | tf_op jit(solution)/shard_map/cond/branch_0_fun/ppermute | solution.py:80
  47.2 16.3 %collective-permute-start.11 = (bf16[2,64,2304]{2,1,0:T(8,128)(2,1)S(1)}, bf16[2,64,2304]{2,1,0:T(8,128)(2,1)S(1)}, u32[]{:S(2)}, u32[]{:S(2)}) collective-permute-start(bf16[2,64,2304]{2,1,0:T(8,128)(2,1)S(1)} %collective-permute-done.7.refs_5_), channel_id=1, source_target_pairs={{0,4},{1,3},{2,6},{3,1},{4,0},{5,7},{6,2},{7,5},{8,12},{9,11},{10,... | collective-permute-start | bytes 1769480 | tf_op jit(solution)/shard_map/cond/branch_0_fun/ppermute | solution.py:80
  48.8 5.6 %collective-permute-start.12 = (bf16[4,120,128]{2,1,0:T(8,128)(2,1)S(1)}, bf16[4,120,128]{2,1,0:T(8,128)(2,1)S(1)}, u32[]{:S(2)}, u32[]{:S(2)}) collective-permute-start(bf16[4,120,128]{2,1,0:T(8,128)(2,1)S(1)} %get-tuple-element.105), channel_id=1, source_target_pairs={{0,24},{1,25},{2,26},{3,27},{4,28},{5,29},{6,30},{7,31},{8,0},{9,1... | collective-permute-start | bytes 368648 | tf_op jit(solution)/shard_map/cond/branch_0_fun/ppermute | solution.py:80
  50.7 12.8 %collective-permute-start.10 = (bf16[1,64,2304]{2,1,0:T(8,128)(2,1)S(1)}, bf16[1,64,2304]{2,1,0:T(8,128)(2,1)S(1)}, u32[]{:S(2)}, u32[]{:S(2)}) collective-permute-start(bf16[1,64,2304]{2,1,0:T(8,128)(2,1)S(1)} %collective-permute-done.8.refs_1_), channel_id=1, source_target_pairs={{0,4},{1,3},{2,6},{3,1},{4,0},{5,7},{6,2},{7,5},{8,12},{9,11},{10,... | collective-permute-start | bytes 884744 | tf_op jit(solution)/shard_map/cond/branch_0_fun/ppermute | solution.py:80
  51.2 12.3 %collective-permute-start.9 = (bf16[1,64,2304]{2,1,0:T(8,128)(2,1)S(1)}, bf16[1,64,2304]{2,1,0:T(8,128)(2,1)S(1)}, u32[]{:S(2)}, u32[]{:S(2)}) collective-permute-start(bf16[1,64,2304]{2,1,0:T(8,128)(2,1)S(1)} %collective-permute-done.8.refs_1_), channel_id=1, source_target_pairs={{0,2},{1,5},{2,0},{3,7},{4,6},{5,1},{6,4},{7,3},{8,10},{9,13},{10,... | collective-permute-start | bytes 884744 | tf_op jit(solution)/shard_map/cond/branch_0_fun/ppermute | solution.py:80
  52.5 7.5 %collective-permute-start.14 = (bf16[4,120,128]{2,1,0:T(8,128)(2,1)S(1)}, bf16[4,120,128]{2,1,0:T(8,128)(2,1)S(1)}, u32[]{:S(2)}, u32[]{:S(2)}) collective-permute-start(bf16[4,120,128]{2,1,0:T(8,128)(2,1)S(1)} %get-tuple-element.107), channel_id=1, source_target_pairs={{0,16},{1,17},{2,18},{3,19},{4,20},{5,21},{6,22},{7,23},{8,24},{9,... | collective-permute-start | bytes 368648 | tf_op jit(solution)/shard_map/cond/branch_0_fun/ppermute | solution.py:80
  54.4 7.1 %collective-permute-start.13 = (bf16[4,120,128]{2,1,0:T(8,128)(2,1)S(1)}, bf16[4,120,128]{2,1,0:T(8,128)(2,1)S(1)}, u32[]{:S(2)}, u32[]{:S(2)}) collective-permute-start(bf16[4,120,128]{2,1,0:T(8,128)(2,1)S(1)} %get-tuple-element.106), channel_id=1, source_target_pairs={{0,8},{1,9},{2,10},{3,11},{4,12},{5,13},{6,14},{7,15},{8,16},{9,17... | collective-permute-start | bytes 368648 | tf_op jit(solution)/shard_map/cond/branch_0_fun/ppermute | solution.py:80
  63.5 6.7 %collective-permute-start.15 = (bf16[1,64,2304]{2,1,0:T(8,128)(2,1)S(1)}, bf16[1,64,2304]{2,1,0:T(8,128)(2,1)S(1)}, u32[]{:S(2)}, u32[]{:S(2)}) collective-permute-start(bf16[1,64,2304]{2,1,0:T(8,128)(2,1)S(1)} %collective-permute-done.9.refs_2_), channel_id=1, source_target_pairs={{0,4},{1,3},{2,6},{3,1},{4,0},{5,7},{6,2},{7,5},{8,12},{9,11},{10,... | collective-permute-start | bytes 884744 | tf_op jit(solution)/shard_map/cond/branch_0_fun/ppermute | solution.py:80
  65.5 1.4 %collective-permute-start.17 = (bf16[1024,128]{1,0:T(8,128)(2,1)S(1)}, bf16[1024,128]{1,0:T(8,128)(2,1)S(1)}, u32[]{:S(2)}, u32[]{:S(2)}) collective-permute-start(bf16[1024,128]{1,0:T(8,128)(2,1)S(1)} %get-tuple-element.335), channel_id=1, source_target_pairs={{6,7},{14,15},{22,23},{30,31}} | collective-permute-start | bytes 786440 | tf_op jit(solution)/shard_map/cond/branch_0_fun/ppermute | solution.py:547
  66.2 0.7 collective-permute-start.16
  71.8 9.3 %copy-start.15 = (s32[2,2]{1,0:T(2,128)S(1)}, s32[2,2]{1,0:T(2,128)}, u32[]{:S(2)}) copy-start(s32[2,2]{1,0:T(2,128)} %get-tuple-element.84.dims) | copy-start | bytes 52 | tf_op jit(solution)/shard_map/cond
  74.3 6.8 %collective-permute-start.18 = (f32[8,64,512]{2,1,0:T(8,128)S(1)}, f32[8,64,512]{2,1,0:T(8,128)S(1)}, u32[]{:S(2)}, u32[]{:S(2)}) collective-permute-start(f32[8,64,512]{2,1,0:T(8,128)S(1)} %get-tuple-element.130), channel_id=1, source_target_pairs={{0,1},{1,0},{2,3},{3,2},{4,5},{5,4},{6,7},{7,6},{8,9},{9,8},{10,11... | collective-permute-start | bytes 3145736 | tf_op jit(solution)/shard_map/cond/branch_0_fun/ppermute | solution.py:108
  74.4 0.7 collective-permute-start.19
  75.1 7.7 %collective-permute-start.22 = (f32[32,512]{1,0:T(8,128)S(1)}, f32[32,512]{1,0:T(8,128)S(1)}, u32[]{:S(2)}, u32[]{:S(2)}) collective-permute-start(f32[32,512]{1,0:T(8,128)S(1)} %get-tuple-element.341), channel_id=1, source_target_pairs={{0,6},{1,7},{2,4},{3,5},{4,2},{5,3},{6,0},{7,1},{8,14},{9,15},{10,... | collective-permute-start | bytes 196616 | tf_op jit(solution)/shard_map/cond/branch_0_fun/ppermute | solution.py:80
  80.4 4.3 %collective-permute-start.21 = (f32[32,512]{1,0:T(8,128)S(1)}, f32[32,512]{1,0:T(8,128)S(1)}, u32[]{:S(2)}, u32[]{:S(2)}) collective-permute-start(f32[32,512]{1,0:T(8,128)S(1)} %get-tuple-element.342), channel_id=1, source_target_pairs={{0,4},{1,5},{2,6},{3,7},{4,0},{5,1},{6,2},{7,3},{8,12},{9,13},{10,... | collective-permute-start | bytes 196616 | tf_op jit(solution)/shard_map/cond/branch_0_fun/ppermute | solution.py:80
  80.4 4.3 %collective-permute-start.20 = (f32[32,512]{1,0:T(8,128)S(1)}, f32[32,512]{1,0:T(8,128)S(1)}, u32[]{:S(2)}, u32[]{:S(2)}) collective-permute-start(f32[32,512]{1,0:T(8,128)S(1)} %get-tuple-element.343), channel_id=1, source_target_pairs={{0,2},{1,3},{2,0},{3,1},{4,6},{5,7},{6,4},{7,5},{8,10},{9,11},{10,... | collective-permute-start | bytes 196616 | tf_op jit(solution)/shard_map/cond/branch_0_fun/ppermute | solution.py:80
